TPU v7x, 32 devices: a whole 2x2x4 slice. The times are simulated.
32 devices in a mesh: gx: 4 (over x, core), gy: 8 (over z, y).
Axes of the slice: x: 2, y: 2, z: 4, core: 2. Of those that a mesh axis runs over, the one named last changes fastest.
Arguments:
- positions: float32 [4, 8, 3, 32], P('gx', 'gy'), may hold values from 0 to 12, as said below
- features: float32 [4, 8, 32, 128], P('gx', 'gy'), may hold values from -6 to 6
- cotangent: float32 [4, 8, 32, 1152], P('gx', 'gy'), may hold values from -6 to 6
- nbr_src: int32 [4, 8, 5, 5, 32], P('gx', 'gy'), may hold values from 0 to 31
- nbr_tgt: int32 [4, 8, 5, 5, 32], P('gx', 'gy'), may hold values from 0 to 31
- pair_mask: int32 [4, 8, 5, 5, 32], P('gx', 'gy'), may hold values 0 or 1
- pair_species: int32 [4, 8, 5, 5, 32], P('gx', 'gy'), may hold values from 0 to 9
- w_in: float32 [8, 32], replicated, may hold values from -2 to 2
- species_emb: float32 [10, 32], replicated, may hold values from -6 to 6
- w_out: float32 [32, 384], replicated, may hold values from -1 to 1
Outputs:
- pos_grad: float32 [4, 8, 3, 32], P('gx', 'gy')
- feat_grad: float32 [4, 8, 32, 128], P('gx', 'gy')
Inputs may be any that keep to these rules, and one draw needn't show every extreme that they name: `positions`: the first two coordinates lie in 0 to 5, the third in 0 to 12.
All inputs are finite; a program needn't handle non-finite values. No bound on the sum of `pair_mask` on one device may be relied on, other than what follows from the above.
Results may differ from a plain program's by a relative error of at most 0.0003.
Values sent between devices are 32-bit elements; how exact they have to be, the bound alone decides.
No kernel may reach another device: no remote copies, remote signals or barrier semaphores. Data moves between devices by JAX's collectives and lax.ppermute only.
A program may use at most 64 MiB of HBM per device.

v0:
```python
import math

import jax
import jax.numpy as jnp
from jax import lax
from jax.sharding import PartitionSpec as P

domain_side = 5.0
cutoff = 12.0
soften = 0.25
highest = lax.Precision.HIGHEST


def shifted(value, axis, by):
    peers = lax.axis_size(axis)
    return lax.ppermute(value, axis, [(i, (i + by) % peers) for i in range(peers)])


def harmonics(unit):
    unit_x, unit_y, unit_z = (unit[0], unit[1], unit[2])
    root_three = math.sqrt(3.0)
    root_five = math.sqrt(5.0)
    root_fifteen = math.sqrt(15.0)
    return jnp.stack(
        [
            jnp.ones_like(unit_x),
            root_three * unit_x,
            root_three * unit_y,
            root_three * unit_z,
            root_fifteen * unit_x * unit_y,
            root_fifteen * unit_y * unit_z,
            0.5 * root_five * (2.0 * unit_z * unit_z - unit_x * unit_x - unit_y * unit_y),
            root_fifteen * unit_x * unit_z,
            0.5 * root_fifteen * (unit_x * unit_x - unit_y * unit_y),
        ],
        axis=0,
    )


def tile_geometry(
    tgt_pos,
    src_pos,
    offset,
    src_onehot,
    tgt_onehot,
    live_pair,
    species,
    w_in,
    species_emb,
    w_out,
    channels,
):
    pair_count = src_onehot.shape[0]
    relative = (
        jnp.dot(src_pos, src_onehot.T, precision=highest)
        + offset[:, None]
        - jnp.dot(tgt_pos, tgt_onehot.T, precision=highest)
    )
    distance = jnp.sqrt(jnp.sum(relative * relative, axis=0) + soften)
    scaled = distance / cutoff
    envelope = jnp.where(scaled < 1.0, (1.0 - scaled * scaled) ** 2, 0.0) * live_pair.astype(
        jnp.float32
    )
    orders = jnp.arange(1, w_in.shape[0] + 1, dtype=jnp.int32).astype(jnp.float32)
    radial_basis = (
        math.sqrt(2.0 / cutoff)
        * jnp.sin(orders[None, :] * math.pi * scaled[:, None])
        / distance[:, None]
    )
    picked = (
        species[:, None] == jnp.arange(species_emb.shape[0], dtype=jnp.int32)[None, :]
    ).astype(jnp.float32)
    hidden = jax.nn.silu(
        jnp.dot(radial_basis, w_in, precision=highest)
        + jnp.dot(picked, species_emb, precision=highest)
    )
    radial = (
        jnp.dot(hidden, w_out, precision=highest).reshape(pair_count, 3, channels)
        * envelope[:, None, None]
    )
    shapes = harmonics(relative / distance[None, :])
    return (radial, shapes)


def tile_grads(
    tgt_pos,
    src_pos,
    src_feats,
    offset,
    source_index,
    target_index,
    live_pair,
    species,
    w_in,
    species_emb,
    w_out,
    cot_block,
):
    atom_count = src_feats.shape[0]
    channels = src_feats.shape[1]
    pair_count = source_index.shape[0]
    atom_ids = jnp.arange(atom_count, dtype=jnp.int32)
    src_onehot = (source_index[:, None] == atom_ids[None, :]).astype(jnp.float32)
    tgt_onehot = (target_index[:, None] == atom_ids[None, :]).astype(jnp.float32)

    def geometry(target_xyz, source_xyz):
        return tile_geometry(
            target_xyz,
            source_xyz,
            offset,
            src_onehot,
            tgt_onehot,
            live_pair,
            species,
            w_in,
            species_emb,
            w_out,
            channels,
        )

    (radial, shapes), pullback = jax.vjp(geometry, tgt_pos, src_pos)
    sph = shapes.T
    gathered_feats = jnp.dot(src_onehot, src_feats, precision=highest)
    gathered_cot = jnp.dot(tgt_onehot, cot_block, precision=highest).reshape(
        pair_count, 9, channels
    )
    weighted = gathered_cot * gathered_feats[:, None, :]
    sum_zero = weighted[:, 0] * sph[:, 0:1]
    sum_one = jnp.sum(weighted[:, 1:4] * sph[:, 1:4, None], axis=1)
    sum_two = jnp.sum(weighted[:, 4:9] * sph[:, 4:9, None], axis=1)
    d_radial = jnp.stack([sum_zero, sum_one, sum_two], axis=1)
    d_zero = jnp.sum(radial[:, 0] * weighted[:, 0], axis=1)[:, None]
    d_one = jnp.sum(radial[:, 1][:, None, :] * weighted[:, 1:4], axis=2)
    d_two = jnp.sum(radial[:, 2][:, None, :] * weighted[:, 4:9], axis=2)
    d_shapes = jnp.concatenate([d_zero, d_one, d_two], axis=1).T
    cot_zero = gathered_cot[:, 0] * sph[:, 0:1]
    cot_one = jnp.sum(gathered_cot[:, 1:4] * sph[:, 1:4, None], axis=1)
    cot_two = jnp.sum(gathered_cot[:, 4:9] * sph[:, 4:9, None], axis=1)
    per_pair = radial[:, 0] * cot_zero + radial[:, 1] * cot_one + radial[:, 2] * cot_two
    feat_part = jnp.dot(src_onehot.T, per_pair, precision=highest)
    tgt_part, src_part = pullback((d_radial, d_shapes))
    return (tgt_part, src_part, feat_part)


def fetch_sources(own_block, fetch_plan):
    fetched = {0: own_block}
    for step_to, shift_by, anchor in fetch_plan:
        held = fetched[anchor]
        fetched[step_to] = shifted((held[0], held[1]), "gx", shift_by)
    return fetched


def fetch_targets(own_block, fetch_plan):
    fetched = {0: own_block}
    for step_to, shift_by, anchor in fetch_plan:
        held = fetched[anchor]
        fetched[step_to] = shifted((held[0], held[1]), "gy", shift_by)
    return fetched


def return_sources(partials, return_plan):
    summed_all = partials[0]
    running = partials[0]
    for step_from, shift_by, chained, finish in return_plan:
        outgoing = partials[step_from]
        running = shifted((outgoing[0], outgoing[1]), "gx", shift_by)
        summed_all = jax.tree.map(jnp.add, summed_all, running)
    return summed_all


def return_targets(partials, return_plan):
    summed_all = partials[0]
    running = partials[0]
    for step_from, shift_by, chained, finish in return_plan:
        outgoing = partials[step_from]
        running = shifted(outgoing, "gy", shift_by)
        summed_all = summed_all + running
    return summed_all


def local(
    positions,
    features,
    cotangent,
    nbr_src,
    nbr_tgt,
    pair_mask,
    pair_species,
    w_in,
    species_emb,
    w_out,
):
    own_pos = positions[0, 0]
    own_feats = features[0, 0]
    own_cot = cotangent[0, 0]
    fetch_plan = [(1, -1, 0), (2, -2, 0), (-1, 1, 0), (-2, 2, 0)]
    return_plan = [
        (1, 1, False, True),
        (2, 2, False, True),
        (-1, -1, False, True),
        (-2, -2, False, True),
    ]
    sources = fetch_sources((own_pos, own_feats), fetch_plan)
    targets = fetch_targets((own_pos, own_cot), fetch_plan)
    steps_order = [-2, -1, 0, 1, 2]
    src_pos_stack = jnp.stack([sources[step][0] for step in steps_order])
    src_feat_stack = jnp.stack([sources[step][1] for step in steps_order])
    tgt_pos_stack = jnp.stack([targets[step][0] for step in steps_order])
    cot_stack = jnp.stack([targets[step][1] for step in steps_order])
    rel_steps = (jnp.arange(5, dtype=jnp.int32) - 2).astype(jnp.float32)
    offset_x = jnp.broadcast_to(rel_steps[:, None] * domain_side, (5, 5))
    offset_y = jnp.broadcast_to(-rel_steps[None, :] * domain_side, (5, 5))
    offsets = jnp.stack([offset_x, offset_y, jnp.zeros((5, 5), jnp.float32)], axis=2)
    inner = jax.vmap(tile_grads, in_axes=(0, None, None, 0, 0, 0, 0, 0, None, None, None, 0))
    outer = jax.vmap(inner, in_axes=(None, 0, 0, 0, 0, 0, 0, 0, None, None, None, None))
    tgt_part, src_part, feat_part = outer(
        tgt_pos_stack,
        src_pos_stack,
        src_feat_stack,
        offsets,
        nbr_src[0, 0],
        nbr_tgt[0, 0],
        pair_mask[0, 0],
        pair_species[0, 0],
        w_in,
        species_emb,
        w_out,
        cot_stack,
    )
    tgt_sums = jnp.sum(tgt_part, axis=0)
    src_sums = jnp.sum(src_part, axis=1)
    feat_sums = jnp.sum(feat_part, axis=1)
    src_partials = {}
    tgt_partials = {}
    for step in steps_order:
        tgt_partials[step] = tgt_sums[step + 2]
        src_partials[step] = (src_sums[step + 2], feat_sums[step + 2])
    src_home = return_sources(src_partials, return_plan)
    tgt_home = return_targets(tgt_partials, return_plan)
    pos_total = src_home[0] + tgt_home
    return (pos_total[None, None], src_home[1][None, None])


def solution(mesh):
    in_specs = (
        P("gx", "gy", None, None),
        P("gx", "gy", None, None),
        P("gx", "gy", None, None),
        P("gx", "gy", None, None, None),
        P("gx", "gy", None, None, None),
        P("gx", "gy", None, None, None),
        P("gx", "gy", None, None, None),
        P(),
        P(),
        P(),
    )
    out_specs = (P("gx", "gy", None, None), P("gx", "gy", None, None))
    return jax.shard_map(local, mesh=mesh, in_specs=in_specs, out_specs=out_specs, check_vma=False)
```

profile of v0, /device:TPU:0, one launch (start us, length us, event | category | flops | bytes accessed | tf_op | source)
XLA Modules:
  0.0 81.4 jit_solution(4566751669858278940)
XLA Ops:
  1.3 3.0 %collective-permute-start.3 = (f32[3,32]{1,0:T(4,128)S(1)}, f32[3,32]{1,0:T(4,128)S(1)}, u32[]{:S(2)}, u32[]{:S(2)}) collective-permute-start(f32[3,32]{1,0:T(4,128)S(1)} %bitcast.267), channel_id=1, source_target_pairs={{0,2},{1,3},{2,4},{3,5},{4,6},{5,7},{6,0},{7,1},{8,10},{9,11},{10,... | collective-permute-start | bytes 1160 | tf_op jit(solution)/shard_map/ppermute | solution.py:16
  4.4 1.5 %collective-permute-start.4 = (f32[3,32]{1,0:T(4,128)S(1)}, f32[3,32]{1,0:T(4,128)S(1)}, u32[]{:S(2)}, u32[]{:S(2)}) collective-permute-start(f32[3,32]{1,0:T(4,128)S(1)} %bitcast.268), channel_id=1, source_target_pairs={{0,1},{1,2},{2,3},{3,4},{4,5},{5,6},{6,7},{7,0},{8,9},{9,10},{10,1... | collective-permute-start | bytes 1160 | tf_op jit(solution)/shard_map/ppermute | solution.py:16
  5.9 1.5 %collective-permute-start = (f32[3,32]{1,0:T(4,128)S(1)}, f32[3,32]{1,0:T(4,128)S(1)}, u32[]{:S(2)}, u32[]{:S(2)}) collective-permute-start(f32[3,32]{1,0:T(4,128)S(1)} %bitcast.269), channel_id=1, source_target_pairs={{0,16},{8,24},{16,0},{24,8},{1,17},{9,25},{17,1},{25,9},{2,18},{10... | collective-permute-start | bytes 1160 | tf_op jit(solution)/shard_map/ppermute | solution.py:16
  7.4 1.7 %collective-permute-start.2 = (f32[3,32]{1,0:T(4,128)S(1)}, f32[3,32]{1,0:T(4,128)S(1)}, u32[]{:S(2)}, u32[]{:S(2)}) collective-permute-start(f32[3,32]{1,0:T(4,128)S(1)} %bitcast.271), channel_id=1, source_target_pairs={{0,24},{8,0},{16,8},{24,16},{1,25},{9,1},{17,9},{25,17},{2,26},{10... | collective-permute-start | bytes 1160 | tf_op jit(solution)/shard_map/ppermute | solution.py:16
  9.9 1.2 %fusion.35 = f32[5,5,32,32]{3,2,1,0:T(8,128)S(1)} fusion(s32[5,5,32]{2,1,0:T(8,128)S(1)} %bitcast.262, f32[10,32]{1,0:T(8,128)} %param.18), kind=kOutput, calls=%fused_computation.62 | convolution fusion | flops 3080000 | bytes 106880 | tf_op jit(solution)/shard_map/vmap(vmap(jvp()))/dot_general | solution.py:75
  12.8 0.7 convert_element_type.37
  13.6 3.3 %collective-permute-start.5 = (f32[3,32]{1,0:T(4,128)S(1)}, f32[3,32]{1,0:T(4,128)S(1)}, u32[]{:S(2)}, u32[]{:S(2)}) collective-permute-start(f32[3,32]{1,0:T(4,128)S(1)} %bitcast.272), channel_id=1, source_target_pairs={{0,7},{1,0},{2,1},{3,2},{4,3},{5,4},{6,5},{7,6},{8,15},{9,8},{10,9... | collective-permute-start | bytes 1160 | tf_op jit(solution)/shard_map/ppermute | solution.py:16
  18.4 1.7 %collective-permute-start.13 = (f32[32,128]{1,0:T(8,128)}, f32[32,128]{1,0:T(8,128)}, u32[]{:S(2)}, u32[]{:S(2)}) collective-permute-start(f32[32,128]{1,0:T(8,128)} %bitcast.265), channel_id=1, source_target_pairs={{0,24},{8,0},{16,8},{24,16},{1,25},{9,1},{17,9},{25,17},{2,26},{10... | collective-permute-start | bytes 49160 | tf_op jit(solution)/shard_map/ppermute | solution.py:16
  20.4 1.8 %collective-permute-start.7 = (f32[32,1152]{1,0:T(8,128)}, f32[32,1152]{1,0:T(8,128)}, u32[]{:S(2)}, u32[]{:S(2)}) collective-permute-start(f32[32,1152]{1,0:T(8,128)} %bitcast.255), channel_id=1, source_target_pairs={{0,2},{1,3},{2,4},{3,5},{4,6},{5,7},{6,0},{7,1},{8,10},{9,11},{10,... | collective-permute-start | bytes 442376 | tf_op jit(solution)/shard_map/ppermute | solution.py:16
  23.2 1.9 %convolution_add_fusion = f32[5,5,32,32]{3,2,1,0:T(8,128)S(1)} fusion(f32[5,5,32,32]{3,2,1,0:T(8,128)S(1)} %fusion.35, f32[5,5,32]{2,1,0:T(8,128)S(1)} %get-tuple-element.38, f32[5,5,32]{2,1,0:T(8,128)S(1)} %get-tuple-element.36, f32[8]{0:T(128)S(1)} %convert_multiply_fusion, f32[8,32]{1,0:T(8,128)} %param.17), kind=kOutput, calls=%fused_computation.15 | convolution fusion | flops 2502400 | bytes 212256 | tf_op jit(solution)/shard_map/vmap(vmap(jvp()))/dot_general | solution.py:74
  25.1 1.2 %fusion.24 = f32[5,5,32,384]{3,2,1,0:T(8,128)S(1)} fusion(f32[5,5,32,32]{3,2,1,0:T(8,128)S(1)} %convolution_add_fusion, f32[32,384]{1,0:T(8,128)S(1)} %copy-done), kind=kOutput, calls=%fused_computation.45 | convolution fusion | flops 118067200 | bytes 1380352 | tf_op jit(solution)/shard_map/vmap(vmap(jvp()))/dot_general | solution.py:78
  26.9 1.1 %broadcast_multiply_fusion.1 = f32[5,5,32,3,128]{4,3,2,1,0:T(4,128)S(1)} fusion(f32[5,5,32,3,128]{4,3,2,1,0:T(4,128)S(1)} %reshape.99, f32[5,5,32]{2,1,0:T(8,128)S(1)} %get-tuple-element.37), kind=kLoop, calls=%fused_computation.24 | loop fusion | flops 307200 | bytes 2460800 | tf_op jit(solution)/shard_map/vmap(vmap(jvp()))/mul | solution.py:78
  27.9 1.3 %fusion.96 = (f32[5,5,32,1,128]{4,3,2,1,0:T(1,128)S(1)}, f32[5,5,32,1,128]{4,3,2,1,0:T(1,128)S(1)}, f32[5,5,32,1,128]{4,3,2,1,0:T(1,128)S(1)}) fusion(f32[5,5,32,3,128]{4,3,2,1,0:T(4,128)S(1)} %broadcast_multiply_fusion.1), kind=kLoop, calls=%fused_computation.198 | loop fusion | bytes 2457600 | tf_op jit(solution)/shard_map/vmap(vmap())/slice | solution.py:132
  30.9 4.7 %collective-permute-start.9 = (f32[32,1152]{1,0:T(8,128)}, f32[32,1152]{1,0:T(8,128)S(1)}, u32[]{:S(2)}, u32[]{:S(2)}) collective-permute-start(f32[32,1152]{1,0:T(8,128)} %bitcast.257), channel_id=1, source_target_pairs={{0,7},{1,0},{2,1},{3,2},{4,3},{5,4},{6,5},{7,6},{8,15},{9,8},{10,9... | collective-permute-start | bytes 442376 | tf_op jit(solution)/shard_map/ppermute | solution.py:16
  38.8 1.2 %fusion.23 = f32[5,5,32,128]{3,2,1,0:T(8,128)S(1)} fusion(s32[5,5,32]{2,1,0:T(8,128)} %bitcast.250, f32[5,32,128]{2,1,0:T(8,128)S(1)} %constant_dynamic-update-slice_fusion.10), kind=kOutput, calls=%fused_computation.43 | convolution fusion | flops 39347200 | bytes 494720 | tf_op jit(solution)/shard_map/vmap(vmap())/dot_general | solution.py:123
  40.0 0.9 %bitcast_dynamic-update-slice_fusion.4 = f32[5,32,1152]{2,1,0:T(8,128)S(1)} fusion(f32[32,1152]{1,0:T(8,128)} %collective-permute-done.7), kind=kLoop, calls=%fused_computation.69 | loop fusion | bytes 294912
  40.9 0.9 %bitcast_dynamic-update-slice_fusion.3 = f32[5,32,1152]{2,1,0:T(8,128)S(1)} fusion(f32[5,32,1152]{2,1,0:T(8,128)S(1)} %bitcast_dynamic-update-slice_fusion.4, f32[32,1152]{1,0:T(8,128)} %collective-permute-done.8), kind=kLoop, calls=%fused_computation.68 | loop fusion | bytes 294912
  41.9 0.9 %bitcast_dynamic-update-slice_fusion.2 = f32[5,32,1152]{2,1,0:T(8,128)S(1)} fusion(f32[5,32,1152]{2,1,0:T(8,128)S(1)} %bitcast_dynamic-update-slice_fusion.3, f32[1,1,32,1152]{3,2,1,0:T(8,128)} %param.12), kind=kLoop, calls=%fused_computation.67 | loop fusion | bytes 294912
  42.8 4.3 %convolution_bitcast_fusion = f32[5,5,32,1152]{3,2,0,1:T(8,128)} fusion(f32[5,32,1152]{2,1,0:T(8,128)S(1)} %bitcast_dynamic-update-slice_fusion, s32[5,5,32]{2,1,0:T(8,128)} %bitcast.260), kind=kOutput, calls=%fused_computation | convolution fusion | flops 353920000 | bytes 4426880 | tf_op jit(solution)/shard_map/vmap(vmap())/dot_general | solution.py:124
  47.1 5.8 %reshape.111 = f32[5,5,32,9,128]{4,3,2,0,1:T(8,128)} reshape(f32[5,5,32,1152]{3,2,0,1:T(8,128)} %convolution_bitcast_fusion) | data formatting | bytes 7372800 | tf_op jit(solution)/shard_map/vmap(vmap())/reshape | solution.py:124
  52.9 4.1 %broadcast_multiply_fusion = (f32[5,5,32,9,128]{4,2,1,0,3:T(8,128)S(1)}, f32[5,5,32,9,128]{4,2,1,0,3:T(8,128)S(1)}) fusion(f32[5,5,32,128]{3,2,1,0:T(8,128)S(1)} %fusion.23, f32[5,5,32,9,128]{4,3,2,0,1:T(8,128)} %reshape.111), kind=kLoop, calls=%fused_computation.5 | loop fusion | flops 921600 | bytes 11468800 | tf_op jit(solution)/shard_map/vmap(vmap())/mul | solution.py:127
  57.0 1.2 %multiply_reduce_fusion = (f32[5,5,32,128]{3,2,1,0:T(8,128)S(1)}, f32[5,5,32,5]{2,1,0,3:T(8,128)S(1)}, f32[5,5,32,128]{3,2,1,0:T(8,128)S(1)}) fusion(f32[5,5,32,9,128]{4,2,1,0,3:T(8,128)S(1)} %get-tuple-element.16, f32[5,5,32,5]{2,1,0,3:T(8,128)S(1)} %copy.59, f32[5,5,32,128]{3,2,1,0:T(8,128)S(1)} %bitcast.238, f32[5,5,32,9,128]{4,2,1,0,3:T(8,128)S(1)} %get-tuple-element.17), kind=kLoop, calls=%fused_computation.3 | loop fusion | flops 2863200 | bytes 5356800 | tf_op jit(solution)/shard_map/vmap(vmap())/reduce_sum | solution.py:130
  58.3 0.7 multiply_reduce_fusion.2
  60.0 1.2 %fusion.1 = f32[5,5,32,32]{3,2,1,0:T(8,128)S(1)} fusion(f32[5,5,32]{2,1,0:T(8,128)S(1)} %copy-done.8, f32[32,384]{1,0:T(8,128)S(1)} %copy-done, f32[5,5,32,1,128]{4,2,1,0,3:T(8,128)S(1)} %bitcast.242, f32[5,5,32,1,128]{4,2,1,0,3:T(8,128)S(1)} %bitcast.244, f32[5,5,32,1,128]{4,2,1,0,3:T(8,128)S(1)} %slice_multiply_fusion.2), kind=kOutput, calls=%fused_computation.8 | convolution fusion | flops 118886400 | bytes 1383552 | tf_op jit(solution)/shard_map/vmap(vmap(transpose(jvp())))/dot_general | solution.py:78
  62.0 1.8 %fusion.40 = (f32[5,5,32]{2,1,0:T(8,128)S(1)}, f32[5,5,32]{2,1,0:T(8,128)S(1)}) fusion(f32[5,5,32]{2,1,0:T(8,128)S(1)} %copy-done.15, f32[5,5,32]{2,1,0:T(8,128)S(1)} %copy-done.12, f32[8]{0:T(128)S(1)} %copy-done.19, f32[5,5,32]{2,1,0:T(8,128)S(1)} %get-tuple-element.38, f32[8,32]{1,0:T(8,128)S(1)} %copy-done.17, ...), kind=kOutput, calls=%fused_computation.73 | convolution fusion | flops 2750400 | bytes 221856 | tf_op jit(solution)/shard_map/vmap(vmap(transpose(jvp())))/dot_general | solution.py:74
  64.8 3.0 %collective-permute-start.21 = (f32[3,32]{1,0:T(4,128)S(1)}, f32[3,32]{1,0:T(4,128)S(1)}, u32[]{:S(2)}, u32[]{:S(2)}) collective-permute-start(f32[3,32]{1,0:T(4,128)S(1)} %get-tuple-element.44), channel_id=1, source_target_pairs={{0,6},{1,7},{2,0},{3,1},{4,2},{5,3},{6,4},{7,5},{8,14},{9,15},{10,... | collective-permute-start | bytes 1160 | tf_op jit(solution)/shard_map/ppermute | solution.py:16
  67.9 1.4 %collective-permute-start.19 = (f32[3,32]{1,0:T(4,128)S(1)}, f32[3,32]{1,0:T(4,128)S(1)}, u32[]{:S(2)}, u32[]{:S(2)}) collective-permute-start(f32[3,32]{1,0:T(4,128)S(1)} %get-tuple-element.46), channel_id=1, source_target_pairs={{0,2},{1,3},{2,4},{3,5},{4,6},{5,7},{6,0},{7,1},{8,10},{9,11},{10,... | collective-permute-start | bytes 1160 | tf_op jit(solution)/shard_map/ppermute | solution.py:16
  71.4 1.2 %collective-permute-start.15 = (f32[3,32]{1,0:T(4,128)S(1)}, f32[3,32]{1,0:T(4,128)S(1)}, u32[]{:S(2)}, u32[]{:S(2)}) collective-permute-start(f32[3,32]{1,0:T(4,128)S(1)} %get-tuple-element.42), channel_id=1, source_target_pairs={{0,16},{8,24},{16,0},{24,8},{1,17},{9,25},{17,1},{25,9},{2,18},{10... | collective-permute-start | bytes 1160 | tf_op jit(solution)/shard_map/ppermute | solution.py:16
  73.2 2.3 %collective-permute-done.18 = f32[3,32]{1,0:T(4,128)S(1)} collective-permute-done((f32[3,32]{1,0:T(4,128)S(1)}, f32[3,32]{1,0:T(4,128)S(1)}, u32[]{:S(2)}, u32[]{:S(2)}) %collective-permute-start.18) | collective-permute-done | bytes 416 | tf_op jit(solution)/shard_map/ppermute | solution.py:16
  76.0 1.6 %collective-permute-start.23 = (f32[32,128]{1,0:T(8,128)S(1)}, f32[32,128]{1,0:T(8,128)S(1)}, u32[]{:S(2)}, u32[]{:S(2)}) collective-permute-start(f32[32,128]{1,0:T(8,128)S(1)} %get-tuple-element.26), channel_id=1, source_target_pairs={{0,16},{8,24},{16,0},{24,8},{1,17},{9,25},{17,1},{25,9},{2,18},{10... | collective-permute-start | bytes 49160 | tf_op jit(solution)/shard_map/ppermute | solution.py:16
  78.4 1.0 %collective-permute-done.25 = f32[32,128]{1,0:T(8,128)S(1)} collective-permute-done((f32[32,128]{1,0:T(8,128)S(1)}, f32[32,128]{1,0:T(8,128)S(1)}, u32[]{:S(2)}, u32[]{:S(2)}) %collective-permute-start.25) | collective-permute-done | bytes 16416 | tf_op jit(solution)/shard_map/ppermute | solution.py:16
  79.8 0.9 %collective-permute-done.22 = f32[32,128]{1,0:T(8,128)S(1)} collective-permute-done((f32[32,128]{1,0:T(8,128)S(1)}, f32[32,128]{1,0:T(8,128)S(1)}, u32[]{:S(2)}, u32[]{:S(2)}) %collective-permute-start.22) | collective-permute-done | bytes 16416 | tf_op jit(solution)/shard_map/ppermute | solution.py:16
  (139 shorter events, 19.0 us)
Async XLA Ops:
  0.6 24.5 %copy-start = (f32[32,384]{1,0:T(8,128)S(1)}, f32[32,384]{1,0:T(8,128)}, u32[]{:S(2)}) copy-start(f32[32,384]{1,0:T(8,128)} %param.19) | copy-start | bytes 147460
  1.3 12.2 %collective-permute-start.3 = (f32[3,32]{1,0:T(4,128)S(1)}, f32[3,32]{1,0:T(4,128)S(1)}, u32[]{:S(2)}, u32[]{:S(2)}) collective-permute-start(f32[3,32]{1,0:T(4,128)S(1)} %bitcast.267), channel_id=1, source_target_pairs={{0,2},{1,3},{2,4},{3,5},{4,6},{5,7},{6,0},{7,1},{8,10},{9,11},{10,... | collective-permute-start | bytes 1160 | tf_op jit(solution)/shard_map/ppermute | solution.py:16
  4.4 12.9 %collective-permute-start.4 = (f32[3,32]{1,0:T(4,128)S(1)}, f32[3,32]{1,0:T(4,128)S(1)}, u32[]{:S(2)}, u32[]{:S(2)}) collective-permute-start(f32[3,32]{1,0:T(4,128)S(1)} %bitcast.268), channel_id=1, source_target_pairs={{0,1},{1,2},{2,3},{3,4},{4,5},{5,6},{6,7},{7,0},{8,9},{9,10},{10,1... | collective-permute-start | bytes 1160 | tf_op jit(solution)/shard_map/ppermute | solution.py:16
  5.9 11.0 %collective-permute-start = (f32[3,32]{1,0:T(4,128)S(1)}, f32[3,32]{1,0:T(4,128)S(1)}, u32[]{:S(2)}, u32[]{:S(2)}) collective-permute-start(f32[3,32]{1,0:T(4,128)S(1)} %bitcast.269), channel_id=1, source_target_pairs={{0,16},{8,24},{16,0},{24,8},{1,17},{9,25},{17,1},{25,9},{2,18},{10... | collective-permute-start | bytes 1160 | tf_op jit(solution)/shard_map/ppermute | solution.py:16
  7.4 10.3 %collective-permute-start.1 = (f32[3,32]{1,0:T(4,128)S(1)}, f32[3,32]{1,0:T(4,128)S(1)}, u32[]{:S(2)}, u32[]{:S(2)}) collective-permute-start(f32[3,32]{1,0:T(4,128)S(1)} %bitcast.270), channel_id=1, source_target_pairs={{0,8},{8,16},{16,24},{24,0},{1,9},{9,17},{17,25},{25,1},{2,10},{10... | collective-permute-start | bytes 1160 | tf_op jit(solution)/shard_map/ppermute | solution.py:16
  7.4 11.0 %collective-permute-start.2 = (f32[3,32]{1,0:T(4,128)S(1)}, f32[3,32]{1,0:T(4,128)S(1)}, u32[]{:S(2)}, u32[]{:S(2)}) collective-permute-start(f32[3,32]{1,0:T(4,128)S(1)} %bitcast.271), channel_id=1, source_target_pairs={{0,24},{8,0},{16,8},{24,16},{1,25},{9,1},{17,9},{25,17},{2,26},{10... | collective-permute-start | bytes 1160 | tf_op jit(solution)/shard_map/ppermute | solution.py:16
  11.4 14.9 %copy-start.18 = (f32[8]{0:T(128)}, f32[8]{0:T(128)S(1)}, u32[]{:S(2)}) copy-start(f32[8]{0:T(128)S(1)} %convert_multiply_fusion) | copy-start | bytes 100
  12.1 11.1 %copy-start.2 = (s32[1,1,5,5,32]{4,3,1,2,0:T(8,128)}, s32[1,1,5,5,32]{4,3,1,2,0:T(8,128)S(1)}, u32[]{:S(2)}) copy-start(s32[1,1,5,5,32]{4,3,1,2,0:T(8,128)S(1)} %copy.117) | copy-start | bytes 9604
  12.8 10.4 %copy-start.9 = (s32[1,1,5,5,32]{4,3,1,2,0:T(8,128)}, s32[1,1,5,5,32]{4,3,1,2,0:T(8,128)S(1)}, u32[]{:S(2)}) copy-start(s32[1,1,5,5,32]{4,3,1,2,0:T(8,128)S(1)} %copy.116) | copy-start | bytes 9604
  13.6 9.6 %copy-start.5 = (f32[1,1,5,5,32]{4,1,3,2,0:T(1,128)}, f32[1,1,5,5,32]{4,1,3,2,0:T(1,128)S(1)}, u32[]{:S(2)}) copy-start(f32[1,1,5,5,32]{4,1,3,2,0:T(1,128)S(1)} %convert_element_type.37) | copy-start | bytes 9604
  13.6 6.8 %collective-permute-start.5 = (f32[3,32]{1,0:T(4,128)S(1)}, f32[3,32]{1,0:T(4,128)S(1)}, u32[]{:S(2)}, u32[]{:S(2)}) collective-permute-start(f32[3,32]{1,0:T(4,128)S(1)} %bitcast.272), channel_id=1, source_target_pairs={{0,7},{1,0},{2,1},{3,2},{4,3},{5,4},{6,5},{7,6},{8,15},{9,8},{10,9... | collective-permute-start | bytes 1160 | tf_op jit(solution)/shard_map/ppermute | solution.py:16
  16.8 5.4 %collective-permute-start.6 = (f32[3,32]{1,0:T(4,128)S(1)}, f32[3,32]{1,0:T(4,128)S(1)}, u32[]{:S(2)}, u32[]{:S(2)}) collective-permute-start(f32[3,32]{1,0:T(4,128)S(1)} %bitcast.273), channel_id=1, source_target_pairs={{0,6},{1,7},{2,0},{3,1},{4,2},{5,3},{6,4},{7,5},{8,14},{9,15},{10,... | collective-permute-start | bytes 1160 | tf_op jit(solution)/shard_map/ppermute | solution.py:16
  17.3 13.6 %collective-permute-start.11 = (f32[32,128]{1,0:T(8,128)}, f32[32,128]{1,0:T(8,128)}, u32[]{:S(2)}, u32[]{:S(2)}) collective-permute-start(f32[32,128]{1,0:T(8,128)} %bitcast.263), channel_id=1, source_target_pairs={{0,16},{8,24},{16,0},{24,8},{1,17},{9,25},{17,1},{25,9},{2,18},{10... | collective-permute-start | bytes 49160 | tf_op jit(solution)/shard_map/ppermute | solution.py:16
  17.7 18.6 %collective-permute-start.12 = (f32[32,128]{1,0:T(8,128)}, f32[32,128]{1,0:T(8,128)}, u32[]{:S(2)}, u32[]{:S(2)}) collective-permute-start(f32[32,128]{1,0:T(8,128)} %bitcast.264), channel_id=1, source_target_pairs={{0,8},{8,16},{16,24},{24,0},{1,9},{9,17},{17,25},{25,1},{2,10},{10... | collective-permute-start | bytes 49160 | tf_op jit(solution)/shard_map/ppermute | solution.py:16
  18.4 18.9 %collective-permute-start.13 = (f32[32,128]{1,0:T(8,128)}, f32[32,128]{1,0:T(8,128)}, u32[]{:S(2)}, u32[]{:S(2)}) collective-permute-start(f32[32,128]{1,0:T(8,128)} %bitcast.265), channel_id=1, source_target_pairs={{0,24},{8,0},{16,8},{24,16},{1,25},{9,1},{17,9},{25,17},{2,26},{10... | collective-permute-start | bytes 49160 | tf_op jit(solution)/shard_map/ppermute | solution.py:16
  20.4 19.6 %collective-permute-start.7 = (f32[32,1152]{1,0:T(8,128)}, f32[32,1152]{1,0:T(8,128)}, u32[]{:S(2)}, u32[]{:S(2)}) collective-permute-start(f32[32,1152]{1,0:T(8,128)} %bitcast.255), channel_id=1, source_target_pairs={{0,2},{1,3},{2,4},{3,5},{4,6},{5,7},{6,0},{7,1},{8,10},{9,11},{10,... | collective-permute-start | bytes 442376 | tf_op jit(solution)/shard_map/ppermute | solution.py:16
  22.2 18.7 %collective-permute-start.8 = (f32[32,1152]{1,0:T(8,128)}, f32[32,1152]{1,0:T(8,128)}, u32[]{:S(2)}, u32[]{:S(2)}) collective-permute-start(f32[32,1152]{1,0:T(8,128)} %bitcast.256), channel_id=1, source_target_pairs={{0,1},{1,2},{2,3},{3,4},{4,5},{5,6},{6,7},{7,0},{8,9},{9,10},{10,1... | collective-permute-start | bytes 442376 | tf_op jit(solution)/shard_map/ppermute | solution.py:16
  27.9 9.4 %copy-start.16 = (f32[1,1,32,128]{3,2,1,0:T(8,128)S(1)}, f32[1,1,32,128]{3,2,1,0:T(8,128)}, u32[]{:S(2)}) copy-start(f32[1,1,32,128]{3,2,1,0:T(8,128)} %param.11) | copy-start | bytes 49156
  30.9 11.9 %collective-permute-start.9 = (f32[32,1152]{1,0:T(8,128)}, f32[32,1152]{1,0:T(8,128)S(1)}, u32[]{:S(2)}, u32[]{:S(2)}) collective-permute-start(f32[32,1152]{1,0:T(8,128)} %bitcast.257), channel_id=1, source_target_pairs={{0,7},{1,0},{2,1},{3,2},{4,3},{5,4},{6,5},{7,6},{8,15},{9,8},{10,9... | collective-permute-start | bytes 442376 | tf_op jit(solution)/shard_map/ppermute | solution.py:16
  36.3 6.5 %collective-permute-start.10 = (f32[32,1152]{1,0:T(8,128)}, f32[32,1152]{1,0:T(8,128)S(1)}, u32[]{:S(2)}, u32[]{:S(2)}) collective-permute-start(f32[32,1152]{1,0:T(8,128)} %bitcast.258), channel_id=1, source_target_pairs={{0,6},{1,7},{2,0},{3,1},{4,2},{5,3},{6,4},{7,5},{8,14},{9,15},{10,... | collective-permute-start | bytes 442376 | tf_op jit(solution)/shard_map/ppermute | solution.py:16
  64.8 6.3 %collective-permute-start.21 = (f32[3,32]{1,0:T(4,128)S(1)}, f32[3,32]{1,0:T(4,128)S(1)}, u32[]{:S(2)}, u32[]{:S(2)}) collective-permute-start(f32[3,32]{1,0:T(4,128)S(1)} %get-tuple-element.44), channel_id=1, source_target_pairs={{0,6},{1,7},{2,0},{3,1},{4,2},{5,3},{6,4},{7,5},{8,14},{9,15},{10,... | collective-permute-start | bytes 1160 | tf_op jit(solution)/shard_map/ppermute | solution.py:16
  67.8 3.6 %collective-permute-start.20 = (f32[3,32]{1,0:T(4,128)S(1)}, f32[3,32]{1,0:T(4,128)S(1)}, u32[]{:S(2)}, u32[]{:S(2)}) collective-permute-start(f32[3,32]{1,0:T(4,128)S(1)} %get-tuple-element.45), channel_id=1, source_target_pairs={{0,7},{1,0},{2,1},{3,2},{4,3},{5,4},{6,5},{7,6},{8,15},{9,8},{10,9... | collective-permute-start | bytes 1160 | tf_op jit(solution)/shard_map/ppermute | solution.py:16
  67.9 5.4 %collective-permute-start.19 = (f32[3,32]{1,0:T(4,128)S(1)}, f32[3,32]{1,0:T(4,128)S(1)}, u32[]{:S(2)}, u32[]{:S(2)}) collective-permute-start(f32[3,32]{1,0:T(4,128)S(1)} %get-tuple-element.46), channel_id=1, source_target_pairs={{0,2},{1,3},{2,4},{3,5},{4,6},{5,7},{6,0},{7,1},{8,10},{9,11},{10,... | collective-permute-start | bytes 1160 | tf_op jit(solution)/shard_map/ppermute | solution.py:16
  69.2 6.3 %collective-permute-start.18 = (f32[3,32]{1,0:T(4,128)S(1)}, f32[3,32]{1,0:T(4,128)S(1)}, u32[]{:S(2)}, u32[]{:S(2)}) collective-permute-start(f32[3,32]{1,0:T(4,128)S(1)} %get-tuple-element.43), channel_id=1, source_target_pairs={{0,1},{1,2},{2,3},{3,4},{4,5},{5,6},{6,7},{7,0},{8,9},{9,10},{10,1... | collective-permute-start | bytes 1160 | tf_op jit(solution)/shard_map/ppermute | solution.py:16
  69.9 6.2 %collective-permute-start.17 = (f32[3,32]{1,0:T(4,128)S(1)}, f32[3,32]{1,0:T(4,128)S(1)}, u32[]{:S(2)}, u32[]{:S(2)}) collective-permute-start(f32[3,32]{1,0:T(4,128)S(1)} %get-tuple-element.40), channel_id=1, source_target_pairs={{0,16},{8,24},{16,0},{24,8},{1,17},{9,25},{17,1},{25,9},{2,18},{10... | collective-permute-start | bytes 1160 | tf_op jit(solution)/shard_map/ppermute | solution.py:16
  71.2 4.9 %collective-permute-start.16 = (f32[3,32]{1,0:T(4,128)S(1)}, f32[3,32]{1,0:T(4,128)S(1)}, u32[]{:S(2)}, u32[]{:S(2)}) collective-permute-start(f32[3,32]{1,0:T(4,128)S(1)} %get-tuple-element.41), channel_id=1, source_target_pairs={{0,24},{8,0},{16,8},{24,16},{1,25},{9,1},{17,9},{25,17},{2,26},{10... | collective-permute-start | bytes 1160 | tf_op jit(solution)/shard_map/ppermute | solution.py:16
  71.4 6.2 %collective-permute-start.15 = (f32[3,32]{1,0:T(4,128)S(1)}, f32[3,32]{1,0:T(4,128)S(1)}, u32[]{:S(2)}, u32[]{:S(2)}) collective-permute-start(f32[3,32]{1,0:T(4,128)S(1)} %get-tuple-element.42), channel_id=1, source_target_pairs={{0,16},{8,24},{16,0},{24,8},{1,17},{9,25},{17,1},{25,9},{2,18},{10... | collective-permute-start | bytes 1160 | tf_op jit(solution)/shard_map/ppermute | solution.py:16
  73.2 4.5 %collective-permute-start.14 = (f32[3,32]{1,0:T(4,128)S(1)}, f32[3,32]{1,0:T(4,128)S(1)}, u32[]{:S(2)}, u32[]{:S(2)}) collective-permute-start(f32[3,32]{1,0:T(4,128)S(1)} %get-tuple-element.39), channel_id=1, source_target_pairs={{0,8},{8,16},{16,24},{24,0},{1,9},{9,17},{17,25},{25,1},{2,10},{10... | collective-permute-start | bytes 1160 | tf_op jit(solution)/shard_map/ppermute | solution.py:16
  75.5 3.8 %collective-permute-start.25 = (f32[32,128]{1,0:T(8,128)S(1)}, f32[32,128]{1,0:T(8,128)S(1)}, u32[]{:S(2)}, u32[]{:S(2)}) collective-permute-start(f32[32,128]{1,0:T(8,128)S(1)} %get-tuple-element.24), channel_id=1, source_target_pairs={{0,16},{8,24},{16,0},{24,8},{1,17},{9,25},{17,1},{25,9},{2,18},{10... | collective-permute-start | bytes 49160 | tf_op jit(solution)/shard_map/ppermute | solution.py:16
  76.0 3.3 %collective-permute-start.24 = (f32[32,128]{1,0:T(8,128)S(1)}, f32[32,128]{1,0:T(8,128)S(1)}, u32[]{:S(2)}, u32[]{:S(2)}) collective-permute-start(f32[32,128]{1,0:T(8,128)S(1)} %get-tuple-element.25), channel_id=1, source_target_pairs={{0,24},{8,0},{16,8},{24,16},{1,25},{9,1},{17,9},{25,17},{2,26},{10... | collective-permute-start | bytes 49160 | tf_op jit(solution)/shard_map/ppermute | solution.py:16
  76.0 3.8 %collective-permute-start.23 = (f32[32,128]{1,0:T(8,128)S(1)}, f32[32,128]{1,0:T(8,128)S(1)}, u32[]{:S(2)}, u32[]{:S(2)}) collective-permute-start(f32[32,128]{1,0:T(8,128)S(1)} %get-tuple-element.26), channel_id=1, source_target_pairs={{0,16},{8,24},{16,0},{24,8},{1,17},{9,25},{17,1},{25,9},{2,18},{10... | collective-permute-start | bytes 49160 | tf_op jit(solution)/shard_map/ppermute | solution.py:16
  77.6 3.2 %collective-permute-start.22 = (f32[32,128]{1,0:T(8,128)S(1)}, f32[32,128]{1,0:T(8,128)S(1)}, u32[]{:S(2)}, u32[]{:S(2)}) collective-permute-start(f32[32,128]{1,0:T(8,128)S(1)} %get-tuple-element.23), channel_id=1, source_target_pairs={{0,8},{8,16},{16,24},{24,0},{1,9},{9,17},{17,25},{25,1},{2,10},{10... | collective-permute-start | bytes 49160 | tf_op jit(solution)/shard_map/ppermute | solution.py:16
  (14 other events, 27.0 us)
where the time goes:
time: 82.6 us; the launch traced here: 81.4 us
  starting transfers between devices  29.6 us (36%)
  local copies, waits for them, and re-layouts  19.9 us (24%)
  matrix products  14.7 us (18%)
  other arithmetic  10.3 us (12%)
  waiting for transfers between devices  5.57 us (7%)
  between operations  1.23 us (1%)
    ppermute x26, starting transfers between devices, shifted(): lax.ppermute(value, axis, [(i, (i + by) % peers) for i in range(peers)])  29.6 us
    unnamed x61, local copies, waits for them, and re-layouts  10.4 us
    reshape x1, local copies, waits for them, and re-layouts, tile_grads(): jnp.dot(tgt_onehot, cot_block, precision=highest)  5.85 us
    ppermute x26, waiting for transfers between devices, shifted(): lax.ppermute(value, axis, [(i, (i + by) % peers) for i in range(peers)])  5.57 us
    dot_general x1, matrix products, tile_grads(): jnp.dot(tgt_onehot, cot_block, precision=highest)  4.25 us
    mul x1, other arithmetic, tile_grads(): weighted = gathered_cot * gathered_feats[:, None, :]  4.08 us
    dot_general x2, matrix products, tile_geometry(): jnp.dot(radial_basis, w_in, precision=highest)  3.7 us
    dot_general x2, matrix products, tile_geometry(): jnp.dot(hidden, w_out, precision=highest).reshape(pair_count, 3, channels)  2.43 us
  transfers between devices with their start and end apart: 26, of which 6 were waited for; matrix products, arithmetic and copies ran while one was open for 27% of the time, Pallas kernels for 0%

commit v1 on v0

v1 whole, which is shorter than its diff:
```python
import functools
import math

import jax
import jax.numpy as jnp
from jax import lax
from jax.experimental import pallas as pl
from jax.experimental.pallas import tpu as pltpu
from jax.sharding import PartitionSpec as P

domain_side = 5.0
cutoff = 12.0
soften = 0.25
reach = 2
sublanes = 8
f32 = jnp.float32
bf16 = jnp.bfloat16


class Link:
    def __init__(self, step, bit, peers):
        self.step, self.bit, self.peers = step, bit, peers

    def delta(self, i):
        return self.step if self.bit is None else self.step * (1 - 2 * ((i >> self.bit) & 1))

    def fetch(self, value, axis):
        n = self.peers
        return lax.ppermute(value, axis, [((i + self.delta(i)) % n, i) for i in range(n)])

    def give(self, value, axis):
        n = self.peers
        return lax.ppermute(value, axis, [(i, (i + self.delta(i)) % n) for i in range(n)])


def links_of(peers):
    if peers % 4 == 0:
        steps = [(1, 0), (-1, 0), (2, 1)] + ([(-2, 1)] if peers > 4 else [])
    else:
        steps = [(1, None), (-1, None), (2, None), (-2, None)]
    return [Link(step, bit, peers) for step, bit in steps]


def spots_of(links):
    spots = [(0, None, 0)]
    for table, link in enumerate(links):
        spots.append((table + 1, link, 1))
        if link.peers == 4 and abs(link.step) == 2:
            spots.append((table + 1, link, -1))
    return spots


def pieces(x, count):
    out = []
    for _ in range(count):
        out.append(x.astype(bf16).astype(f32))
        x = x - out[-1]
    return out


def dot(a, b):
    return jnp.dot(a, b, preferred_element_type=f32)


def dot_rows(a, b):
    return lax.dot_general(a, b, (((1,), (1,)), ((), ())), preferred_element_type=f32)


def dot_cols(a, b):
    return lax.dot_general(a, b, (((0,), (0,)), ((), ())), preferred_element_type=f32)


def pack_kernel(pos_ref, feat_ref, cot_ref, gx_ref, gy_ref):
    atoms, channels = feat_ref.shape[2:]
    gx_ref[0:atoms] = feat_ref[0, 0]
    gy_ref[0:atoms] = cot_ref[0, 0]
    zero = jnp.zeros((sublanes, channels), f32)
    gx_ref[atoms:] = zero
    gy_ref[atoms:, 0:channels] = zero
    gx_ref[atoms : atoms + 3, 0:atoms] = pos_ref[0, 0]
    gy_ref[atoms : atoms + 3, 0:atoms] = pos_ref[0, 0]


def prep_kernel(
    gx_spots, gy_spots, place_ref, src_ref, tgt_ref, mask_ref, spec_ref, in_ref, emb_ref, out_ref,
    rows_ref, wide_ref, back_ref, first_ref,
):
    atoms = pairs = src_ref.shape[4]
    at_x, at_y = place_ref[0], place_ref[1]
    rows_ref[...] = jnp.zeros(rows_ref.shape, jnp.int32)
    for spot, (_, gy_link, gy_sign) in enumerate(gy_spots):
        step_y = 0 if gy_link is None else gy_sign * gy_link.delta(at_y)
        for slot, (table, gx_link, gx_sign) in enumerate(gx_spots):
            step_x = 0 if gx_link is None else gx_sign * gx_link.delta(at_x)
            lanes = slice(slot * pairs, (slot + 1) * pairs)
            tile = (0, 0, pl.ds(reach + step_x, 1), pl.ds(reach + step_y, 1))
            rows_ref[spot, 0:1, lanes] = src_ref[tile][0, 0:1] + table * atoms
            rows_ref[spot, 1:2, lanes] = tgt_ref[tile][0, 0:1]
            rows_ref[spot, 2:3, lanes] = mask_ref[tile][0, 0:1]
            rows_ref[spot, 3:4, lanes] = spec_ref[tile][0, 0:1]
            rows_ref[spot, 4:5, lanes] = jnp.full((1, pairs), step_x, jnp.int32)
            rows_ref[spot, 5:6, lanes] = jnp.full((1, pairs), -step_y, jnp.int32)
    high, low = pieces(out_ref[...], 2)
    back_ref[...] = jnp.concatenate([high, high, low], axis=1).astype(bf16)
    wide_ref[...] = jnp.concatenate([high, high, low], axis=0).T.astype(bf16)
    orders, hidden = in_ref.shape
    kinds = emb_ref.shape[0]
    spare = first_ref.shape[0] - orders - kinds
    parts = [in_ref[...], emb_ref[...], jnp.zeros((spare, hidden), f32)]
    first_ref[...] = jnp.concatenate(parts, axis=0)


def radial_waves(dist, orders):
    order = (lax.broadcasted_iota(jnp.int32, (orders, 1), 0) + 1).astype(f32)
    turn = order * (dist * (1.0 / cutoff))
    whole = jnp.floor(turn + 0.5)
    part = turn - whole
    sign = 1.0 - 2.0 * (whole - 2.0 * jnp.floor(0.5 * whole))
    square = part * part
    sine = jnp.zeros_like(square)
    for k in (11, 9, 7, 5, 3, 1):
        sine = sine * square + (-1.0) ** (k // 2) * math.pi**k / math.factorial(k)
    cosine = jnp.zeros_like(square)
    for k in (12, 10, 8, 6, 4, 2, 0):
        cosine = cosine * square + (-1.0) ** (k // 2) * math.pi**k / math.factorial(k)
    return order, sign * part * sine, sign * cosine


def spot_grads(rows, cot_ref, src_pos, feats, first, wide, back, orders):
    slots = rows.shape[1]
    sources = feats[0].shape[1]
    atoms = cot_ref.shape[0] - sublanes
    channels = feats[0].shape[0]
    hidden = first.shape[1]

    def onehot(ids, count):
        return jnp.where(lax.broadcasted_iota(jnp.int32, (count, slots), 0) == ids, 1.0, 0.0)

    src_hot = onehot(rows[0:1], sources).astype(bf16)
    tgt_hot32 = onehot(rows[1:2], atoms)
    tgt_hot = tgt_hot32.astype(bf16)
    mask = rows[2:3].astype(f32)
    offset = rows[4:6].astype(f32) * domain_side

    tgt_pos = jnp.concatenate(pieces(cot_ref[atoms:, 0:atoms], 3), axis=0).astype(bf16)
    from_src = dot(src_pos, src_hot)
    from_tgt = dot(tgt_pos, tgt_hot)
    from_src = from_src[0:8] + from_src[8:16] + from_src[16:24]
    from_tgt = from_tgt[0:8] + from_tgt[8:16] + from_tgt[16:24]
    rel = [
        from_src[0:1] + offset[0:1] - from_tgt[0:1],
        from_src[1:2] + offset[1:2] - from_tgt[1:2],
        from_src[2:3] - from_tgt[2:3],
    ]
    dist = jnp.sqrt(rel[0] * rel[0] + rel[1] * rel[1] + rel[2] * rel[2] + soften)
    near = 1.0 / dist
    x, y, z = (r * near for r in rel)
    scaled = dist * (1.0 / cutoff)
    room = jnp.where(scaled < 1.0, 1.0 - scaled * scaled, 0.0)
    env = room * room * mask
    d_env = (-4.0 / cutoff) * scaled * room * mask

    order, sine, cosine = radial_waves(dist, orders)
    norm = math.sqrt(2.0 / cutoff)
    basis = norm * near * sine
    d_basis = norm * near * ((math.pi / cutoff) * order * cosine - sine * near)
    species = onehot(rows[3:4], first.shape[0] - orders)
    before = lax.dot_general(
        first, jnp.concatenate([basis, species], axis=0), (((0,), (0,)), ((), ())),
        precision=lax.Precision.HIGHEST, preferred_element_type=f32,
    )
    gate = 1.0 / (1.0 + jnp.exp(-before))
    act = before * gate
    d_act = gate * (1.0 + before * (1.0 - gate))
    act_high, act_low = pieces(act, 2)
    radial = dot(wide, jnp.concatenate([act_high, act_low, act_high], axis=0).astype(bf16))

    gathered = dot(feats[0], src_hot) + dot(feats[1], src_hot)

    root3, root5, root15 = math.sqrt(3.0), math.sqrt(5.0), math.sqrt(15.0)
    shapes = [
        None, root3 * x, root3 * y, root3 * z, root15 * x * y, root15 * y * z,
        0.5 * root5 * (2.0 * z * z - x * x - y * y), root15 * x * z, 0.5 * root15 * (x * x - y * y),
    ]
    tgt_twice = jnp.concatenate([tgt_hot32, tgt_hot32], axis=0).astype(bf16)
    d_shapes = [None] * 9
    d_radial = []
    through = None
    for low, high in ((0, 1), (1, 4), (4, 9)):
        l = len(d_radial)
        own = radial[l * channels : (l + 1) * channels]
        with_feats = own * gathered
        total = None
        for m in range(low, high):
            block = cot_ref[0:atoms, m * channels : (m + 1) * channels]
            cot = dot_cols(jnp.concatenate(pieces(block, 2), axis=0).astype(bf16), tgt_twice)
            if m:
                d_shapes[m] = jnp.sum(with_feats * cot, axis=0, keepdims=True) * env
                cot = cot * shapes[m]
            total = cot if total is None else total + cot
        d_radial.append(total * gathered)
        own = own * total
        through = own if through is None else through + own
    to_env = jnp.sum(through * gathered, axis=0, keepdims=True)
    through = through * env
    d_radial = jnp.concatenate(d_radial, axis=0) * env
    d_high, d_low = pieces(d_radial, 2)
    d_hidden = dot(back, jnp.concatenate([d_high, d_low, d_high], axis=0).astype(bf16))
    d_before = d_hidden * d_act
    to_basis = lax.dot_general(
        first[0:orders], d_before, (((1,), (0,)), ((), ())),
        precision=lax.Precision.HIGHEST, preferred_element_type=f32,
    )
    d_dist = jnp.sum(to_basis * d_basis, axis=0, keepdims=True) + to_env * d_env

    s = d_shapes
    d_x = root3 * s[1] + root15 * (y * s[4] + z * s[7] + x * s[8]) - root5 * x * s[6]
    d_y = root3 * s[2] + root15 * (x * s[4] + z * s[5] - y * s[8]) - root5 * y * s[6]
    d_z = root3 * s[3] + root15 * (y * s[5] + x * s[7]) + 2.0 * root5 * z * s[6]
    d_dist = d_dist - near * (x * d_x + y * d_y + z * d_z)
    grad = jnp.concatenate(
        [near * d_x + x * d_dist, near * d_y + y * d_dist, near * d_z + z * d_dist,
         jnp.zeros((sublanes - 3, slots), f32)], axis=0,
    )
    grad = jnp.concatenate(pieces(grad, 2), axis=0).astype(bf16)
    pos_src = dot_rows(grad, src_hot)
    pos_tgt = dot_rows(grad, tgt_hot)
    through_high, through_low = (p.astype(bf16) for p in pieces(through, 2))
    feat_src = dot_rows(src_hot, through_high) + dot_rows(src_hot, through_low)
    return pos_src[0:8] + pos_src[8:16], -(pos_tgt[0:8] + pos_tgt[8:16]), feat_src


def main_kernel(gy_spots, gx_count, gy_count, orders, *refs):
    rows_ref, wide_ref, back_ref, first_ref = refs[:4]
    gx_refs = refs[4 : 4 + gx_count]
    gy_refs = refs[4 + gx_count : 4 + gx_count + gy_count]
    outs = refs[4 + gx_count + gy_count :]
    gx_outs, gy_outs, place = outs[:gx_count], outs[gx_count : gx_count + gy_count], outs[-1]
    atoms = gx_refs[0].shape[0] - sublanes
    for table, ref in enumerate(gx_refs):
        place[:, table * atoms : (table + 1) * atoms] = ref[atoms:, 0:atoms]
    src_pos = jnp.concatenate(pieces(place[...], 3), axis=0).astype(bf16)
    feats = jnp.concatenate([ref[0:atoms] for ref in gx_refs], axis=0).T
    feats = [p.astype(bf16) for p in pieces(feats, 2)]
    first, wide, back = first_ref[...], wide_ref[...], back_ref[...]
    pos_sum = feat_sum = None
    tgt_sums = [None] * gy_count
    for spot, (table, _, _) in enumerate(gy_spots):
        pos_src, pos_tgt, feat_src = spot_grads(
            rows_ref[spot], gy_refs[table], src_pos, feats, first, wide, back, orders
        )
        pos_sum = pos_src if pos_sum is None else pos_sum + pos_src
        feat_sum = feat_src if feat_sum is None else feat_sum + feat_src
        held = tgt_sums[table]
        tgt_sums[table] = pos_tgt if held is None else held + pos_tgt
    for table, ref in enumerate(gx_outs):
        part = slice(table * atoms, (table + 1) * atoms)
        ref[0:atoms] = feat_sum[part]
        ref[atoms:] = jnp.zeros((sublanes, ref.shape[1]), f32)
        ref[atoms:, 0:atoms] = pos_sum[:, part]
    for total, ref in zip(tgt_sums, gy_outs):
        ref[...] = jnp.zeros(ref.shape, f32)
        ref[:, 0:atoms] = total


def sum_kernel(gx_count, *refs):
    gx_refs, gy_refs = refs[:gx_count], refs[gx_count:-2]
    pos_ref, feat_ref = refs[-2:]
    atoms = pos_ref.shape[3]
    feat = gx_refs[0][...]
    for ref in gx_refs[1:]:
        feat = feat + ref[...]
    pos = feat[atoms : atoms + 3, 0:atoms]
    for ref in gy_refs:
        pos = pos + ref[0:3, 0:atoms]
    pos_ref[0, 0] = pos
    feat_ref[0, 0] = feat[0:atoms]


vmem = pl.BlockSpec(memory_space=pltpu.VMEM)
smem = pl.BlockSpec(memory_space=pltpu.SMEM)


def local(
    gx_size, gy_size, positions, features, cotangent, nbr_src, nbr_tgt, pair_mask, pair_species,
    w_in, species_emb, w_out,
):
    atoms, channels = features.shape[2:]
    wide = cotangent.shape[3]
    steps, _, pairs = nbr_src.shape[2:]
    orders, hidden = w_in.shape
    kinds = species_emb.shape[0]
    slots = steps * pairs
    gx_links, gy_links = links_of(gx_size), links_of(gy_size)
    gx_spots, gy_spots = spots_of(gx_links), spots_of(gy_links)
    gx_count, gy_count = len(gx_links) + 1, len(gy_links) + 1
    sds = jax.ShapeDtypeStruct

    gx_own, gy_own = pl.pallas_call(
        pack_kernel,
        out_shape=(sds((atoms + sublanes, channels), f32), sds((atoms + sublanes, wide), f32)),
        in_specs=[vmem] * 3,
        out_specs=(vmem, vmem),
        name="pack",
    )(positions, features, cotangent)
    gy_packs = [gy_own] + [link.fetch(gy_own, "gy") for link in gy_links]
    gx_packs = [gx_own] + [link.fetch(gx_own, "gx") for link in gx_links]

    place = jnp.stack([lax.axis_index("gx"), lax.axis_index("gy")]).astype(jnp.int32)
    padded = -(-(orders + kinds) // sublanes) * sublanes
    prepared = pl.pallas_call(
        functools.partial(prep_kernel, gx_spots, gy_spots),
        out_shape=(
            sds((len(gy_spots), sublanes, slots), jnp.int32),
            sds((w_out.shape[1], 3 * hidden), bf16),
            sds((hidden, 3 * w_out.shape[1]), bf16),
            sds((padded, hidden), f32),
        ),
        in_specs=[smem] + [vmem] * 7,
        out_specs=(vmem,) * 4,
        name="prepare",
    )(place, nbr_src, nbr_tgt, pair_mask, pair_species, w_in, species_emb, w_out)

    outs = pl.pallas_call(
        functools.partial(main_kernel, gy_spots, gx_count, gy_count, orders),
        out_shape=(sds((atoms + sublanes, channels), f32),) * gx_count
        + (sds((sublanes, channels), f32),) * gy_count,
        in_specs=[vmem] * (4 + gx_count + gy_count),
        out_specs=(vmem,) * (gx_count + gy_count),
        scratch_shapes=[pltpu.VMEM((sublanes, gx_count * atoms), f32)],
        compiler_params=pltpu.CompilerParams(vmem_limit_bytes=32 * 1024 * 1024),
        name="tiles",
    )(*prepared, *gx_packs, *gy_packs)
    gx_outs, gy_outs = list(outs[:gx_count]), list(outs[gx_count:])
    gx_back = gx_outs[:1] + [l.give(o, "gx") for l, o in zip(gx_links, gx_outs[1:])]
    gy_back = gy_outs[:1] + [l.give(o, "gy") for l, o in zip(gy_links, gy_outs[1:])]
    return pl.pallas_call(
        functools.partial(sum_kernel, gx_count),
        out_shape=(sds(positions.shape, f32), sds(features.shape, f32)),
        in_specs=[vmem] * (gx_count + gy_count),
        out_specs=(vmem, vmem),
        name="sums",
    )(*gx_back, *gy_back)


def solution(mesh):
    split = [P("gx", "gy")] * 7 + [P()] * 3
    return jax.shard_map(
        functools.partial(local, mesh.shape["gx"], mesh.shape["gy"]),
        mesh=mesh,
        in_specs=tuple(split),
        out_specs=(P("gx", "gy"), P("gx", "gy")),
        check_vma=False,
    )
```

time: 82.6 us -> 52.7 us (0.64)
  matrix products: 14.7 us -> 0 us
  starting transfers between devices: 29.6 us -> 15.7 us
  Pallas kernels: 0 us -> 10.9 us
  local copies, waits for them, and re-layouts: 19.9 us -> 9.37 us
  other arithmetic: 10.3 us -> 0.6 us
  waiting for transfers between devices: 5.57 us -> 14.9 us
    dot_general x12 -> x0, matrix products: 14.7 us -> none  [the longest x1 4.25 us: tile_grads(): jnp.dot(tgt_onehot, cot_block, precision=highest)]
    ppermute x26 -> x14, starting transfers between devices: 29.6 us -> 15.7 us  [the longest x7 10.2 us: fetch(): lax.ppermute(value, axis, [((i + self.delta(i)) % n, i) for i in range(n)])]
    pallas_call x0 -> x4, Pallas kernels: none -> 10.9 us  [the longest x1 6.07 us: local(): pl.pallas_call(functools.partial(main_kernel, gy_spots, gx_count, gy_coun...]
    ppermute x26 -> x14, waiting for transfers between devices: 5.57 us -> 14.9 us  [the longest x7 8.79 us: give(): lax.ppermute(value, axis, [(i, (i + self.delta(i)) % n) for i in range(n)])]
    reshape x2 -> x0, local copies, waits for them, and re-layouts: 6.39 us -> none  [the longest x1 5.85 us: tile_grads(): jnp.dot(tgt_onehot, cot_block, precision=highest)]
    mul x8 -> x0, other arithmetic: 5.44 us -> none  [the longest x1 4.08 us: tile_grads(): weighted = gathered_cot * gathered_feats[:, None, :]]
    reduce_sum x5 -> x0, other arithmetic: 2.45 us -> none  [the longest x1 1.23 us: tile_grads(): sum_two = jnp.sum(weighted[:, 4:9] * sph[:, 4:9, None], axis=1)]
    unnamed x61 -> x43, local copies, waits for them, and re-layouts: 10.4 us -> 8.15 us
  transfers between devices with their start and end apart: 26 -> 14, of which waited for: 6 -> 6; matrix products, arithmetic and copies ran while one was open for 27% -> 6% of each run, Pallas kernels for 0% -> 3%
where the time goes in v1:
time: 52.7 us; the launch traced here: 52.2 us
  starting transfers between devices  15.7 us (30%)
  waiting for transfers between devices  14.9 us (28%)
  Pallas kernels  10.9 us (21%)
  local copies, waits for them, and re-layouts  9.37 us (18%)
  between operations  0.77 us (1%)
  other arithmetic  0.6 us (1%)
    ppermute x7, starting transfers between devices, fetch(): lax.ppermute(value, axis, [((i + self.delta(i)) % n, i) for i in range(n)])  10.2 us
    ppermute x7, waiting for transfers between devices, give(): lax.ppermute(value, axis, [(i, (i + self.delta(i)) % n) for i in range(n)])  8.79 us
    unnamed x43, local copies, waits for them, and re-layouts  8.15 us
    ppermute x7, waiting for transfers between devices, fetch(): lax.ppermute(value, axis, [((i + self.delta(i)) % n, i) for i in range(n)])  6.11 us
    pallas_call x1, Pallas kernels, local(): pl.pallas_call(functools.partial(main_kernel, gy_spots, gx_count, gy_coun...  6.07 us
    ppermute x7, starting transfers between devices, give(): lax.ppermute(value, axis, [(i, (i + self.delta(i)) % n) for i in range(n)])  5.47 us
    pallas_call x1, Pallas kernels, local(): pl.pallas_call(functools.partial(prep_kernel, gx_spots, gy_spots), out_sh...  1.77 us
    pallas_call x1, Pallas kernels, local(): pl.pallas_call(pack_kernel, out_shape=(sds((atoms + sublanes, channels),...  1.68 us
  transfers between devices with their start and end apart: 14, of which 6 were waited for; matrix products, arithmetic and copies ran while one was open for 6% of the time, Pallas kernels for 3%

profile of v1, /device:TPU:0, one launch (start us, length us, event | category | flops | bytes accessed | tf_op | source)
XLA Modules:
  0.0 52.2 jit_solution(13295143788866023218)
XLA Ops:
  0.6 1.3 %copy.16.pos_ref = f32[1,1,3,32]{3,2,1,0:T(4,128)} copy(f32[1,1,3,32]{3,1,2,0:T(1,128)} %param.10) | data formatting | bytes 768 | tf_op args[0]
  1.9 1.7 %pack.1 = (f32[40,128]{1,0:T(8,128)}, f32[40,1152]{1,0:T(8,128)}) custom-call(f32[1,1,3,32]{3,2,1,0:T(4,128)} %copy.16.pos_ref, f32[1,1,32,128]{3,2,1,0:T(8,128)} %feat_ref.1, f32[1,1,32,1152]{3,2,1,0:T(8,128)} %cot_ref.1), custom_call_target="tpu_custom_call" | custom-call | tf_op jit(solution)/shard_map/pack/pallas_call | solution.py:299
  3.6 5.0 %collective-permute-start.6 = (f32[40,1152]{1,0:T(8,128)}, f32[40,1152]{1,0:T(8,128)S(1)}, u32[]{:S(2)}, u32[]{:S(2)}) collective-permute-start(f32[40,1152]{1,0:T(8,128)} %get-tuple-element.22.refs_8_), channel_id=1, source_target_pairs={{6,0},{7,1},{4,2},{5,3},{2,4},{3,5},{0,6},{1,7},{14,8},{15,9},{12,... | collective-permute-start | bytes 552968 | tf_op jit(solution)/shard_map/ppermute | solution.py:29
  8.6 1.9 %collective-permute-start.4 = (f32[40,1152]{1,0:T(8,128)}, f32[40,1152]{1,0:T(8,128)S(1)}, u32[]{:S(2)}, u32[]{:S(2)}) collective-permute-start(f32[40,1152]{1,0:T(8,128)} %get-tuple-element.22.refs_8_), channel_id=1, source_target_pairs={{7,0},{2,1},{1,2},{4,3},{3,4},{6,5},{5,6},{0,7},{15,8},{10,9},{9,1... | collective-permute-start | bytes 552968 | tf_op jit(solution)/shard_map/ppermute | solution.py:29
  10.5 1.6 %collective-permute-start.3 = (f32[40,1152]{1,0:T(8,128)}, f32[40,1152]{1,0:T(8,128)S(1)}, u32[]{:S(2)}, u32[]{:S(2)}) collective-permute-start(f32[40,1152]{1,0:T(8,128)} %get-tuple-element.22.refs_8_), channel_id=1, source_target_pairs={{1,0},{0,1},{3,2},{2,3},{5,4},{4,5},{7,6},{6,7},{9,8},{8,9},{11,10... | collective-permute-start | bytes 552968 | tf_op jit(solution)/shard_map/ppermute | solution.py:29
  12.1 1.5 %collective-permute-start.2 = (f32[40,128]{1,0:T(8,128)}, f32[40,128]{1,0:T(8,128)S(1)}, u32[]{:S(2)}, u32[]{:S(2)}) collective-permute-start(f32[40,128]{1,0:T(8,128)} %get-tuple-element.21.refs_4_), channel_id=1, source_target_pairs={{16,0},{24,8},{0,16},{8,24},{17,1},{25,9},{1,17},{9,25},{18,2},{26... | collective-permute-start | bytes 61448 | tf_op jit(solution)/shard_map/ppermute | solution.py:29
  13.6 2.5 %collective-permute-done.2.refs_7_ = f32[40,128]{1,0:T(8,128)S(1)} collective-permute-done((f32[40,128]{1,0:T(8,128)}, f32[40,128]{1,0:T(8,128)S(1)}, u32[]{:S(2)}, u32[]{:S(2)}) %collective-permute-start.2) | collective-permute-done | bytes 20512 | tf_op jit(solution)/shard_map/ppermute | solution.py:29
  16.1 3.6 %collective-permute-done.1.refs_6_ = f32[40,128]{1,0:T(8,128)S(1)} collective-permute-done((f32[40,128]{1,0:T(8,128)}, f32[40,128]{1,0:T(8,128)S(1)}, u32[]{:S(2)}, u32[]{:S(2)}) %collective-permute-start.1) | collective-permute-done | bytes 20512 | tf_op jit(solution)/shard_map/ppermute | solution.py:29
  19.9 0.6 %pad_add_fusion.place_ref = s32[2]{0:T(128)} fusion(s32[1]{0:T(128)} %bitcast.1, s32[1]{0:T(128)} %bitcast), kind=kLoop, calls=%fused_computation | loop fusion | flops 2 | bytes 16 | tf_op jit(solution)/shard_map/stack | solution.py:309
  20.5 0.6 %copy.12.src_ref = s32[1,1,5,5,32]{4,3,2,1,0:T(8,128)} copy(s32[1,1,5,5,32]{4,1,3,2,0:T(1,128)S(1)} %copy-done.11) | data formatting | bytes 6400 | tf_op args[3]
  21.1 0.6 %copy.13.tgt_ref = s32[1,1,5,5,32]{4,3,2,1,0:T(8,128)} copy(s32[1,1,5,5,32]{4,1,3,2,0:T(1,128)S(1)} %copy-done.12) | data formatting | bytes 6400 | tf_op args[4]
  21.7 0.6 %copy.14.mask_ref = s32[1,1,5,5,32]{4,3,2,1,0:T(8,128)} copy(s32[1,1,5,5,32]{4,1,3,2,0:T(1,128)S(1)} %copy-done.13) | data formatting | bytes 6400 | tf_op args[5]
  22.3 0.6 %copy.15.spec_ref = s32[1,1,5,5,32]{4,3,2,1,0:T(8,128)} copy(s32[1,1,5,5,32]{4,1,3,2,0:T(1,128)S(1)} %copy-done.14) | data formatting | bytes 6400 | tf_op args[6]
  22.9 1.8 %prepare.1 = (s32[5,8,160]{2,1,0:T(8,128)}, bf16[384,96]{1,0:T(8,128)(2,1)}, bf16[32,1152]{1,0:T(8,128)(2,1)}, f32[24,32]{1,0:T(8,128)}) custom-call(s32[2]{0:T(128)} %pad_add_fusion.place_ref, s32[1,1,5,5,32]{4,3,2,1,0:T(8,128)} %copy.12.src_ref, s32[1,1,5,5,32]{4,3,2,1,0:T(8,128)} %copy.13.tgt_ref, s32[1,1,5,5,32]{4,3,2,1,0:T(8,128)} %copy.14.mask_ref, ...), custom_call_target="tpu_custom_call" | custom-call | tf_op jit(solution)/shard_map/prepare/pallas_call | solution.py:311
  24.7 0.9 %copy-done.1 = bf16[384,96]{1,0:T(8,128)(2,1)S(1)} copy-done((bf16[384,96]{1,0:T(8,128)(2,1)S(1)}, bf16[384,96]{1,0:T(8,128)(2,1)}, u32[]{:S(2)}) %copy-start.1) | copy-done | bytes 73752
  25.6 0.9 %copy-done.2 = bf16[32,1152]{1,0:T(8,128)(2,1)S(1)} copy-done((bf16[32,1152]{1,0:T(8,128)(2,1)S(1)}, bf16[32,1152]{1,0:T(8,128)(2,1)}, u32[]{:S(2)}) %copy-start.2) | copy-done | bytes 73752
  26.5 0.8 %copy-done.3 = s32[5,8,160]{2,1,0:T(8,128)S(1)} copy-done((s32[5,8,160]{2,1,0:T(8,128)S(1)}, s32[5,8,160]{2,1,0:T(8,128)}, u32[]{:S(2)}) %copy-start.3) | copy-done | bytes 25624
  27.3 0.7 %copy-done.6 = f32[24,32]{1,0:T(8,128)S(1)} copy-done((f32[24,32]{1,0:T(8,128)S(1)}, f32[24,32]{1,0:T(8,128)}, u32[]{:S(2)}) %copy-start.6) | copy-done | bytes 3096
  28.0 6.1 %tiles.1 = (f32[40,128]{1,0:T(8,128)S(1)}, f32[40,128]{1,0:T(8,128)S(1)}, f32[40,128]{1,0:T(8,128)S(1)}, f32[40,128]{1,0:T(8,128)S(1)}, f32[8,128]{1,0:T(8,128)S...) custom-call(s32[5,8,160]{2,1,0:T(8,128)S(1)} %copy-done.3, ...), custom_call_target="tpu_custom_call" | custom-call | tf_op jit(solution)/shard_map/tiles/pallas_call | solution.py:324
  34.1 0.6 %copy-done.4 = f32[40,128]{1,0:T(8,128)} copy-done((f32[40,128]{1,0:T(8,128)}, f32[40,128]{1,0:T(8,128)S(1)}, u32[]{:S(2)}) %copy-start.4) | copy-done | bytes 20504
  34.7 0.3 collective-permute-start.7
  35.0 0.9 %collective-permute-start.8 = (f32[40,128]{1,0:T(8,128)S(1)}, f32[40,128]{1,0:T(8,128)S(1)}, u32[]{:S(2)}, u32[]{:S(2)}) collective-permute-start(f32[40,128]{1,0:T(8,128)S(1)} %get-tuple-element.25), channel_id=1, source_target_pairs={{0,24},{8,16},{16,8},{24,0},{1,25},{9,17},{17,9},{25,1},{2,26},{10... | collective-permute-start | bytes 61448 | tf_op jit(solution)/shard_map/ppermute | solution.py:33
  36.0 0.9 %collective-permute-start.9 = (f32[40,128]{1,0:T(8,128)S(1)}, f32[40,128]{1,0:T(8,128)S(1)}, u32[]{:S(2)}, u32[]{:S(2)}) collective-permute-start(f32[40,128]{1,0:T(8,128)S(1)} %get-tuple-element.26), channel_id=1, source_target_pairs={{0,16},{8,24},{16,0},{24,8},{1,17},{9,25},{17,1},{25,9},{2,18},{10... | collective-permute-start | bytes 61448 | tf_op jit(solution)/shard_map/ppermute | solution.py:33
  36.8 0.4 collective-permute-start.10
  37.2 2.9 %collective-permute-start.11 = (f32[8,128]{1,0:T(8,128)S(1)}, f32[8,128]{1,0:T(8,128)S(1)}, u32[]{:S(2)}, u32[]{:S(2)}) collective-permute-start(f32[8,128]{1,0:T(8,128)S(1)} %get-tuple-element.29), channel_id=1, source_target_pairs={{0,7},{1,2},{2,1},{3,4},{4,3},{5,6},{6,5},{7,0},{8,15},{9,10},{10,... | collective-permute-start | bytes 12296 | tf_op jit(solution)/shard_map/ppermute | solution.py:33
  40.1 0.3 collective-permute-done.10.refs_5_
  40.5 3.0 %collective-permute-done.11.refs_6_ = f32[8,128]{1,0:T(8,128)S(1)} collective-permute-done((f32[8,128]{1,0:T(8,128)S(1)}, f32[8,128]{1,0:T(8,128)S(1)}, u32[]{:S(2)}, u32[]{:S(2)}) %collective-permute-start.11) | collective-permute-done | bytes 4128 | tf_op jit(solution)/shard_map/ppermute | solution.py:33
  43.5 0.5 collective-permute-done.12.refs_7_
  44.0 4.9 %collective-permute-done.13.refs_8_ = f32[8,128]{1,0:T(8,128)S(1)} collective-permute-done((f32[8,128]{1,0:T(8,128)S(1)}, f32[8,128]{1,0:T(8,128)S(1)}, u32[]{:S(2)}, u32[]{:S(2)}) %collective-permute-start.13) | collective-permute-done | bytes 4128 | tf_op jit(solution)/shard_map/ppermute | solution.py:33
  49.0 0.5 copy-done.18
  49.6 1.4 %sums.1 = (f32[1,1,3,32]{3,2,1,0:T(4,128)}, f32[1,1,32,128]{3,2,1,0:T(8,128)}) custom-call(f32[40,128]{1,0:T(8,128)} %copy-done.4, f32[40,128]{1,0:T(8,128)} %copy-done.8, f32[40,128]{1,0:T(8,128)} %copy-done.9, f32[40,128]{1,0:T(8,128)} %copy-done.10, f32[8,128]{1,0:T(8,128)} %copy-done.7, f32[8,128]{1,0:T(8,128)} %copy-done.15, f32[8,128]{1,0:T(8,128)} %copy-done.16, ...), custom_call_target="tpu_custom_call" | custom-call | tf_op jit(solution)/shard_map/sums/pallas_call | solution.py:337
  51.0 1.2 %copy.17 = f32[1,1,3,32]{3,1,2,0:T(1,128)} copy(f32[1,1,3,32]{3,2,1,0:T(4,128)} %get-tuple-element.32) | data formatting | bytes 768 | tf_op jit(solution)/shard_map/sums/pallas_call | solution.py:337
  (45 shorter events, 0.3 us)
Async XLA Ops:
  1.9 18.6 %copy-start.11 = (s32[1,1,5,5,32]{4,1,3,2,0:T(1,128)S(1)}, s32[1,1,5,5,32]{4,1,3,2,0:T(1,128)}, u32[]{:S(2)}) copy-start(s32[1,1,5,5,32]{4,1,3,2,0:T(1,128)} %param.13) | copy-start | bytes 9604
  1.9 19.2 %copy-start.12 = (s32[1,1,5,5,32]{4,1,3,2,0:T(1,128)S(1)}, s32[1,1,5,5,32]{4,1,3,2,0:T(1,128)}, u32[]{:S(2)}) copy-start(s32[1,1,5,5,32]{4,1,3,2,0:T(1,128)} %param.14) | copy-start | bytes 9604
  1.9 19.8 %copy-start.13 = (s32[1,1,5,5,32]{4,1,3,2,0:T(1,128)S(1)}, s32[1,1,5,5,32]{4,1,3,2,0:T(1,128)}, u32[]{:S(2)}) copy-start(s32[1,1,5,5,32]{4,1,3,2,0:T(1,128)} %param.15) | copy-start | bytes 9604
  1.9 20.4 %copy-start.14 = (s32[1,1,5,5,32]{4,1,3,2,0:T(1,128)S(1)}, s32[1,1,5,5,32]{4,1,3,2,0:T(1,128)}, u32[]{:S(2)}) copy-start(s32[1,1,5,5,32]{4,1,3,2,0:T(1,128)} %param.16) | copy-start | bytes 9604
  3.6 21.1 %copy-start = (f32[40,1152]{1,0:T(8,128)S(1)}, f32[40,1152]{1,0:T(8,128)}, u32[]{:S(2)}) copy-start(f32[40,1152]{1,0:T(8,128)} %get-tuple-element.22.refs_8_) | copy-start | bytes 552964
  3.6 21.1 %collective-permute-start.6 = (f32[40,1152]{1,0:T(8,128)}, f32[40,1152]{1,0:T(8,128)S(1)}, u32[]{:S(2)}, u32[]{:S(2)}) collective-permute-start(f32[40,1152]{1,0:T(8,128)} %get-tuple-element.22.refs_8_), channel_id=1, source_target_pairs={{6,0},{7,1},{4,2},{5,3},{2,4},{3,5},{0,6},{1,7},{14,8},{15,9},{12,... | collective-permute-start | bytes 552968 | tf_op jit(solution)/shard_map/ppermute | solution.py:29
  8.6 16.1 %collective-permute-start.5 = (f32[40,1152]{1,0:T(8,128)}, f32[40,1152]{1,0:T(8,128)S(1)}, u32[]{:S(2)}, u32[]{:S(2)}) collective-permute-start(f32[40,1152]{1,0:T(8,128)} %get-tuple-element.22.refs_8_), channel_id=1, source_target_pairs={{2,0},{3,1},{0,2},{1,3},{6,4},{7,5},{4,6},{5,7},{10,8},{11,9},{8,1... | collective-permute-start | bytes 552968 | tf_op jit(solution)/shard_map/ppermute | solution.py:29
  8.6 16.1 %collective-permute-start.4 = (f32[40,1152]{1,0:T(8,128)}, f32[40,1152]{1,0:T(8,128)S(1)}, u32[]{:S(2)}, u32[]{:S(2)}) collective-permute-start(f32[40,1152]{1,0:T(8,128)} %get-tuple-element.22.refs_8_), channel_id=1, source_target_pairs={{7,0},{2,1},{1,2},{4,3},{3,4},{6,5},{5,6},{0,7},{15,8},{10,9},{9,1... | collective-permute-start | bytes 552968 | tf_op jit(solution)/shard_map/ppermute | solution.py:29
  10.5 14.2 %collective-permute-start.3 = (f32[40,1152]{1,0:T(8,128)}, f32[40,1152]{1,0:T(8,128)S(1)}, u32[]{:S(2)}, u32[]{:S(2)}) collective-permute-start(f32[40,1152]{1,0:T(8,128)} %get-tuple-element.22.refs_8_), channel_id=1, source_target_pairs={{1,0},{0,1},{3,2},{2,3},{5,4},{4,5},{7,6},{6,7},{9,8},{8,9},{11,10... | collective-permute-start | bytes 552968 | tf_op jit(solution)/shard_map/ppermute | solution.py:29
  12.1 4.0 %collective-permute-start.2 = (f32[40,128]{1,0:T(8,128)}, f32[40,128]{1,0:T(8,128)S(1)}, u32[]{:S(2)}, u32[]{:S(2)}) collective-permute-start(f32[40,128]{1,0:T(8,128)} %get-tuple-element.21.refs_4_), channel_id=1, source_target_pairs={{16,0},{24,8},{0,16},{8,24},{17,1},{25,9},{1,17},{9,25},{18,2},{26... | collective-permute-start | bytes 61448 | tf_op jit(solution)/shard_map/ppermute | solution.py:29
  16.1 3.6 %collective-permute-start.1 = (f32[40,128]{1,0:T(8,128)}, f32[40,128]{1,0:T(8,128)S(1)}, u32[]{:S(2)}, u32[]{:S(2)}) collective-permute-start(f32[40,128]{1,0:T(8,128)} %get-tuple-element.21.refs_4_), channel_id=1, source_target_pairs={{24,0},{16,8},{8,16},{0,24},{25,1},{17,9},{9,17},{1,25},{26,2},{18... | collective-permute-start | bytes 61448 | tf_op jit(solution)/shard_map/ppermute | solution.py:29
  19.7 5.0 %collective-permute-start = (f32[40,128]{1,0:T(8,128)}, f32[40,128]{1,0:T(8,128)S(1)}, u32[]{:S(2)}, u32[]{:S(2)}) collective-permute-start(f32[40,128]{1,0:T(8,128)} %get-tuple-element.21.refs_4_), channel_id=1, source_target_pairs={{8,0},{0,8},{24,16},{16,24},{9,1},{1,9},{25,17},{17,25},{10,2},{2,... | collective-permute-start | bytes 61448 | tf_op jit(solution)/shard_map/ppermute | solution.py:29
  22.9 1.8 %copy-start.5 = (f32[40,128]{1,0:T(8,128)S(1)}, f32[40,128]{1,0:T(8,128)}, u32[]{:S(2)}) copy-start(f32[40,128]{1,0:T(8,128)} %get-tuple-element.21.refs_4_) | copy-start | bytes 61444
  24.7 0.9 %copy-start.1 = (bf16[384,96]{1,0:T(8,128)(2,1)S(1)}, bf16[384,96]{1,0:T(8,128)(2,1)}, u32[]{:S(2)}) copy-start(bf16[384,96]{1,0:T(8,128)(2,1)} %get-tuple-element.18.refs_1_) | copy-start | bytes 221188
  25.6 0.9 %copy-start.2 = (bf16[32,1152]{1,0:T(8,128)(2,1)S(1)}, bf16[32,1152]{1,0:T(8,128)(2,1)}, u32[]{:S(2)}) copy-start(bf16[32,1152]{1,0:T(8,128)(2,1)} %get-tuple-element.19.refs_2_) | copy-start | bytes 221188
  26.5 0.8 %copy-start.3 = (s32[5,8,160]{2,1,0:T(8,128)S(1)}, s32[5,8,160]{2,1,0:T(8,128)}, u32[]{:S(2)}) copy-start(s32[5,8,160]{2,1,0:T(8,128)} %get-tuple-element.17.refs_0_) | copy-start | bytes 76804
  27.3 0.7 %copy-start.6 = (f32[24,32]{1,0:T(8,128)S(1)}, f32[24,32]{1,0:T(8,128)}, u32[]{:S(2)}) copy-start(f32[24,32]{1,0:T(8,128)} %get-tuple-element.20.refs_3_) | copy-start | bytes 9220
  34.1 0.6 %copy-start.4 = (f32[40,128]{1,0:T(8,128)}, f32[40,128]{1,0:T(8,128)S(1)}, u32[]{:S(2)}) copy-start(f32[40,128]{1,0:T(8,128)S(1)} %get-tuple-element.23.refs_0_) | copy-start | bytes 61444
  34.7 2.6 %copy-start.7 = (f32[8,128]{1,0:T(8,128)}, f32[8,128]{1,0:T(8,128)S(1)}, u32[]{:S(2)}) copy-start(f32[8,128]{1,0:T(8,128)S(1)} %get-tuple-element.27.refs_4_) | copy-start | bytes 12292
  34.7 14.3 %collective-permute-start.7 = (f32[40,128]{1,0:T(8,128)S(1)}, f32[40,128]{1,0:T(8,128)S(1)}, u32[]{:S(2)}, u32[]{:S(2)}) collective-permute-start(f32[40,128]{1,0:T(8,128)S(1)} %get-tuple-element.24), channel_id=1, source_target_pairs={{0,8},{8,0},{16,24},{24,16},{1,9},{9,1},{17,25},{25,17},{2,10},{10... | collective-permute-start | bytes 61448 | tf_op jit(solution)/shard_map/ppermute | solution.py:33
  35.0 13.9 %collective-permute-start.8 = (f32[40,128]{1,0:T(8,128)S(1)}, f32[40,128]{1,0:T(8,128)S(1)}, u32[]{:S(2)}, u32[]{:S(2)}) collective-permute-start(f32[40,128]{1,0:T(8,128)S(1)} %get-tuple-element.25), channel_id=1, source_target_pairs={{0,24},{8,16},{16,8},{24,0},{1,25},{9,17},{17,9},{25,1},{2,26},{10... | collective-permute-start | bytes 61448 | tf_op jit(solution)/shard_map/ppermute | solution.py:33
  36.0 13.0 %collective-permute-start.9 = (f32[40,128]{1,0:T(8,128)S(1)}, f32[40,128]{1,0:T(8,128)S(1)}, u32[]{:S(2)}, u32[]{:S(2)}) collective-permute-start(f32[40,128]{1,0:T(8,128)S(1)} %get-tuple-element.26), channel_id=1, source_target_pairs={{0,16},{8,24},{16,0},{24,8},{1,17},{9,25},{17,1},{25,9},{2,18},{10... | collective-permute-start | bytes 61448 | tf_op jit(solution)/shard_map/ppermute | solution.py:33
  36.8 3.6 %collective-permute-start.10 = (f32[8,128]{1,0:T(8,128)S(1)}, f32[8,128]{1,0:T(8,128)S(1)}, u32[]{:S(2)}, u32[]{:S(2)}) collective-permute-start(f32[8,128]{1,0:T(8,128)S(1)} %get-tuple-element.28), channel_id=1, source_target_pairs={{0,1},{1,0},{2,3},{3,2},{4,5},{5,4},{6,7},{7,6},{8,9},{9,8},{10,11... | collective-permute-start | bytes 12296 | tf_op jit(solution)/shard_map/ppermute | solution.py:33
  37.2 6.3 %collective-permute-start.11 = (f32[8,128]{1,0:T(8,128)S(1)}, f32[8,128]{1,0:T(8,128)S(1)}, u32[]{:S(2)}, u32[]{:S(2)}) collective-permute-start(f32[8,128]{1,0:T(8,128)S(1)} %get-tuple-element.29), channel_id=1, source_target_pairs={{0,7},{1,2},{2,1},{3,4},{4,3},{5,6},{6,5},{7,0},{8,15},{9,10},{10,... | collective-permute-start | bytes 12296 | tf_op jit(solution)/shard_map/ppermute | solution.py:33
  40.4 8.6 %copy-start.15 = (f32[8,128]{1,0:T(8,128)}, f32[8,128]{1,0:T(8,128)S(1)}, u32[]{:S(2)}) copy-start(f32[8,128]{1,0:T(8,128)S(1)} %collective-permute-done.10.refs_5_) | copy-start | bytes 12292
  40.4 3.6 %collective-permute-start.12 = (f32[8,128]{1,0:T(8,128)S(1)}, f32[8,128]{1,0:T(8,128)S(1)}, u32[]{:S(2)}, u32[]{:S(2)}) collective-permute-start(f32[8,128]{1,0:T(8,128)S(1)} %get-tuple-element.30), channel_id=1, source_target_pairs={{0,2},{1,3},{2,0},{3,1},{4,6},{5,7},{6,4},{7,5},{8,10},{9,11},{10,... | collective-permute-start | bytes 12296 | tf_op jit(solution)/shard_map/ppermute | solution.py:33
  43.5 5.5 %copy-start.16 = (f32[8,128]{1,0:T(8,128)}, f32[8,128]{1,0:T(8,128)S(1)}, u32[]{:S(2)}) copy-start(f32[8,128]{1,0:T(8,128)S(1)} %collective-permute-done.11.refs_6_) | copy-start | bytes 12292
  43.5 5.4 %collective-permute-start.13 = (f32[8,128]{1,0:T(8,128)S(1)}, f32[8,128]{1,0:T(8,128)S(1)}, u32[]{:S(2)}, u32[]{:S(2)}) collective-permute-start(f32[8,128]{1,0:T(8,128)S(1)} %get-tuple-element.31), channel_id=1, source_target_pairs={{0,6},{1,7},{2,4},{3,5},{4,2},{5,3},{6,0},{7,1},{8,14},{9,15},{10,... | collective-permute-start | bytes 12296 | tf_op jit(solution)/shard_map/ppermute | solution.py:33
  44.0 5.0 %copy-start.17 = (f32[8,128]{1,0:T(8,128)}, f32[8,128]{1,0:T(8,128)S(1)}, u32[]{:S(2)}) copy-start(f32[8,128]{1,0:T(8,128)S(1)} %collective-permute-done.12.refs_7_) | copy-start | bytes 12292
  49.0 0.6 %copy-start.8 = (f32[40,128]{1,0:T(8,128)}, f32[40,128]{1,0:T(8,128)S(1)}, u32[]{:S(2)}) copy-start(f32[40,128]{1,0:T(8,128)S(1)} %collective-permute-done.7.refs_1_) | copy-start | bytes 61444
  49.0 0.6 %copy-start.9 = (f32[40,128]{1,0:T(8,128)}, f32[40,128]{1,0:T(8,128)S(1)}, u32[]{:S(2)}) copy-start(f32[40,128]{1,0:T(8,128)S(1)} %collective-permute-done.8.refs_2_) | copy-start | bytes 61444
  49.0 0.6 %copy-start.10 = (f32[40,128]{1,0:T(8,128)}, f32[40,128]{1,0:T(8,128)S(1)}, u32[]{:S(2)}) copy-start(f32[40,128]{1,0:T(8,128)S(1)} %collective-permute-done.9.refs_3_) | copy-start | bytes 61444
  (1 other events, 0.6 us)

commit v2 on v1

v2 whole, which is shorter than its diff:
```python
import functools
import math

import jax
import jax.numpy as jnp
from jax import lax
from jax.experimental import pallas as pl
from jax.experimental.pallas import tpu as pltpu
from jax.sharding import PartitionSpec as P

domain_side = 5.0
cutoff = 12.0
soften = 0.25
reach = 2
sublanes = 8
degree = (0, 1, 1, 1, 2, 2, 2, 2, 2)
megabyte = 1024 * 1024
f32 = jnp.float32
bf16 = jnp.bfloat16


class Link:
    def __init__(self, step, bit, peers):
        self.step, self.bit, self.peers = step, bit, peers

    def delta(self, i):
        return self.step * (1 - 2 * ((i >> self.bit) & 1))

    def swap(self, value, axis):
        n = self.peers
        return lax.ppermute(value, axis, [(i, (i + self.delta(i)) % n) for i in range(n)])


def links_of(peers):
    assert peers % 4 == 0, peers
    steps = [(1, 0), (-1, 0), (2, 1)] + ([(-2, 1)] if peers > 4 else [])
    return [Link(step, bit, peers) for step, bit in steps]


def spots_of(links):
    spots = [(0, None, 0)]
    for table, link in enumerate(links):
        spots.append((table + 1, link, 1))
        if link.peers == 4 and abs(link.step) == 2:
            spots.append((table + 1, link, -1))
    return spots


def pieces(x, count):
    out = []
    for _ in range(count):
        out.append(x.astype(bf16).astype(f32))
        x = x - out[-1]
    return out


def dot(a, b):
    return jnp.dot(a, b, preferred_element_type=f32)


def dot_rows(a, b):
    return lax.dot_general(a, b, (((1,), (1,)), ((), ())), preferred_element_type=f32)


def dot_cols(a, b):
    return lax.dot_general(a, b, (((0,), (0,)), ((), ())), preferred_element_type=f32)


def pack_targets_kernel(pos_ref, cot_ref, out_ref):
    atoms = cot_ref.shape[2]
    parts = len(degree)
    channels = out_ref.shape[1]
    for m in range(parts):
        out_ref[m * atoms : (m + 1) * atoms] = cot_ref[0, 0, :, m * channels : (m + 1) * channels]
    out_ref[parts * atoms :] = jnp.zeros((sublanes, channels), f32)
    for axis in range(3):
        out_ref[parts * atoms + axis : parts * atoms + axis + 1, 0:atoms] = pos_ref[0, axis]


def pack_sources_kernel(pos_ref, feat_ref, out_ref):
    atoms, channels = feat_ref.shape[2:]
    out_ref[0:atoms] = feat_ref[0, 0]
    out_ref[atoms:] = jnp.zeros((sublanes, channels), f32)
    for axis in range(3):
        out_ref[atoms + axis : atoms + axis + 1, 0:atoms] = pos_ref[0, axis]


def stack_kernel(upper_ref, lower_ref, out_ref):
    rows = upper_ref.shape[0]
    out_ref[0:rows] = upper_ref[...]
    out_ref[rows:] = lower_ref[...]


def prep_kernel(
    gx_spots, gy_spots, groups, src_ref, tgt_ref, mask_ref, spec_ref, in_ref, emb_ref, out_ref,
    *outs,
):
    atoms = pairs = src_ref.shape[4]
    at_x, at_y = lax.axis_index("gx"), lax.axis_index("gy")
    wide_ref, back_ref, first_ref, last_ref = outs[len(groups) :]
    for group, rows_ref in zip(groups, outs):
        slot = 0
        for place, spot in enumerate(group):
            _, link, sign = gy_spots[spot]
            step_y = 0 if link is None else sign * link.delta(at_y)
            for table, link, sign in gx_spots:
                step_x = 0 if link is None else sign * link.delta(at_x)
                lanes = slice(slot * pairs, (slot + 1) * pairs)
                row, col = reach + step_x, reach + step_y
                rows_ref[0:1, lanes] = src_ref[0, row, col] + table * atoms
                rows_ref[1:2, lanes] = tgt_ref[0, row, col] + place * atoms
                rows_ref[2:3, lanes] = mask_ref[0, row, col]
                rows_ref[3:4, lanes] = spec_ref[0, row, col]
                rows_ref[4:5, lanes] = jnp.full((1, pairs), step_x, jnp.int32)
                rows_ref[5:6, lanes] = jnp.full((1, pairs), -step_y, jnp.int32)
                slot += 1
        rows_ref[6:8] = jnp.zeros((2, rows_ref.shape[1]), jnp.int32)
    high, low = pieces(out_ref[...], 2)
    wide_ref[...] = jnp.concatenate([high, high, low], axis=0).T.astype(bf16)
    upper = jnp.concatenate([high, high], axis=1)
    lower = jnp.concatenate([low, jnp.zeros_like(low)], axis=1)
    back_ref[...] = jnp.concatenate([upper, lower], axis=0).astype(bf16)
    orders, hidden = in_ref.shape
    spare = jnp.zeros((sublanes * 2 - emb_ref.shape[0], hidden), f32)
    high, low = pieces(jnp.concatenate([in_ref[...], emb_ref[...], spare], axis=0), 2)
    first_ref[...] = jnp.concatenate([high, high, low], axis=0).T.astype(bf16)
    last_ref[...] = jnp.concatenate([high[0:orders], high[0:orders], low[0:orders]], axis=1).astype(bf16)


def radial_waves(dist, orders):
    order = (lax.broadcasted_iota(jnp.int32, (orders, 1), 0) + 1).astype(f32)
    turn = order * (dist * (1.0 / cutoff))
    whole = jnp.floor(turn + 0.5)
    part = turn - whole
    sign = 1.0 - 2.0 * (whole - 2.0 * jnp.floor(0.5 * whole))
    square = part * part
    sine = jnp.zeros_like(square)
    for k in (11, 9, 7, 5, 3, 1):
        sine = sine * square + (-1.0) ** (k // 2) * math.pi**k / math.factorial(k)
    cosine = jnp.zeros_like(square)
    for k in (12, 10, 8, 6, 4, 2, 0):
        cosine = cosine * square + (-1.0) ** (k // 2) * math.pi**k / math.factorial(k)
    return order, sign * part * sine, sign * cosine


def thrice(x):
    high, low = pieces(x, 2)
    return jnp.concatenate([high, low, high], axis=0).astype(bf16)


def onehot(ids, count):
    return jnp.where(lax.broadcasted_iota(jnp.int32, (count, ids.shape[1]), 0) == ids, 1.0, 0.0)


def slot_grads(rows, cot_refs, src_pos, feats, weights, orders):
    wide, back, first, last = weights
    slots = rows.shape[1]
    sources = src_pos.shape[1]
    channels = feats.shape[0]
    hidden = last.shape[1] // 3
    parts = len(degree)
    atoms = (cot_refs[0].shape[0] - sublanes) // parts
    targets = atoms * len(cot_refs)

    src_hot = onehot(rows[0:1], sources).astype(bf16)
    tgt_hot = onehot(rows[1:2], targets).astype(bf16)
    mask = rows[2:3].astype(f32)
    offset = rows[4:6].astype(f32) * domain_side

    tgt_pos = [jnp.concatenate(pieces(ref[parts * atoms :, 0:atoms], 3), axis=0) for ref in cot_refs]
    from_src = dot(src_pos, src_hot)
    from_tgt = dot(jnp.concatenate(tgt_pos, axis=1).astype(bf16), tgt_hot)
    from_src = from_src[0:8] + from_src[8:16] + from_src[16:24]
    from_tgt = from_tgt[0:8] + from_tgt[8:16] + from_tgt[16:24]
    rel = [
        from_src[0:1] + offset[0:1] - from_tgt[0:1],
        from_src[1:2] + offset[1:2] - from_tgt[1:2],
        from_src[2:3] - from_tgt[2:3],
    ]
    dist = jnp.sqrt(rel[0] * rel[0] + rel[1] * rel[1] + rel[2] * rel[2] + soften)
    near = 1.0 / dist
    x, y, z = (r * near for r in rel)
    scaled = dist * (1.0 / cutoff)
    room = jnp.where(scaled < 1.0, 1.0 - scaled * scaled, 0.0)
    env = room * room * mask
    d_env = (-4.0 / cutoff) * scaled * room * mask

    order, sine, cosine = radial_waves(dist, orders)
    norm = math.sqrt(2.0 / cutoff)
    basis = norm * near * sine
    d_basis = norm * near * ((math.pi / cutoff) * order * cosine - sine * near)
    species = onehot(rows[3:4], 2 * sublanes)
    before = dot(first, thrice(jnp.concatenate([basis, species], axis=0)))
    gate = 1.0 / (1.0 + jnp.exp(-before))
    act = before * gate
    d_act = gate * (1.0 + before * (1.0 - gate))
    radial = dot(wide, thrice(act))
    gathered = dot(feats, jnp.concatenate([src_hot, src_hot], axis=0))

    root3, root5, root15 = math.sqrt(3.0), math.sqrt(5.0), math.sqrt(15.0)
    shapes = [
        None, root3 * x, root3 * y, root3 * z, root15 * x * y, root15 * y * z,
        0.5 * root5 * (2.0 * z * z - x * x - y * y), root15 * x * z, 0.5 * root15 * (x * x - y * y),
    ]
    twice = lax.broadcasted_iota(jnp.int32, (2 * targets, slots), 0)
    twice = (twice // (2 * atoms)) * atoms + lax.rem(twice, atoms)
    twice = jnp.where(twice == rows[1:2], 1.0, 0.0).astype(bf16)
    d_shapes = [None] * parts
    d_radial = []
    through = None
    for low, high in ((0, 1), (1, 4), (4, 9)):
        l = len(d_radial)
        own = radial[l * channels : (l + 1) * channels]
        with_feats = own * gathered
        total = None
        for m in range(low, high):
            blocks = []
            for ref in cot_refs:
                blocks += pieces(ref[m * atoms : (m + 1) * atoms], 2)
            cot = dot_cols(jnp.concatenate(blocks, axis=0).astype(bf16), twice)
            if m:
                d_shapes[m] = jnp.sum(with_feats * cot, axis=0, keepdims=True) * env
                cot = cot * shapes[m]
            total = cot if total is None else total + cot
        d_radial.append(total * gathered)
        own = own * total
        through = own if through is None else through + own
    to_env = jnp.sum(through * gathered, axis=0, keepdims=True)
    through = through * env
    d_hidden = dot(back, jnp.concatenate(
        [p.astype(bf16) for p in pieces(jnp.concatenate(d_radial, axis=0), 2)], axis=0
    ))
    d_before = (d_hidden[0:hidden] + d_hidden[hidden:]) * (d_act * env)
    to_basis = dot(last, thrice(d_before))
    d_dist = jnp.sum(to_basis * d_basis, axis=0, keepdims=True) + to_env * d_env

    s = d_shapes
    d_x = root3 * s[1] + root15 * (y * s[4] + z * s[7] + x * s[8]) - root5 * x * s[6]
    d_y = root3 * s[2] + root15 * (x * s[4] + z * s[5] - y * s[8]) - root5 * y * s[6]
    d_z = root3 * s[3] + root15 * (y * s[5] + x * s[7]) + 2.0 * root5 * z * s[6]
    d_dist = d_dist - near * (x * d_x + y * d_y + z * d_z)
    grad = jnp.concatenate(
        [near * d_x + x * d_dist, near * d_y + y * d_dist, near * d_z + z * d_dist,
         jnp.zeros((sublanes - 3, slots), f32)], axis=0,
    )
    grad = jnp.concatenate(pieces(grad, 2), axis=0).astype(bf16)
    pos_src = dot_rows(grad, src_hot)
    pos_tgt = dot_rows(grad, tgt_hot)
    feat_src = sum(dot_rows(src_hot, p.astype(bf16)) for p in pieces(through, 2))
    return pos_src[0:8] + pos_src[8:16], -(pos_tgt[0:8] + pos_tgt[8:16]), feat_src


def blocks_of(refs, rows):
    return [
        ref.at[start : start + rows] for ref in refs for start in range(0, ref.shape[0], rows)
    ]


def first_kernel(orders, group, gx_count, rows_ref, *refs):
    refs = list(refs)
    weights = [refs.pop(0)[...] for _ in range(4)]
    gx_refs = [refs.pop(0) for _ in range(gx_count)]
    gy_refs = [refs.pop(0) for _ in group]
    atoms = (gy_refs[0].shape[0] - sublanes) // len(degree)
    gx_refs = blocks_of(gx_refs, atoms + sublanes)
    src_pos_ref, feats_ref, feat_ref, pos_ref, tgt_ref, place = refs
    for table, ref in enumerate(gx_refs):
        place[:, table * atoms : (table + 1) * atoms] = ref[atoms:, 0:atoms]
    src_pos = jnp.concatenate(pieces(place[...], 3), axis=0).astype(bf16)
    feats = pieces(jnp.concatenate([ref[0:atoms] for ref in gx_refs], axis=0), 2)
    feats = jnp.concatenate(feats, axis=0).T.astype(bf16)
    src_pos_ref[...] = src_pos
    feats_ref[...] = feats
    pos_src, pos_tgt, feat_src = slot_grads(
        rows_ref[...], gy_refs, src_pos, feats, weights, orders
    )
    feat_ref[...] = feat_src
    pos_ref[...] = pos_src
    pos_ref[:, 0:atoms] = pos_src[:, 0:atoms] + pos_tgt[:, 0:atoms]
    tgt_ref[...] = jnp.zeros(tgt_ref.shape, f32)
    for place_in, table in enumerate(group):
        if table:
            tgt_ref[:, (table - 1) * atoms : table * atoms] = pos_tgt[
                :, place_in * atoms : (place_in + 1) * atoms
            ]


def last_kernel(orders, group, gx_count, rows_ref, *refs):
    refs = list(refs)
    weights = [refs.pop(0)[...] for _ in range(4)]
    src_pos, feats = (refs.pop(0)[...] for _ in range(2))
    held_feat, held_pos = (refs.pop(0) for _ in range(2))
    gy_refs = [refs.pop(0) for _ in group]
    gx_outs, (near_ref, far_ref) = refs[:gx_count], refs[gx_count:]
    pos_src, pos_tgt, feat_src = slot_grads(
        rows_ref[...], gy_refs, src_pos, feats, weights, orders
    )
    atoms = pos_tgt.shape[1] // len(group)
    feat = held_feat[...] + feat_src
    pos = held_pos[...] + pos_src
    tables = (0, 2, 1, 3) if len(gx_outs) == 3 else range(len(gx_outs))
    for table, ref in zip(tables, blocks_of(gx_outs, atoms + sublanes)):
        part = slice(table * atoms, (table + 1) * atoms)
        ref[0:atoms] = feat[part]
        ref[atoms:] = jnp.zeros((sublanes, ref.shape[1]), f32)
        ref[atoms:, 0:atoms] = pos[:, part]
    near_ref[...] = jnp.zeros(near_ref.shape, f32)
    far_ref[...] = jnp.zeros(far_ref.shape, f32)
    near_ref[:, 0:atoms] = pos_tgt[:, group.index(3) * atoms :][:, 0:atoms]
    far_ref[:, 0:atoms] = pos_tgt[:, group.index(4) * atoms :][:, 0:atoms]


def join_kernel(atoms, relay_ref, near_ref, far_ref, near_out, far_out):
    at_y = lax.axis_index("gy")
    to_far = ((at_y + (at_y >> 1)) & 1).astype(f32)
    relay = relay_ref[:, atoms : 2 * atoms]
    near_out[...] = near_ref[...]
    far_out[...] = far_ref[...]
    near_out[:, 0:atoms] = near_ref[:, 0:atoms] + relay * (1.0 - to_far)
    far_out[:, 0:atoms] = far_ref[:, 0:atoms] + relay * to_far


def sum_kernel(gx_count, *refs):
    gx_refs, gy_refs = refs[:gx_count], refs[gx_count:-2]
    pos_ref, feat_ref = refs[-2:]
    atoms = pos_ref.shape[3]
    feat = gx_refs[0][...]
    for ref in gx_refs[1:]:
        feat = feat + ref[ref.shape[0] - atoms - sublanes :]
    pos = feat[atoms : atoms + 3, 0:atoms]
    for ref in gy_refs:
        pos = pos + ref[0:3, 0:atoms]
    for axis in range(3):
        pos_ref[0, axis] = pos[axis : axis + 1]
    feat_ref[0, 0] = feat[0:atoms]


vmem = pl.BlockSpec(memory_space=pltpu.VMEM)
hbm = pl.BlockSpec(memory_space=pltpu.HBM)


def call(kernel, name, out_shape, operands, scratch=(), room=4, space=vmem):
    return pl.pallas_call(
        kernel,
        out_shape=out_shape,
        in_specs=[space] * len(operands),
        out_specs=(vmem,) * len(out_shape),
        scratch_shapes=list(scratch),
        compiler_params=pltpu.CompilerParams(vmem_limit_bytes=room and room * megabyte),
        name=name,
    )(*operands)


def gather(links, own):
    if links[0].peers > 4:
        return [own] + [link.swap(own, "gx") for link in links]
    one = links[0].swap(own, "gx")
    rows, columns = own.shape
    (both,) = call(
        stack_kernel, "stack", (jax.ShapeDtypeStruct((2 * rows, columns), own.dtype),), (one, own)
    )
    return [own, one, links[2].swap(both, "gx")]


def gx_shapes(links, block):
    if links[0].peers > 4:
        return (block,) * (len(links) + 1)
    rows, columns = block.shape
    return (block, jax.ShapeDtypeStruct((2 * rows, columns), block.dtype), block)


def scatter(links, outs):
    if links[0].peers > 4:
        return outs[:1] + [link.swap(out, "gx") for link, out in zip(links, outs[1:])]
    own, pair, far = outs
    rows = own.shape[0]
    pair = links[0].swap(pair, "gx")
    far = links[2].swap(far + pair[0:rows], "gx")
    return [own, pair, far]


def local(
    gx_size, gy_size, positions, features, cotangent, nbr_src, nbr_tgt, pair_mask, pair_species,
    w_in, species_emb, w_out,
):
    atoms, channels = features.shape[2:]
    steps, _, pairs = nbr_src.shape[2:]
    orders, hidden = w_in.shape
    slots = steps * pairs
    gx_links, gy_links = links_of(gx_size), links_of(gy_size)
    gx_spots, gy_spots = spots_of(gx_links), spots_of(gy_links)
    gx_count = len(gx_links) + 1
    sources = gx_count * atoms
    sds = jax.ShapeDtypeStruct
    groups = ((0, 2, 1), (4, 3))

    by_axis = jnp.transpose(positions, (0, 2, 1, 3))
    lists = [jnp.transpose(x, (0, 2, 3, 1, 4)) for x in (nbr_src, nbr_tgt, pair_mask, pair_species)]
    gx_pack = sds((atoms + sublanes, channels), f32)
    gy_pack = sds((len(degree) * atoms + sublanes, channels), f32)
    (gy_own,) = call(
        pack_targets_kernel, "pack_targets", (gy_pack,), (by_axis, cotangent), room=None
    )
    (gx_own,) = call(pack_sources_kernel, "pack_sources", (gx_pack,), (by_axis, features))
    gy_packs = [gy_own] + [link.swap(gy_own, "gy") for link in gy_links]
    gx_packs = gather(gx_links, gx_own)

    *rows, wide, back, first, last = call(
        functools.partial(prep_kernel, gx_spots, gy_spots, groups),
        "prepare",
        (
            *(sds((sublanes, len(group) * slots), jnp.int32) for group in groups),
            sds((w_out.shape[1], 3 * hidden), bf16),
            sds((2 * hidden, 2 * w_out.shape[1]), bf16),
            sds((hidden, 3 * (orders + 2 * sublanes)), bf16),
            sds((orders, 3 * hidden), bf16),
        ),
        (*lists, w_in, species_emb, w_out),
    )
    weights = (wide, back, first, last)
    packs = [[gy_packs[table] for table in group] for group in groups]
    tgt_pack = sds((sublanes, channels), f32)
    src_pos, feats, feat, pos, tgt = call(
        functools.partial(first_kernel, orders, groups[0], len(gx_packs)), "tiles",
        (
            sds((3 * sublanes, sources), bf16), sds((channels, 2 * sources), bf16),
            sds((sources, channels), f32), sds((sublanes, sources), f32), tgt_pack,
        ),
        (rows[0], *weights, *gx_packs, *packs[0]),
        [pltpu.VMEM((sublanes, sources), f32)], 16,
    )
    relay = gy_links[0].swap(tgt, "gy")
    *gx_outs, near, far = call(
        functools.partial(last_kernel, orders, groups[1], len(gx_packs)), "tiles",
        gx_shapes(gx_links, gx_pack) + (tgt_pack,) * 2,
        (rows[1], *weights, src_pos, feats, feat, pos, *packs[1]), room=16,
    )
    near, far = call(functools.partial(join_kernel, atoms), "join", (tgt_pack,) * 2, (relay, near, far))
    *gx_outs, near, far = lax.optimization_barrier((*gx_outs, near, far))
    back_gy = [gy_links[3].swap(far, "gy"), gy_links[2].swap(near, "gy"), relay]
    back_gx = scatter(gx_links, gx_outs)
    pos, feat = call(
        functools.partial(sum_kernel, len(back_gx)), "sums",
        (sds(by_axis.shape, f32), sds(features.shape, f32)),
        (*back_gx, *back_gy),
    )
    return jnp.transpose(pos, (0, 2, 1, 3)), feat


def solution(mesh):
    split = [P("gx", "gy")] * 7 + [P()] * 3
    return jax.shard_map(
        functools.partial(local, mesh.shape["gx"], mesh.shape["gy"]),
        mesh=mesh,
        in_specs=tuple(split),
        out_specs=(P("gx", "gy"), P("gx", "gy")),
        check_vma=False,
    )
```

time: 52.7 us -> 31.5 us (0.60)
  local copies, waits for them, and re-layouts: 9.37 us -> 0.04 us
  Pallas kernels: 10.9 us -> 6.11 us
  waiting for transfers between devices: 14.9 us -> 10.6 us
  starting transfers between devices: 15.7 us -> 13.8 us
  other arithmetic: 0.6 us -> 0.01 us
    unnamed x43 -> x20, local copies, waits for them, and re-layouts: 8.15 us -> 0.04 us
    pallas_call x4 -> x8, Pallas kernels: 10.9 us -> 6.11 us  [call(): pl.pallas_call(kernel, out_shape=out_shape, in_specs=[space] * len(operan...]
    ppermute x14 -> x11, waiting for transfers between devices: 14.9 us -> 10.6 us  [swap(): lax.ppermute(value, axis, [(i, (i + self.delta(i)) % n) for i in range(n)])]
    ppermute x14 -> x11, starting transfers between devices: 15.7 us -> 13.8 us  [swap(): lax.ppermute(value, axis, [(i, (i + self.delta(i)) % n) for i in range(n)])]
    pallas_call x1 -> x0, local copies, waits for them, and re-layouts: 1.22 us -> none  [local(): pl.pallas_call(functools.partial(sum_kernel, gx_count), out_shape=(sds(po...]
    another operation x1 -> x0, other arithmetic: 0.6 us -> none  [local(): jnp.stack([lax.axis_index('gx'), lax.axis_index('gy')]).astype(jnp.int32)]
  transfers between devices with their start and end apart: 14 -> 11, of which waited for: 6 -> 8; matrix products, arithmetic and copies ran while one was open for 6% -> 0% of each run, Pallas kernels for 3% -> 12%
where the time goes in v2:
time: 31.5 us; the launch traced here: 31.4 us
  starting transfers between devices  13.8 us (44%)
  waiting for transfers between devices  10.6 us (34%)
  Pallas kernels  6.11 us (19%)
  between operations  0.79 us (3%)
    ppermute x11, starting transfers between devices, swap(): lax.ppermute(value, axis, [(i, (i + self.delta(i)) % n) for i in range(n)])  13.8 us
    ppermute x11, waiting for transfers between devices, swap(): lax.ppermute(value, axis, [(i, (i + self.delta(i)) % n) for i in range(n)])  10.6 us
    pallas_call x8, Pallas kernels, call(): pl.pallas_call(kernel, out_shape=out_shape, in_specs=[space] * len(operan...  6.11 us
  transfers between devices with their start and end apart: 11, of which 8 were waited for; matrix products, arithmetic and copies ran while one was open for 0% of the time, Pallas kernels for 12%

profile of v2, /device:TPU:0, one launch (start us, length us, event | category | flops | bytes accessed | tf_op | source)
XLA Modules:
  0.0 31.4 jit_solution(18090150042578362390)
XLA Ops:
  0.6 0.0 copy-start.2
  0.6 0.0 copy-start.8
  0.7 1.7 %pack_targets.1.refs_7_ = f32[296,128]{1,0:T(8,128)} custom-call(f32[1,3,1,32]{3,2,1,0:T(1,128)} %bitcast.10, f32[1,1,32,1152]{3,2,1,0:T(8,128)} %cot_ref.1), custom_call_target="tpu_custom_call" | custom-call | tf_op jit(solution)/shard_map/pack_targets/pallas_call | solution.py:343
  2.4 6.0 %collective-permute-start.2 = (f32[296,128]{1,0:T(8,128)}, f32[296,128]{1,0:T(8,128)S(1)}, u32[]{:S(2)}, u32[]{:S(2)}) collective-permute-start(f32[296,128]{1,0:T(8,128)} %pack_targets.1.refs_7_), channel_id=1, source_target_pairs={{0,7},{1,2},{2,1},{3,4},{4,3},{5,6},{6,5},{7,0},{8,15},{9,10},{10,... | collective-permute-start | bytes 454664 | tf_op jit(solution)/shard_map/ppermute | solution.py:31
  8.4 0.0 collective-permute-start.3
  8.4 0.6 %collective-permute-start.4 = (f32[296,128]{1,0:T(8,128)}, f32[296,128]{1,0:T(8,128)S(1)}, u32[]{:S(2)}, u32[]{:S(2)}) collective-permute-start(f32[296,128]{1,0:T(8,128)} %pack_targets.1.refs_7_), channel_id=1, source_target_pairs={{0,6},{1,7},{2,4},{3,5},{4,2},{5,3},{6,0},{7,1},{8,14},{9,15},{10,... | collective-permute-start | bytes 454664 | tf_op jit(solution)/shard_map/ppermute | solution.py:31
  9.0 1.1 %collective-permute-start.5 = (f32[296,128]{1,0:T(8,128)}, f32[296,128]{1,0:T(8,128)S(1)}, u32[]{:S(2)}, u32[]{:S(2)}) collective-permute-start(f32[296,128]{1,0:T(8,128)} %pack_targets.1.refs_7_), channel_id=1, source_target_pairs={{0,2},{1,3},{2,0},{3,1},{4,6},{5,7},{6,4},{7,5},{8,10},{9,11},{10,... | collective-permute-start | bytes 454664 | tf_op jit(solution)/shard_map/ppermute | solution.py:31
  10.0 0.1 collective-permute-start
  10.1 1.2 %collective-permute-done.upper_ref.refs_5_ = f32[40,128]{1,0:T(8,128)S(1)} collective-permute-done((f32[40,128]{1,0:T(8,128)S(1)}, f32[40,128]{1,0:T(8,128)S(1)}, u32[]{:S(2)}, u32[]{:S(2)}) %collective-permute-start) | collective-permute-done | bytes 20512 | tf_op jit(solution)/shard_map/ppermute | solution.py:31
  11.3 1.5 %collective-permute-start.1 = (f32[80,128]{1,0:T(8,128)S(1)}, f32[80,128]{1,0:T(8,128)S(1)}, u32[]{:S(2)}, u32[]{:S(2)}) collective-permute-start(f32[80,128]{1,0:T(8,128)S(1)} %stack.1), channel_id=1, source_target_pairs={{0,16},{8,24},{16,0},{24,8},{1,17},{9,25},{17,1},{25,9},{2,18},{10... | collective-permute-start | bytes 122888 | tf_op jit(solution)/shard_map/ppermute | solution.py:31
  12.8 0.0 copy-done.3
  12.8 0.0 copy-done.5
  12.8 0.2 prepare.1
  13.0 2.2 %collective-permute-done.1.refs_6_ = f32[80,128]{1,0:T(8,128)S(1)} collective-permute-done((f32[80,128]{1,0:T(8,128)S(1)}, f32[80,128]{1,0:T(8,128)S(1)}, u32[]{:S(2)}, u32[]{:S(2)}) %collective-permute-start.1) | collective-permute-done | bytes 40992 | tf_op jit(solution)/shard_map/ppermute | solution.py:31
  15.3 0.0 collective-permute-done.2.refs_8_
  15.3 0.6 %collective-permute-done.3.refs_9_ = f32[296,128]{1,0:T(8,128)S(1)} collective-permute-done((f32[296,128]{1,0:T(8,128)}, f32[296,128]{1,0:T(8,128)S(1)}, u32[]{:S(2)}, u32[]{:S(2)}) %collective-permute-start.3) | collective-permute-done | bytes 151584 | tf_op jit(solution)/shard_map/ppermute | solution.py:31
  15.9 1.9 %tiles.2 = (bf16[24,128]{1,0:T(8,128)(2,1)S(1)}, bf16[128,256]{1,0:T(8,128)(2,1)S(1)}, f32[128,128]{1,0:T(8,128)S(1)}, f32[8,128]{1,0:T(8,128)S(1)}, f32[8,128]{1,0:T(8,128)S(1)}) custom-call(s32[8,480]{1,0:T(8,128)S(1)} %get-tuple-element.32.rows_ref, bf16[384,96]{1,0:T(8,128)(2,1)S(1)} %get-tuple-element.28.refs_0_, ...), custom_call_target="tpu_custom_call" | custom-call | tf_op jit(solution)/shard_map/tiles/pallas_call | solution.py:343
  17.9 0.3 collective-permute-start.6
  18.2 0.0 collective-permute-done.4.refs_8_
  18.2 0.3 %collective-permute-done.5.refs_9_ = f32[296,128]{1,0:T(8,128)S(1)} collective-permute-done((f32[296,128]{1,0:T(8,128)}, f32[296,128]{1,0:T(8,128)S(1)}, u32[]{:S(2)}, u32[]{:S(2)}) %collective-permute-start.5) | collective-permute-done | bytes 151584 | tf_op jit(solution)/shard_map/ppermute | solution.py:31
  18.5 1.6 %tiles.3 = (f32[40,128]{1,0:T(8,128)S(1)}, f32[80,128]{1,0:T(8,128)S(1)}, f32[40,128]{1,0:T(8,128)S(1)}, f32[8,128]{1,0:T(8,128)S(1)}, f32[8,128]{1,0:T(8,128)S(1)}) custom-call(s32[8,320]{1,0:T(8,128)S(1)} %get-tuple-element.27.rows_ref, bf16[384,96]{1,0:T(8,128)(2,1)S(1)} %get-tuple-element.28.refs_0_, bf16[64,768]{1,0:T(8,128)(2,1)S(1)} %get-tuple-element.29.refs_1_, ...), custom_call_target="tpu_custom_call" | custom-call | tf_op jit(solution)/shard_map/tiles/pallas_call | solution.py:343
  20.1 1.4 %collective-permute-done.6.relay_ref.refs_5_ = f32[8,128]{1,0:T(8,128)S(1)} collective-permute-done((f32[8,128]{1,0:T(8,128)S(1)}, f32[8,128]{1,0:T(8,128)S(1)}, u32[]{:S(2)}, u32[]{:S(2)}) %collective-permute-start.6) | collective-permute-done | bytes 4128 | tf_op jit(solution)/shard_map/ppermute | solution.py:31
  21.5 0.1 join.1
  21.6 0.0 collective-permute-start.7
  21.6 1.2 %collective-permute-done.7.refs_1_ = f32[80,128]{1,0:T(8,128)S(1)} collective-permute-done((f32[80,128]{1,0:T(8,128)S(1)}, f32[80,128]{1,0:T(8,128)S(1)}, u32[]{:S(2)}, u32[]{:S(2)}) %collective-permute-start.7) | collective-permute-done | bytes 40992 | tf_op jit(solution)/shard_map/ppermute | solution.py:31
  22.8 1.5 %collective-permute-start.8 = (f32[40,128]{1,0:T(8,128)S(1)}, f32[40,128]{1,0:T(8,128)S(1)}, u32[]{:S(2)}, u32[]{:S(2)}) collective-permute-start(f32[40,128]{1,0:T(8,128)S(1)} %slice_add_fusion), channel_id=1, source_target_pairs={{0,16},{8,24},{16,0},{24,8},{1,17},{9,25},{17,1},{25,9},{2,18},{10... | collective-permute-start | bytes 61448 | tf_op jit(solution)/shard_map/ppermute | solution.py:31
  24.3 2.8 %collective-permute-start.9 = (f32[8,128]{1,0:T(8,128)S(1)}, f32[8,128]{1,0:T(8,128)S(1)}, u32[]{:S(2)}, u32[]{:S(2)}) collective-permute-start(f32[8,128]{1,0:T(8,128)S(1)} %get-tuple-element.48), channel_id=1, source_target_pairs={{0,6},{1,7},{2,4},{3,5},{4,2},{5,3},{6,0},{7,1},{8,14},{9,15},{10,... | collective-permute-start | bytes 12296 | tf_op jit(solution)/shard_map/ppermute | solution.py:31
  27.1 0.0 collective-permute-start.10
  27.1 2.6 %collective-permute-done.9.refs_3_ = f32[8,128]{1,0:T(8,128)S(1)} collective-permute-done((f32[8,128]{1,0:T(8,128)S(1)}, f32[8,128]{1,0:T(8,128)S(1)}, u32[]{:S(2)}, u32[]{:S(2)}) %collective-permute-start.9) | collective-permute-done | bytes 4128 | tf_op jit(solution)/shard_map/ppermute | solution.py:31
  29.7 1.0 %collective-permute-done.10.refs_4_ = f32[8,128]{1,0:T(8,128)S(1)} collective-permute-done((f32[8,128]{1,0:T(8,128)S(1)}, f32[8,128]{1,0:T(8,128)S(1)}, u32[]{:S(2)}, u32[]{:S(2)}) %collective-permute-start.10) | collective-permute-done | bytes 4128 | tf_op jit(solution)/shard_map/ppermute | solution.py:31
  30.7 0.0 collective-permute-done.8.refs_2_
  30.7 0.6 %sums.1 = (f32[1,3,1,32]{3,2,1,0:T(1,128)}, f32[1,1,32,128]{3,2,1,0:T(8,128)}) custom-call(f32[40,128]{1,0:T(8,128)S(1)} %get-tuple-element.45.refs_0_, f32[80,128]{1,0:T(8,128)S(1)} %collective-permute-done.7.refs_1_, f32[40,128]{1,0:T(8,128)S(1)} %collective-permute-done.8.refs_2_, f32[8,128]{1,0:T(8,128)S(1)} %collective-permute-done.9.refs_3_, ...), custom_call_target="tpu_custom_call" | custom-call | tf_op jit(solution)/shard_map/sums/pallas_call | solution.py:343
  (19 shorter events, 0.0 us)
Async XLA Ops:
  0.6 9.4 %copy-start.2 = (f32[1,1,32,128]{3,2,1,0:T(8,128)S(1)}, f32[1,1,32,128]{3,2,1,0:T(8,128)}, u32[]{:S(2)}) copy-start(f32[1,1,32,128]{3,2,1,0:T(8,128)} %feat_ref.1) | copy-start | bytes 49156
  0.6 9.4 %copy-start.8 = (f32[1,1,3,32]{3,1,2,0:T(1,128)S(1)}, f32[1,1,3,32]{3,1,2,0:T(1,128)}, u32[]{:S(2)}) copy-start(f32[1,1,3,32]{3,1,2,0:T(1,128)} %param.10) | copy-start | bytes 1156
  0.7 12.1 %copy-start.1 = (f32[32,384]{1,0:T(8,128)S(1)}, f32[32,384]{1,0:T(8,128)}, u32[]{:S(2)}) copy-start(f32[32,384]{1,0:T(8,128)} %out_ref.1) | copy-start | bytes 147460
  0.7 12.1 %copy-start.3 = (s32[1,1,5,5,32]{4,1,3,2,0:T(1,128)S(1)}, s32[1,1,5,5,32]{4,1,3,2,0:T(1,128)}, u32[]{:S(2)}) copy-start(s32[1,1,5,5,32]{4,1,3,2,0:T(1,128)} %param.13) | copy-start | bytes 9604
  0.7 12.1 %copy-start.4 = (s32[1,1,5,5,32]{4,1,3,2,0:T(1,128)S(1)}, s32[1,1,5,5,32]{4,1,3,2,0:T(1,128)}, u32[]{:S(2)}) copy-start(s32[1,1,5,5,32]{4,1,3,2,0:T(1,128)} %param.14) | copy-start | bytes 9604
  0.7 12.1 %copy-start.5 = (s32[1,1,5,5,32]{4,1,3,2,0:T(1,128)S(1)}, s32[1,1,5,5,32]{4,1,3,2,0:T(1,128)}, u32[]{:S(2)}) copy-start(s32[1,1,5,5,32]{4,1,3,2,0:T(1,128)} %param.15) | copy-start | bytes 9604
  0.7 12.1 %copy-start.6 = (s32[1,1,5,5,32]{4,1,3,2,0:T(1,128)S(1)}, s32[1,1,5,5,32]{4,1,3,2,0:T(1,128)}, u32[]{:S(2)}) copy-start(s32[1,1,5,5,32]{4,1,3,2,0:T(1,128)} %param.16) | copy-start | bytes 9604
  0.7 12.1 %copy-start.7 = (f32[10,32]{1,0:T(8,128)S(1)}, f32[10,32]{1,0:T(8,128)}, u32[]{:S(2)}) copy-start(f32[10,32]{1,0:T(8,128)} %emb_ref.1) | copy-start | bytes 3844
  0.7 12.1 %copy-start.9 = (f32[8,32]{1,0:T(8,128)S(1)}, f32[8,32]{1,0:T(8,128)}, u32[]{:S(2)}) copy-start(f32[8,32]{1,0:T(8,128)} %in_ref.1) | copy-start | bytes 3076
  2.4 13.6 %copy-start = (f32[296,128]{1,0:T(8,128)S(1)}, f32[296,128]{1,0:T(8,128)}, u32[]{:S(2)}) copy-start(f32[296,128]{1,0:T(8,128)} %pack_targets.1.refs_7_) | copy-start | bytes 454660
  2.4 12.9 %collective-permute-start.2 = (f32[296,128]{1,0:T(8,128)}, f32[296,128]{1,0:T(8,128)S(1)}, u32[]{:S(2)}, u32[]{:S(2)}) collective-permute-start(f32[296,128]{1,0:T(8,128)} %pack_targets.1.refs_7_), channel_id=1, source_target_pairs={{0,7},{1,2},{2,1},{3,4},{4,3},{5,6},{6,5},{7,0},{8,15},{9,10},{10,... | collective-permute-start | bytes 454664 | tf_op jit(solution)/shard_map/ppermute | solution.py:31
  8.4 7.6 %collective-permute-start.3 = (f32[296,128]{1,0:T(8,128)}, f32[296,128]{1,0:T(8,128)S(1)}, u32[]{:S(2)}, u32[]{:S(2)}) collective-permute-start(f32[296,128]{1,0:T(8,128)} %pack_targets.1.refs_7_), channel_id=1, source_target_pairs={{0,1},{1,0},{2,3},{3,2},{4,5},{5,4},{6,7},{7,6},{8,9},{9,8},{10,11... | collective-permute-start | bytes 454664 | tf_op jit(solution)/shard_map/ppermute | solution.py:31
  8.4 9.8 %collective-permute-start.4 = (f32[296,128]{1,0:T(8,128)}, f32[296,128]{1,0:T(8,128)S(1)}, u32[]{:S(2)}, u32[]{:S(2)}) collective-permute-start(f32[296,128]{1,0:T(8,128)} %pack_targets.1.refs_7_), channel_id=1, source_target_pairs={{0,6},{1,7},{2,4},{3,5},{4,2},{5,3},{6,0},{7,1},{8,14},{9,15},{10,... | collective-permute-start | bytes 454664 | tf_op jit(solution)/shard_map/ppermute | solution.py:31
  9.0 9.5 %collective-permute-start.5 = (f32[296,128]{1,0:T(8,128)}, f32[296,128]{1,0:T(8,128)S(1)}, u32[]{:S(2)}, u32[]{:S(2)}) collective-permute-start(f32[296,128]{1,0:T(8,128)} %pack_targets.1.refs_7_), channel_id=1, source_target_pairs={{0,2},{1,3},{2,0},{3,1},{4,6},{5,7},{6,4},{7,5},{8,10},{9,11},{10,... | collective-permute-start | bytes 454664 | tf_op jit(solution)/shard_map/ppermute | solution.py:31
  10.0 1.3 %collective-permute-start = (f32[40,128]{1,0:T(8,128)S(1)}, f32[40,128]{1,0:T(8,128)S(1)}, u32[]{:S(2)}, u32[]{:S(2)}) collective-permute-start(f32[40,128]{1,0:T(8,128)S(1)} %pack_sources.1.lower_ref.refs_4_), channel_id=1, source_target_pairs={{0,8},{8,0},{16,24},{24,16},{1,9},{9,1},{17,25},{25,17},{2,10},{10... | collective-permute-start | bytes 61448 | tf_op jit(solution)/shard_map/ppermute | solution.py:31
  11.3 4.0 %collective-permute-start.1 = (f32[80,128]{1,0:T(8,128)S(1)}, f32[80,128]{1,0:T(8,128)S(1)}, u32[]{:S(2)}, u32[]{:S(2)}) collective-permute-start(f32[80,128]{1,0:T(8,128)S(1)} %stack.1), channel_id=1, source_target_pairs={{0,16},{8,24},{16,0},{24,8},{1,17},{9,25},{17,1},{25,9},{2,18},{10... | collective-permute-start | bytes 122888 | tf_op jit(solution)/shard_map/ppermute | solution.py:31
  17.9 3.7 %collective-permute-start.6 = (f32[8,128]{1,0:T(8,128)S(1)}, f32[8,128]{1,0:T(8,128)S(1)}, u32[]{:S(2)}, u32[]{:S(2)}) collective-permute-start(f32[8,128]{1,0:T(8,128)S(1)} %get-tuple-element.40), channel_id=1, source_target_pairs={{0,1},{1,0},{2,3},{3,2},{4,5},{5,4},{6,7},{7,6},{8,9},{9,8},{10,11... | collective-permute-start | bytes 12296 | tf_op jit(solution)/shard_map/ppermute | solution.py:31
  21.6 1.2 %collective-permute-start.7 = (f32[80,128]{1,0:T(8,128)S(1)}, f32[80,128]{1,0:T(8,128)S(1)}, u32[]{:S(2)}, u32[]{:S(2)}) collective-permute-start(f32[80,128]{1,0:T(8,128)S(1)} %get-tuple-element.46), channel_id=1, source_target_pairs={{0,8},{8,0},{16,24},{24,16},{1,9},{9,1},{17,25},{25,17},{2,10},{10... | collective-permute-start | bytes 122888 | tf_op jit(solution)/shard_map/ppermute | solution.py:31
  22.8 7.9 %collective-permute-start.8 = (f32[40,128]{1,0:T(8,128)S(1)}, f32[40,128]{1,0:T(8,128)S(1)}, u32[]{:S(2)}, u32[]{:S(2)}) collective-permute-start(f32[40,128]{1,0:T(8,128)S(1)} %slice_add_fusion), channel_id=1, source_target_pairs={{0,16},{8,24},{16,0},{24,8},{1,17},{9,25},{17,1},{25,9},{2,18},{10... | collective-permute-start | bytes 61448 | tf_op jit(solution)/shard_map/ppermute | solution.py:31
  24.3 5.4 %collective-permute-start.9 = (f32[8,128]{1,0:T(8,128)S(1)}, f32[8,128]{1,0:T(8,128)S(1)}, u32[]{:S(2)}, u32[]{:S(2)}) collective-permute-start(f32[8,128]{1,0:T(8,128)S(1)} %get-tuple-element.48), channel_id=1, source_target_pairs={{0,6},{1,7},{2,4},{3,5},{4,2},{5,3},{6,0},{7,1},{8,14},{9,15},{10,... | collective-permute-start | bytes 12296 | tf_op jit(solution)/shard_map/ppermute | solution.py:31
  27.1 3.6 %collective-permute-start.10 = (f32[8,128]{1,0:T(8,128)S(1)}, f32[8,128]{1,0:T(8,128)S(1)}, u32[]{:S(2)}, u32[]{:S(2)}) collective-permute-start(f32[8,128]{1,0:T(8,128)S(1)} %get-tuple-element.49), channel_id=1, source_target_pairs={{0,2},{1,3},{2,0},{3,1},{4,6},{5,7},{6,4},{7,5},{8,10},{9,11},{10,... | collective-permute-start | bytes 12296 | tf_op jit(solution)/shard_map/ppermute | solution.py:31

commit v3 on v2

--- a/solution.py
+++ b/solution.py
@@ -66,23 +66,18 @@
     return lax.dot_general(a, b, (((0,), (0,)), ((), ())), preferred_element_type=f32)
 
 
-def pack_targets_kernel(pos_ref, cot_ref, out_ref):
-    atoms = cot_ref.shape[2]
+def pack_kernel(pos_ref, feat_ref, cot_ref, gx_ref, gy_ref):
+    atoms, channels = feat_ref.shape[2:]
     parts = len(degree)
-    channels = out_ref.shape[1]
+    gx_ref[0:atoms] = feat_ref[0, 0]
     for m in range(parts):
-        out_ref[m * atoms : (m + 1) * atoms] = cot_ref[0, 0, :, m * channels : (m + 1) * channels]
-    out_ref[parts * atoms :] = jnp.zeros((sublanes, channels), f32)
+        gy_ref[m * atoms : (m + 1) * atoms] = cot_ref[0, 0, :, m * channels : (m + 1) * channels]
+    zero = jnp.zeros((sublanes, channels), f32)
+    gx_ref[atoms:] = zero
+    gy_ref[parts * atoms :] = zero
     for axis in range(3):
-        out_ref[parts * atoms + axis : parts * atoms + axis + 1, 0:atoms] = pos_ref[0, axis]
-
-
-def pack_sources_kernel(pos_ref, feat_ref, out_ref):
-    atoms, channels = feat_ref.shape[2:]
-    out_ref[0:atoms] = feat_ref[0, 0]
-    out_ref[atoms:] = jnp.zeros((sublanes, channels), f32)
-    for axis in range(3):
-        out_ref[atoms + axis : atoms + axis + 1, 0:atoms] = pos_ref[0, axis]
+        gx_ref[atoms + axis : atoms + axis + 1, 0:atoms] = pos_ref[0, axis]
+        gy_ref[parts * atoms + axis : parts * atoms + axis + 1, 0:atoms] = pos_ref[0, axis]
 
 
 def stack_kernel(upper_ref, lower_ref, out_ref):
@@ -314,10 +309,12 @@
     at_y = lax.axis_index("gy")
     to_far = ((at_y + (at_y >> 1)) & 1).astype(f32)
     relay = relay_ref[:, atoms : 2 * atoms]
-    near_out[...] = near_ref[...]
-    far_out[...] = far_ref[...]
-    near_out[:, 0:atoms] = near_ref[:, 0:atoms] + relay * (1.0 - to_far)
-    far_out[:, 0:atoms] = far_ref[:, 0:atoms] + relay * to_far
+    near_out[...] = jnp.zeros(near_out.shape, f32)
+    far_out[...] = jnp.zeros(far_out.shape, f32)
+    near_out[0:sublanes] = near_ref[...]
+    far_out[0:sublanes] = far_ref[...]
+    near_out[0:sublanes, 0:atoms] = near_ref[:, 0:atoms] + relay * (1.0 - to_far)
+    far_out[0:sublanes, 0:atoms] = far_ref[:, 0:atoms] + relay * to_far
 
 
 def sum_kernel(gx_count, *refs):
@@ -336,18 +333,20 @@
 
 
 vmem = pl.BlockSpec(memory_space=pltpu.VMEM)
-hbm = pl.BlockSpec(memory_space=pltpu.HBM)
-
-
-def call(kernel, name, out_shape, operands, scratch=(), room=4, space=vmem):
+
+
+def call(kernel, name, out_shape, operands, scratch=(), room=4, us=None):
     return pl.pallas_call(
         kernel,
         out_shape=out_shape,
-        in_specs=[space] * len(operands),
+        in_specs=[vmem] * len(operands),
         out_specs=(vmem,) * len(out_shape),
         scratch_shapes=list(scratch),
         compiler_params=pltpu.CompilerParams(vmem_limit_bytes=room and room * megabyte),
         name=name,
+        cost_estimate=us and pl.CostEstimate(
+            flops=int(us * 1e9), bytes_accessed=0, transcendentals=0
+        ),
     )(*operands)
 
 
@@ -356,10 +355,12 @@
         return [own] + [link.swap(own, "gx") for link in links]
     one = links[0].swap(own, "gx")
     rows, columns = own.shape
+    two = links[2].swap(own, "gx")
     (both,) = call(
-        stack_kernel, "stack", (jax.ShapeDtypeStruct((2 * rows, columns), own.dtype),), (one, own)
-    )
-    return [own, one, links[2].swap(both, "gx")]
+        stack_kernel, "stack", (jax.ShapeDtypeStruct((2 * rows, columns), own.dtype),), (own, two),
+        us=2,
+    )
+    return [own, links[0].swap(both, "gx"), two]
 
 
 def gx_shapes(links, block):
@@ -398,10 +399,9 @@
     lists = [jnp.transpose(x, (0, 2, 3, 1, 4)) for x in (nbr_src, nbr_tgt, pair_mask, pair_species)]
     gx_pack = sds((atoms + sublanes, channels), f32)
     gy_pack = sds((len(degree) * atoms + sublanes, channels), f32)
-    (gy_own,) = call(
-        pack_targets_kernel, "pack_targets", (gy_pack,), (by_axis, cotangent), room=None
-    )
-    (gx_own,) = call(pack_sources_kernel, "pack_sources", (gx_pack,), (by_axis, features))
+    gx_own, gy_own = call(
+        pack_kernel, "pack", (gx_pack, gy_pack), (by_axis, features, cotangent), room=None
+    )
     gy_packs = [gy_own] + [link.swap(gy_own, "gy") for link in gy_links]
     gx_packs = gather(gx_links, gx_own)
 
@@ -420,6 +420,7 @@
     weights = (wide, back, first, last)
     packs = [[gy_packs[table] for table in group] for group in groups]
     tgt_pack = sds((sublanes, channels), f32)
+    far_pack = sds((2 * channels // 4, channels), f32)
     src_pos, feats, feat, pos, tgt = call(
         functools.partial(first_kernel, orders, groups[0], len(gx_packs)), "tiles",
         (
@@ -435,7 +436,7 @@
         gx_shapes(gx_links, gx_pack) + (tgt_pack,) * 2,
         (rows[1], *weights, src_pos, feats, feat, pos, *packs[1]), room=16,
     )
-    near, far = call(functools.partial(join_kernel, atoms), "join", (tgt_pack,) * 2, (relay, near, far))
+    near, far = call(functools.partial(join_kernel, atoms), "join", (far_pack,) * 2, (relay, near, far))
     *gx_outs, near, far = lax.optimization_barrier((*gx_outs, near, far))
     back_gy = [gy_links[3].swap(far, "gy"), gy_links[2].swap(near, "gy"), relay]
     back_gx = scatter(gx_links, gx_outs)

time: 31.5 us -> 30.3 us (0.962)
  waiting for transfers between devices: 10.6 us -> 9.04 us
  local copies, waits for them, and re-layouts: 0.04 us -> 1.43 us
  starting transfers between devices: 13.8 us -> 12.8 us
    ppermute x11, waiting for transfers between devices: 10.6 us -> 9.04 us  [swap(): lax.ppermute(value, axis, [(i, (i + self.delta(i)) % n) for i in range(n)])]
    unnamed x20, local copies, waits for them, and re-layouts: 0.04 us -> 1.43 us
    ppermute x11, starting transfers between devices: 13.8 us -> 12.8 us  [swap(): lax.ppermute(value, axis, [(i, (i + self.delta(i)) % n) for i in range(n)])]
    pallas_call x8 -> x7, Pallas kernels: 6.11 us -> 6.08 us  [call(): pl.pallas_call(kernel, out_shape=out_shape, in_specs=[vmem] * len(operand...]
  transfers between devices with their start and end apart: 11 -> 11, of which waited for: 8 -> 7; matrix products, arithmetic and copies ran while one was open for 0% -> 0% of each run, Pallas kernels for 12% -> 12%
where the time goes in v3:
time: 30.3 us; the launch traced here: 30.1 us
  starting transfers between devices  12.8 us (42%)
  waiting for transfers between devices  9.04 us (30%)
  Pallas kernels  6.08 us (20%)
  local copies, waits for them, and re-layouts  1.43 us (5%)
  between operations  0.75 us (2%)
    ppermute x11, starting transfers between devices, swap(): lax.ppermute(value, axis, [(i, (i + self.delta(i)) % n) for i in range(n)])  12.8 us
    ppermute x11, waiting for transfers between devices, swap(): lax.ppermute(value, axis, [(i, (i + self.delta(i)) % n) for i in range(n)])  9.04 us
    pallas_call x7, Pallas kernels, call(): pl.pallas_call(kernel, out_shape=out_shape, in_specs=[vmem] * len(operand...  6.08 us
    unnamed x20, local copies, waits for them, and re-layouts  1.43 us
  transfers between devices with their start and end apart: 11, of which 7 were waited for; matrix products, arithmetic and copies ran while one was open for 0% of the time, Pallas kernels for 12%

profile of v3, /device:TPU:0, one launch (start us, length us, event | category | flops | bytes accessed | tf_op | source)
XLA Modules:
  0.0 30.1 jit_solution(14611999947432736204)
XLA Ops:
  0.6 1.6 %pack.1 = (f32[40,128]{1,0:T(8,128)}, f32[296,128]{1,0:T(8,128)}) custom-call(f32[1,3,1,32]{3,2,1,0:T(1,128)} %bitcast.10, f32[1,1,32,128]{3,2,1,0:T(8,128)} %feat_ref.1, f32[1,1,32,1152]{3,2,1,0:T(8,128)} %cot_ref.1), custom_call_target="tpu_custom_call" | custom-call | tf_op jit(solution)/shard_map/pack/pallas_call | solution.py:339
  2.3 2.9 %collective-permute-start = (f32[40,128]{1,0:T(8,128)}, f32[40,128]{1,0:T(8,128)S(1)}, u32[]{:S(2)}, u32[]{:S(2)}) collective-permute-start(f32[40,128]{1,0:T(8,128)} %get-tuple-element.35.upper_ref.refs_4_), channel_id=1, source_target_pairs={{0,16},{8,24},{16,0},{24,8},{1,17},{9,25},{17,1},{25,9},{2,18},{10... | collective-permute-start | bytes 61448 | tf_op jit(solution)/shard_map/ppermute | solution.py:31
  5.2 4.6 %collective-permute-start.2 = (f32[296,128]{1,0:T(8,128)}, f32[296,128]{1,0:T(8,128)S(1)}, u32[]{:S(2)}, u32[]{:S(2)}) collective-permute-start(f32[296,128]{1,0:T(8,128)} %get-tuple-element.36.refs_7_), channel_id=1, source_target_pairs={{0,7},{1,2},{2,1},{3,4},{4,3},{5,6},{6,5},{7,0},{8,15},{9,10},{10,... | collective-permute-start | bytes 454664 | tf_op jit(solution)/shard_map/ppermute | solution.py:31
  9.8 0.7 %collective-permute-start.4 = (f32[296,128]{1,0:T(8,128)}, f32[296,128]{1,0:T(8,128)S(1)}, u32[]{:S(2)}, u32[]{:S(2)}) collective-permute-start(f32[296,128]{1,0:T(8,128)} %get-tuple-element.36.refs_7_), channel_id=1, source_target_pairs={{0,6},{1,7},{2,4},{3,5},{4,2},{5,3},{6,0},{7,1},{8,14},{9,15},{10,... | collective-permute-start | bytes 454664 | tf_op jit(solution)/shard_map/ppermute | solution.py:31
  10.5 0.9 %collective-permute-start.5 = (f32[296,128]{1,0:T(8,128)}, f32[296,128]{1,0:T(8,128)S(1)}, u32[]{:S(2)}, u32[]{:S(2)}) collective-permute-start(f32[296,128]{1,0:T(8,128)} %get-tuple-element.36.refs_7_), channel_id=1, source_target_pairs={{0,2},{1,3},{2,0},{3,1},{4,6},{5,7},{6,4},{7,5},{8,10},{9,11},{10,... | collective-permute-start | bytes 454664 | tf_op jit(solution)/shard_map/ppermute | solution.py:31
  11.4 0.0 collective-permute-done.lower_ref.refs_6_
  11.4 0.7 %copy-done.2 = f32[40,128]{1,0:T(8,128)S(1)} copy-done((f32[40,128]{1,0:T(8,128)S(1)}, f32[40,128]{1,0:T(8,128)}, u32[]{:S(2)}) %copy-start.2) | copy-done | bytes 20504
  12.1 0.0 copy-start.8
  12.2 0.0 copy-start.9
  12.2 0.1 collective-permute-start.1
  12.3 0.6 %copy-done.4 = s32[1,1,5,5,32]{4,1,3,2,0:T(1,128)S(1)} copy-done((s32[1,1,5,5,32]{4,1,3,2,0:T(1,128)S(1)}, s32[1,1,5,5,32]{4,1,3,2,0:T(1,128)}, u32[]{:S(2)}) %copy-start.4) | copy-done | bytes 3224
  12.8 0.0 copy-done.5
  12.8 0.0 copy-done.6
  12.9 0.0 copy-done.7
  12.9 0.0 copy-done.8
  12.9 0.1 copy-done.9
  13.0 0.2 prepare.1
  13.2 0.3 collective-permute-done.1.refs_5_
  13.5 1.0 %collective-permute-done.2.refs_8_ = f32[296,128]{1,0:T(8,128)S(1)} collective-permute-done((f32[296,128]{1,0:T(8,128)}, f32[296,128]{1,0:T(8,128)S(1)}, u32[]{:S(2)}, u32[]{:S(2)}) %collective-permute-start.2) | collective-permute-done | bytes 151584 | tf_op jit(solution)/shard_map/ppermute | solution.py:31
  14.5 2.5 %collective-permute-done.3.refs_9_ = f32[296,128]{1,0:T(8,128)S(1)} collective-permute-done((f32[296,128]{1,0:T(8,128)}, f32[296,128]{1,0:T(8,128)S(1)}, u32[]{:S(2)}, u32[]{:S(2)}) %collective-permute-start.3) | collective-permute-done | bytes 151584 | tf_op jit(solution)/shard_map/ppermute | solution.py:31
  17.0 1.9 %tiles.2 = (bf16[24,128]{1,0:T(8,128)(2,1)S(1)}, bf16[128,256]{1,0:T(8,128)(2,1)S(1)}, f32[128,128]{1,0:T(8,128)S(1)}, f32[8,128]{1,0:T(8,128)S(1)}, f32[8,128]{1,0:T(8,128)S(1)}) custom-call(s32[8,480]{1,0:T(8,128)S(1)} %get-tuple-element.34.rows_ref, bf16[384,96]{1,0:T(8,128)(2,1)S(1)} %get-tuple-element.30.refs_0_, ...), custom_call_target="tpu_custom_call" | custom-call | tf_op jit(solution)/shard_map/tiles/pallas_call | solution.py:339
  18.9 0.1 collective-permute-start.6
  19.0 0.6 %collective-permute-done.5.refs_9_ = f32[296,128]{1,0:T(8,128)S(1)} collective-permute-done((f32[296,128]{1,0:T(8,128)}, f32[296,128]{1,0:T(8,128)S(1)}, u32[]{:S(2)}, u32[]{:S(2)}) %collective-permute-start.5) | collective-permute-done | bytes 151584 | tf_op jit(solution)/shard_map/ppermute | solution.py:31
  19.6 1.6 %tiles.3 = (f32[40,128]{1,0:T(8,128)S(1)}, f32[80,128]{1,0:T(8,128)S(1)}, f32[40,128]{1,0:T(8,128)S(1)}, f32[8,128]{1,0:T(8,128)S(1)}, f32[8,128]{1,0:T(8,128)S(1)}) custom-call(s32[8,320]{1,0:T(8,128)S(1)} %get-tuple-element.29.rows_ref, bf16[384,96]{1,0:T(8,128)(2,1)S(1)} %get-tuple-element.30.refs_0_, bf16[64,768]{1,0:T(8,128)(2,1)S(1)} %get-tuple-element.31.refs_1_, ...), custom_call_target="tpu_custom_call" | custom-call | tf_op jit(solution)/shard_map/tiles/pallas_call | solution.py:339
  21.2 1.4 %collective-permute-done.6.relay_ref.refs_5_ = f32[8,128]{1,0:T(8,128)S(1)} collective-permute-done((f32[8,128]{1,0:T(8,128)S(1)}, f32[8,128]{1,0:T(8,128)S(1)}, u32[]{:S(2)}, u32[]{:S(2)}) %collective-permute-start.6) | collective-permute-done | bytes 4128 | tf_op jit(solution)/shard_map/ppermute | solution.py:31
  22.6 0.1 join.1
  22.6 0.0 collective-permute-start.7
  22.7 2.9 %collective-permute-start.9 = (f32[64,128]{1,0:T(8,128)S(1)}, f32[64,128]{1,0:T(8,128)S(1)}, u32[]{:S(2)}, u32[]{:S(2)}) collective-permute-start(f32[64,128]{1,0:T(8,128)S(1)} %get-tuple-element.52), channel_id=1, source_target_pairs={{0,6},{1,7},{2,4},{3,5},{4,2},{5,3},{6,0},{7,1},{8,14},{9,15},{10,... | collective-permute-start | bytes 98312 | tf_op jit(solution)/shard_map/ppermute | solution.py:31
  25.6 0.6 %collective-permute-start.8 = (f32[40,128]{1,0:T(8,128)S(1)}, f32[40,128]{1,0:T(8,128)S(1)}, u32[]{:S(2)}, u32[]{:S(2)}) collective-permute-start(f32[40,128]{1,0:T(8,128)S(1)} %slice_add_fusion), channel_id=1, source_target_pairs={{0,16},{8,24},{16,0},{24,8},{1,17},{9,25},{17,1},{25,9},{2,18},{10... | collective-permute-start | bytes 61448 | tf_op jit(solution)/shard_map/ppermute | solution.py:31
  26.2 2.5 %collective-permute-done.9.refs_3_ = f32[64,128]{1,0:T(8,128)S(1)} collective-permute-done((f32[64,128]{1,0:T(8,128)S(1)}, f32[64,128]{1,0:T(8,128)S(1)}, u32[]{:S(2)}, u32[]{:S(2)}) %collective-permute-start.9) | collective-permute-done | bytes 32800 | tf_op jit(solution)/shard_map/ppermute | solution.py:31
  28.7 0.8 %collective-permute-done.10.refs_4_ = f32[64,128]{1,0:T(8,128)S(1)} collective-permute-done((f32[64,128]{1,0:T(8,128)S(1)}, f32[64,128]{1,0:T(8,128)S(1)}, u32[]{:S(2)}, u32[]{:S(2)}) %collective-permute-start.10) | collective-permute-done | bytes 32800 | tf_op jit(solution)/shard_map/ppermute | solution.py:31
  29.5 0.6 %sums.1 = (f32[1,3,1,32]{3,2,1,0:T(1,128)}, f32[1,1,32,128]{3,2,1,0:T(8,128)}) custom-call(f32[40,128]{1,0:T(8,128)S(1)} %get-tuple-element.49.refs_0_, f32[80,128]{1,0:T(8,128)S(1)} %collective-permute-done.7.refs_1_, f32[40,128]{1,0:T(8,128)S(1)} %collective-permute-done.8.refs_2_, f32[64,128]{1,0:T(8,128)S(1)} %collective-permute-done.9.refs_3_, ...), custom_call_target="tpu_custom_call" | custom-call | tf_op jit(solution)/shard_map/sums/pallas_call | solution.py:339
  (18 shorter events, 0.0 us)
Async XLA Ops:
  2.3 9.1 %collective-permute-start = (f32[40,128]{1,0:T(8,128)}, f32[40,128]{1,0:T(8,128)S(1)}, u32[]{:S(2)}, u32[]{:S(2)}) collective-permute-start(f32[40,128]{1,0:T(8,128)} %get-tuple-element.35.upper_ref.refs_4_), channel_id=1, source_target_pairs={{0,16},{8,24},{16,0},{24,8},{1,17},{9,25},{17,1},{25,9},{2,18},{10... | collective-permute-start | bytes 61448 | tf_op jit(solution)/shard_map/ppermute | solution.py:31
  5.2 7.1 %copy-start.1 = (f32[32,384]{1,0:T(8,128)S(1)}, f32[32,384]{1,0:T(8,128)}, u32[]{:S(2)}) copy-start(f32[32,384]{1,0:T(8,128)} %out_ref.1) | copy-start | bytes 147460
  5.2 9.3 %collective-permute-start.2 = (f32[296,128]{1,0:T(8,128)}, f32[296,128]{1,0:T(8,128)S(1)}, u32[]{:S(2)}, u32[]{:S(2)}) collective-permute-start(f32[296,128]{1,0:T(8,128)} %get-tuple-element.36.refs_7_), channel_id=1, source_target_pairs={{0,7},{1,2},{2,1},{3,4},{4,3},{5,6},{6,5},{7,0},{8,15},{9,10},{10,... | collective-permute-start | bytes 454664 | tf_op jit(solution)/shard_map/ppermute | solution.py:31
  9.8 7.2 %collective-permute-start.3 = (f32[296,128]{1,0:T(8,128)}, f32[296,128]{1,0:T(8,128)S(1)}, u32[]{:S(2)}, u32[]{:S(2)}) collective-permute-start(f32[296,128]{1,0:T(8,128)} %get-tuple-element.36.refs_7_), channel_id=1, source_target_pairs={{0,1},{1,0},{2,3},{3,2},{4,5},{5,4},{6,7},{7,6},{8,9},{9,8},{10,11... | collective-permute-start | bytes 454664 | tf_op jit(solution)/shard_map/ppermute | solution.py:31
  9.8 9.2 %collective-permute-start.4 = (f32[296,128]{1,0:T(8,128)}, f32[296,128]{1,0:T(8,128)S(1)}, u32[]{:S(2)}, u32[]{:S(2)}) collective-permute-start(f32[296,128]{1,0:T(8,128)} %get-tuple-element.36.refs_7_), channel_id=1, source_target_pairs={{0,6},{1,7},{2,4},{3,5},{4,2},{5,3},{6,0},{7,1},{8,14},{9,15},{10,... | collective-permute-start | bytes 454664 | tf_op jit(solution)/shard_map/ppermute | solution.py:31
  10.5 9.1 %collective-permute-start.5 = (f32[296,128]{1,0:T(8,128)}, f32[296,128]{1,0:T(8,128)S(1)}, u32[]{:S(2)}, u32[]{:S(2)}) collective-permute-start(f32[296,128]{1,0:T(8,128)} %get-tuple-element.36.refs_7_), channel_id=1, source_target_pairs={{0,2},{1,3},{2,0},{3,1},{4,6},{5,7},{6,4},{7,5},{8,10},{9,11},{10,... | collective-permute-start | bytes 454664 | tf_op jit(solution)/shard_map/ppermute | solution.py:31
  11.4 0.7 %copy-start.2 = (f32[40,128]{1,0:T(8,128)S(1)}, f32[40,128]{1,0:T(8,128)}, u32[]{:S(2)}) copy-start(f32[40,128]{1,0:T(8,128)} %get-tuple-element.35.upper_ref.refs_4_) | copy-start | bytes 61444
  12.1 0.7 %copy-start.4 = (s32[1,1,5,5,32]{4,1,3,2,0:T(1,128)S(1)}, s32[1,1,5,5,32]{4,1,3,2,0:T(1,128)}, u32[]{:S(2)}) copy-start(s32[1,1,5,5,32]{4,1,3,2,0:T(1,128)} %param.13) | copy-start | bytes 9604
  12.1 0.7 %copy-start.5 = (s32[1,1,5,5,32]{4,1,3,2,0:T(1,128)S(1)}, s32[1,1,5,5,32]{4,1,3,2,0:T(1,128)}, u32[]{:S(2)}) copy-start(s32[1,1,5,5,32]{4,1,3,2,0:T(1,128)} %param.14) | copy-start | bytes 9604
  12.1 0.7 %copy-start.6 = (s32[1,1,5,5,32]{4,1,3,2,0:T(1,128)S(1)}, s32[1,1,5,5,32]{4,1,3,2,0:T(1,128)}, u32[]{:S(2)}) copy-start(s32[1,1,5,5,32]{4,1,3,2,0:T(1,128)} %param.15) | copy-start | bytes 9604
  12.1 0.8 %copy-start.7 = (s32[1,1,5,5,32]{4,1,3,2,0:T(1,128)S(1)}, s32[1,1,5,5,32]{4,1,3,2,0:T(1,128)}, u32[]{:S(2)}) copy-start(s32[1,1,5,5,32]{4,1,3,2,0:T(1,128)} %param.16) | copy-start | bytes 9604
  12.1 0.8 %copy-start.8 = (f32[10,32]{1,0:T(8,128)S(1)}, f32[10,32]{1,0:T(8,128)}, u32[]{:S(2)}) copy-start(f32[10,32]{1,0:T(8,128)} %emb_ref.1) | copy-start | bytes 3844
  12.1 4.8 %copy-start = (f32[296,128]{1,0:T(8,128)S(1)}, f32[296,128]{1,0:T(8,128)}, u32[]{:S(2)}) copy-start(f32[296,128]{1,0:T(8,128)} %get-tuple-element.36.refs_7_) | copy-start | bytes 454660
  12.2 0.8 %copy-start.9 = (f32[8,32]{1,0:T(8,128)S(1)}, f32[8,32]{1,0:T(8,128)}, u32[]{:S(2)}) copy-start(f32[8,32]{1,0:T(8,128)} %in_ref.1) | copy-start | bytes 3076
  12.2 1.3 %collective-permute-start.1 = (f32[80,128]{1,0:T(8,128)S(1)}, f32[80,128]{1,0:T(8,128)S(1)}, u32[]{:S(2)}, u32[]{:S(2)}) collective-permute-start(f32[80,128]{1,0:T(8,128)S(1)} %stack.1), channel_id=1, source_target_pairs={{0,8},{8,0},{16,24},{24,16},{1,9},{9,1},{17,25},{25,17},{2,10},{10... | collective-permute-start | bytes 122888 | tf_op jit(solution)/shard_map/ppermute | solution.py:31
  12.9 4.0 %copy-start.3 = (f32[40,128]{1,0:T(8,128)S(1)}, f32[40,128]{1,0:T(8,128)}, u32[]{:S(2)}) copy-start(f32[40,128]{1,0:T(8,128)} %get-tuple-element.35.upper_ref.refs_4_) | copy-start | bytes 61444
  18.9 3.7 %collective-permute-start.6 = (f32[8,128]{1,0:T(8,128)S(1)}, f32[8,128]{1,0:T(8,128)S(1)}, u32[]{:S(2)}, u32[]{:S(2)}) collective-permute-start(f32[8,128]{1,0:T(8,128)S(1)} %get-tuple-element.44), channel_id=1, source_target_pairs={{0,1},{1,0},{2,3},{3,2},{4,5},{5,4},{6,7},{7,6},{8,9},{9,8},{10,11... | collective-permute-start | bytes 12296 | tf_op jit(solution)/shard_map/ppermute | solution.py:31
  22.6 2.9 %collective-permute-start.7 = (f32[80,128]{1,0:T(8,128)S(1)}, f32[80,128]{1,0:T(8,128)S(1)}, u32[]{:S(2)}, u32[]{:S(2)}) collective-permute-start(f32[80,128]{1,0:T(8,128)S(1)} %get-tuple-element.50), channel_id=1, source_target_pairs={{0,8},{8,0},{16,24},{24,16},{1,9},{9,1},{17,25},{25,17},{2,10},{10... | collective-permute-start | bytes 122888 | tf_op jit(solution)/shard_map/ppermute | solution.py:31
  22.7 6.1 %collective-permute-start.9 = (f32[64,128]{1,0:T(8,128)S(1)}, f32[64,128]{1,0:T(8,128)S(1)}, u32[]{:S(2)}, u32[]{:S(2)}) collective-permute-start(f32[64,128]{1,0:T(8,128)S(1)} %get-tuple-element.52), channel_id=1, source_target_pairs={{0,6},{1,7},{2,4},{3,5},{4,2},{5,3},{6,0},{7,1},{8,14},{9,15},{10,... | collective-permute-start | bytes 98312 | tf_op jit(solution)/shard_map/ppermute | solution.py:31
  25.6 3.9 %collective-permute-start.10 = (f32[64,128]{1,0:T(8,128)S(1)}, f32[64,128]{1,0:T(8,128)S(1)}, u32[]{:S(2)}, u32[]{:S(2)}) collective-permute-start(f32[64,128]{1,0:T(8,128)S(1)} %get-tuple-element.53), channel_id=1, source_target_pairs={{0,2},{1,3},{2,0},{3,1},{4,6},{5,7},{6,4},{7,5},{8,10},{9,11},{10,... | collective-permute-start | bytes 98312 | tf_op jit(solution)/shard_map/ppermute | solution.py:31
  25.6 3.9 %collective-permute-start.8 = (f32[40,128]{1,0:T(8,128)S(1)}, f32[40,128]{1,0:T(8,128)S(1)}, u32[]{:S(2)}, u32[]{:S(2)}) collective-permute-start(f32[40,128]{1,0:T(8,128)S(1)} %slice_add_fusion), channel_id=1, source_target_pairs={{0,16},{8,24},{16,0},{24,8},{1,17},{9,25},{17,1},{25,9},{2,18},{10... | collective-permute-start | bytes 61448 | tf_op jit(solution)/shard_map/ppermute | solution.py:31

commit v4 on v3

v4 whole, which is shorter than its diff:
```python
import functools
import math

import jax
import jax.numpy as jnp
from jax import lax
from jax.experimental import pallas as pl
from jax.experimental.pallas import tpu as pltpu
from jax.sharding import PartitionSpec as P

domain_side = 5.0
cutoff = 12.0
soften = 0.25
reach = 2
sublanes = 8
degree = (0, 1, 1, 1, 2, 2, 2, 2, 2)
megabyte = 1024 * 1024
f32 = jnp.float32
bf16 = jnp.bfloat16


class Link:
    def __init__(self, step, bit, peers):
        self.step, self.bit, self.peers = step, bit, peers

    def delta(self, i):
        return self.step * (1 - 2 * ((i >> self.bit) & 1))

    def swap(self, value, axis):
        n = self.peers
        return lax.ppermute(value, axis, [(i, (i + self.delta(i)) % n) for i in range(n)])


def links_of(peers):
    assert peers % 4 == 0, peers
    steps = [(1, 0), (-1, 0), (2, 1)] + ([(-2, 1)] if peers > 4 else [])
    return [Link(step, bit, peers) for step, bit in steps]


def gx_spots_of(links):
    spots = [(0, None, 0)]
    for table, link in enumerate(links):
        spots.append((table + 1, link, 1))
        if link.peers == 4 and abs(link.step) == 2:
            spots.append((table + 1, link, -1))
    return spots


def pieces(x, count):
    out = []
    for _ in range(count):
        out.append(x.astype(bf16).astype(f32))
        x = x - out[-1]
    return out


def dot(a, b):
    return jnp.dot(a, b, preferred_element_type=f32)


def dot_rows(a, b):
    return lax.dot_general(a, b, (((1,), (1,)), ((), ())), preferred_element_type=f32)


def dot_cols(a, b):
    return lax.dot_general(a, b, (((0,), (0,)), ((), ())), preferred_element_type=f32)


def write_rows(store, gx_spots, at_x, lists, step_y, place, start):
    atoms = pairs = lists[0].shape[4]
    for slot, (table, link, sign) in enumerate(gx_spots):
        step_x = 0 if link is None else sign * link.delta(at_x)
        src, tgt, mask, spec = (ref[0, reach + step_x, reach + step_y] for ref in lists)
        store(0, start + slot * pairs, src + table * atoms)
        store(1, start + slot * pairs, tgt + place * atoms)
        store(2, start + slot * pairs, mask)
        store(3, start + slot * pairs, spec)
        store(4, start + slot * pairs, jnp.full((1, pairs), step_x, jnp.int32))
        store(5, start + slot * pairs, jnp.full((1, pairs), -step_y, jnp.int32))


def pack_kernel(
    gx_spots, gy_links, pos_ref, feat_ref, cot_ref, src_ref, tgt_ref, mask_ref, spec_ref,
    gx_ref, y_ref, gy_ref,
):
    atoms, channels = feat_ref.shape[2:]
    pairs = src_ref.shape[4]
    parts = len(degree)
    zero = jnp.zeros((sublanes, channels), f32)
    for ref in (gx_ref, y_ref):
        ref[0:atoms] = feat_ref[0, 0]
        ref[atoms : atoms + sublanes] = zero
    for m in range(parts):
        gy_ref[m * atoms : (m + 1) * atoms] = cot_ref[0, 0, :, m * channels : (m + 1) * channels]
    gy_ref[parts * atoms :] = zero
    for axis in range(3):
        row = pos_ref[0, axis]
        gx_ref[atoms + axis : atoms + axis + 1, 0:atoms] = row
        y_ref[atoms + axis : atoms + axis + 1, 0:atoms] = row
        gy_ref[parts * atoms + axis : parts * atoms + axis + 1, 0:atoms] = row

    base = atoms + sublanes
    for start in range(base, y_ref.shape[0], sublanes):
        y_ref[start : start + sublanes] = zero

    def store(row, lane, value):
        chunk, lane = divmod(lane, channels)
        at = base + chunk * sublanes + row
        y_ref[at : at + 1, lane : lane + pairs] = value.astype(f32)

    at_x, at_y = lax.axis_index("gx"), lax.axis_index("gy")
    lists = (src_ref, tgt_ref, mask_ref, spec_ref)
    near, other = gy_links[0].delta(at_y), gy_links[1].delta(at_y)
    partner = at_y + near
    to_far = (partner + (partner >> 1)) & 1
    write_rows(store, gx_spots, at_x, lists, near, 0, 0)
    write_rows(store, gx_spots, at_x, lists, other, 1 + to_far, len(gx_spots) * pairs)


def stack_kernel(rows, *refs):
    *refs, out_ref = refs
    for at, ref in enumerate(refs):
        out_ref[at * rows : (at + 1) * rows] = ref[0:rows]


def prep_kernel(
    gx_spots, gy_links, src_ref, tgt_ref, mask_ref, spec_ref, in_ref, emb_ref, out_ref,
    rows_ref, wide_ref, back_ref, first_ref, last_ref,
):
    pairs = src_ref.shape[4]
    rows_ref[...] = jnp.zeros(rows_ref.shape, jnp.int32)

    def store(row, lane, value):
        rows_ref[row : row + 1, lane : lane + pairs] = value

    at_x, at_y = lax.axis_index("gx"), lax.axis_index("gy")
    lists = (src_ref, tgt_ref, mask_ref, spec_ref)
    for place, link in enumerate((None, gy_links[2], gy_links[3])):
        step_y = 0 if link is None else link.delta(at_y)
        write_rows(store, gx_spots, at_x, lists, step_y, place, place * len(gx_spots) * pairs)
    high, low = pieces(out_ref[...], 2)
    wide_ref[...] = jnp.concatenate([high, high, low], axis=0).T.astype(bf16)
    upper = jnp.concatenate([high, high], axis=1)
    lower = jnp.concatenate([low, jnp.zeros_like(low)], axis=1)
    back_ref[...] = jnp.concatenate([upper, lower], axis=0).astype(bf16)
    orders, hidden = in_ref.shape
    spare = jnp.zeros((sublanes * 2 - emb_ref.shape[0], hidden), f32)
    high, low = pieces(jnp.concatenate([in_ref[...], emb_ref[...], spare], axis=0), 2)
    first_ref[...] = jnp.concatenate([high, high, low], axis=0).T.astype(bf16)
    last_ref[...] = jnp.concatenate([high[0:orders], high[0:orders], low[0:orders]], axis=1).astype(bf16)


def radial_waves(dist, orders):
    order = (lax.broadcasted_iota(jnp.int32, (orders, 1), 0) + 1).astype(f32)
    turn = order * (dist * (1.0 / cutoff))
    whole = jnp.floor(turn + 0.5)
    part = turn - whole
    sign = 1.0 - 2.0 * (whole - 2.0 * jnp.floor(0.5 * whole))
    square = part * part
    sine = jnp.zeros_like(square)
    for k in (11, 9, 7, 5, 3, 1):
        sine = sine * square + (-1.0) ** (k // 2) * math.pi**k / math.factorial(k)
    cosine = jnp.zeros_like(square)
    for k in (12, 10, 8, 6, 4, 2, 0):
        cosine = cosine * square + (-1.0) ** (k // 2) * math.pi**k / math.factorial(k)
    return order, sign * part * sine, sign * cosine


def thrice(x):
    high, low = pieces(x, 2)
    return jnp.concatenate([high, low, high], axis=0).astype(bf16)


def onehot(ids, count):
    return jnp.where(lax.broadcasted_iota(jnp.int32, (count, ids.shape[1]), 0) == ids, 1.0, 0.0)


def slot_grads(rows, cot_refs, columns, weights, orders):
    wide, back, first, last = weights
    slots = rows.shape[1]
    sources = columns[0][1].shape[1]
    channels = columns[0][2].shape[0]
    hidden = last.shape[1] // 3
    parts = len(degree)
    atoms = (cot_refs[0].shape[0] - sublanes) // parts
    targets = atoms * len(cot_refs)

    src_hot = onehot(rows[0:1], sources).astype(bf16)
    tgt_hot = onehot(rows[1:2], targets).astype(bf16)
    mask = rows[2:3].astype(f32)
    offset = rows[4:6].astype(f32) * domain_side

    tgt_pos = [jnp.concatenate(pieces(ref[parts * atoms :, 0:atoms], 3), axis=0) for ref in cot_refs]
    hots = [src_hot[:, lanes] for lanes, _, _ in columns]
    from_src = jnp.concatenate([dot(c[1], hot) for c, hot in zip(columns, hots)], axis=1)
    from_tgt = dot(jnp.concatenate(tgt_pos, axis=1).astype(bf16), tgt_hot)
    from_src = from_src[0:8] + from_src[8:16] + from_src[16:24]
    from_tgt = from_tgt[0:8] + from_tgt[8:16] + from_tgt[16:24]
    rel = [
        from_src[0:1] + offset[0:1] - from_tgt[0:1],
        from_src[1:2] + offset[1:2] - from_tgt[1:2],
        from_src[2:3] - from_tgt[2:3],
    ]
    dist = jnp.sqrt(rel[0] * rel[0] + rel[1] * rel[1] + rel[2] * rel[2] + soften)
    near = 1.0 / dist
    x, y, z = (r * near for r in rel)
    scaled = dist * (1.0 / cutoff)
    room = jnp.where(scaled < 1.0, 1.0 - scaled * scaled, 0.0)
    env = room * room * mask
    d_env = (-4.0 / cutoff) * scaled * room * mask

    order, sine, cosine = radial_waves(dist, orders)
    norm = math.sqrt(2.0 / cutoff)
    basis = norm * near * sine
    d_basis = norm * near * ((math.pi / cutoff) * order * cosine - sine * near)
    species = onehot(rows[3:4], 2 * sublanes)
    before = dot(first, thrice(jnp.concatenate([basis, species], axis=0)))
    gate = 1.0 / (1.0 + jnp.exp(-before))
    act = before * gate
    d_act = gate * (1.0 + before * (1.0 - gate))
    radial = dot(wide, thrice(act))
    gathered = jnp.concatenate(
        [dot(c[2], jnp.concatenate([hot, hot], axis=0)) for c, hot in zip(columns, hots)], axis=1
    )

    root3, root5, root15 = math.sqrt(3.0), math.sqrt(5.0), math.sqrt(15.0)
    shapes = [
        None, root3 * x, root3 * y, root3 * z, root15 * x * y, root15 * y * z,
        0.5 * root5 * (2.0 * z * z - x * x - y * y), root15 * x * z, 0.5 * root15 * (x * x - y * y),
    ]
    twice = lax.broadcasted_iota(jnp.int32, (2 * targets, slots), 0)
    twice = (twice // (2 * atoms)) * atoms + lax.rem(twice, atoms)
    twice = jnp.where(twice == rows[1:2], 1.0, 0.0).astype(bf16)
    d_shapes = [None] * parts
    d_radial = []
    through = None
    for low, high in ((0, 1), (1, 4), (4, 9)):
        l = len(d_radial)
        own = radial[l * channels : (l + 1) * channels]
        with_feats = own * gathered
        total = None
        for m in range(low, high):
            blocks = []
            for ref in cot_refs:
                blocks += pieces(ref[m * atoms : (m + 1) * atoms], 2)
            cot = dot_cols(jnp.concatenate(blocks, axis=0).astype(bf16), twice)
            if m:
                d_shapes[m] = jnp.sum(with_feats * cot, axis=0, keepdims=True) * env
                cot = cot * shapes[m]
            total = cot if total is None else total + cot
        d_radial.append(total * gathered)
        own = own * total
        through = own if through is None else through + own
    to_env = jnp.sum(through * gathered, axis=0, keepdims=True)
    through = through * env
    d_hidden = dot(back, jnp.concatenate(
        [p.astype(bf16) for p in pieces(jnp.concatenate(d_radial, axis=0), 2)], axis=0
    ))
    d_before = (d_hidden[0:hidden] + d_hidden[hidden:]) * (d_act * env)
    to_basis = dot(last, thrice(d_before))
    d_dist = jnp.sum(to_basis * d_basis, axis=0, keepdims=True) + to_env * d_env

    s = d_shapes
    d_x = root3 * s[1] + root15 * (y * s[4] + z * s[7] + x * s[8]) - root5 * x * s[6]
    d_y = root3 * s[2] + root15 * (x * s[4] + z * s[5] - y * s[8]) - root5 * y * s[6]
    d_z = root3 * s[3] + root15 * (y * s[5] + x * s[7]) + 2.0 * root5 * z * s[6]
    d_dist = d_dist - near * (x * d_x + y * d_y + z * d_z)
    grad = jnp.concatenate(
        [near * d_x + x * d_dist, near * d_y + y * d_dist, near * d_z + z * d_dist,
         jnp.zeros((sublanes - 3, slots), f32)], axis=0,
    )
    grad = jnp.concatenate(pieces(grad, 2), axis=0).astype(bf16)
    pos_tgt = dot_rows(grad, tgt_hot)
    through = [p.astype(bf16) for p in pieces(through, 2)]
    sums = []
    for (lanes, _, _), hot in zip(columns, hots):
        pos_src = dot_rows(grad[:, lanes], hot)
        feat_src = dot_rows(hot, through[0][:, lanes]) + dot_rows(hot, through[1][:, lanes])
        sums.append((pos_src[0:8] + pos_src[8:16], feat_src))
    return sums, -(pos_tgt[0:8] + pos_tgt[8:16])


def tiles_kernel(orders, tables, homes, rows_ref, *refs):
    refs = list(refs)
    weights = [refs.pop(0)[...] for _ in range(4)]
    y_ref = refs.pop(0)
    block_refs = [refs.pop(0) for _ in range(1 + max(ref for column in tables for ref, _ in column))]
    cot_refs = [refs.pop(0) for _ in range(3)]
    *outs, near_ref, far_ref, place = refs
    atoms = (cot_refs[0].shape[0] - sublanes) // len(degree)
    block = atoms + sublanes
    own_rows = rows_ref[...]
    chunks = [y_ref[at : at + sublanes] for at in range(block, y_ref.shape[0], sublanes)]
    rows = jnp.concatenate([own_rows, jnp.concatenate(chunks, axis=1).astype(jnp.int32)], axis=1)
    split = own_rows.shape[1]
    columns = []
    for at, column in enumerate(tables):
        views = [block_refs[ref].at[start * block : (start + 1) * block] for ref, start in column]
        for table, ref in enumerate(views):
            place[at, :, table * atoms : (table + 1) * atoms] = ref[atoms:, 0:atoms]
        src_pos = jnp.concatenate(pieces(place[at], 3), axis=0).astype(bf16)
        feats = pieces(jnp.concatenate([ref[0:atoms] for ref in views], axis=0), 2)
        lanes = slice(split, None) if at else slice(0, split)
        columns.append((lanes, src_pos, jnp.concatenate(feats, axis=0).T.astype(bf16)))
    sums, pos_tgt = slot_grads(rows, cot_refs, columns, weights, orders)
    for ref, home in zip(outs, homes):
        for at, (column, table) in enumerate(home):
            pos_src, feat_src = sums[column]
            part = slice(table * atoms, (table + 1) * atoms)
            pos = pos_src[:, part]
            if column == 0 and table == 0:
                pos = pos + pos_tgt[:, 0:atoms]
            ref[at * block : at * block + atoms] = feat_src[part]
            ref[at * block + atoms : (at + 1) * block] = jnp.zeros((sublanes, ref.shape[1]), f32)
            ref[at * block + atoms : (at + 1) * block, 0:atoms] = pos
    for at, ref in ((1, near_ref), (2, far_ref)):
        ref[...] = jnp.zeros(ref.shape, f32)
        ref[0:sublanes, 0:atoms] = pos_tgt[:, at * atoms : (at + 1) * atoms]


def add_kernel(count, *refs):
    total = refs[0][...]
    for ref in refs[1:count]:
        total = total + ref[...]
    rows = total.shape[0] // len(refs[count:])
    for at, ref in enumerate(refs[count:]):
        ref[...] = total[at * rows : (at + 1) * rows]


def sum_kernel(gx_count, *refs):
    gx_refs, gy_refs = refs[:gx_count], refs[gx_count:-2]
    pos_ref, feat_ref = refs[-2:]
    atoms = pos_ref.shape[3]
    feat = gx_refs[0][...]
    for ref in gx_refs[1:]:
        feat = feat + ref[...]
    pos = feat[atoms : atoms + 3, 0:atoms]
    for ref in gy_refs:
        pos = pos + ref[0:3, 0:atoms]
    for axis in range(3):
        pos_ref[0, axis] = pos[axis : axis + 1]
    feat_ref[0, 0] = feat[0:atoms]


vmem = pl.BlockSpec(memory_space=pltpu.VMEM)


def call(kernel, name, out_shape, operands, scratch=(), room=4, us=None):
    return pl.pallas_call(
        kernel,
        out_shape=out_shape,
        in_specs=[vmem] * len(operands),
        out_specs=(vmem,) * len(out_shape),
        scratch_shapes=list(scratch),
        compiler_params=pltpu.CompilerParams(vmem_limit_bytes=room and room * megabyte),
        name=name,
        cost_estimate=us and pl.CostEstimate(
            flops=int(us * 1e9), bytes_accessed=0, transcendentals=0
        ),
    )(*operands)


def local(
    gx_size, gy_size, positions, features, cotangent, nbr_src, nbr_tgt, pair_mask, pair_species,
    w_in, species_emb, w_out,
):
    atoms, channels = features.shape[2:]
    steps, _, pairs = nbr_src.shape[2:]
    orders, hidden = w_in.shape
    slots = steps * pairs
    gx_links, gy_links = links_of(gx_size), links_of(gy_size)
    gx_spots = gx_spots_of(gx_links)
    sources = (len(gx_links) + 1) * atoms
    block = atoms + sublanes
    sds = jax.ShapeDtypeStruct

    by_axis = jnp.transpose(positions, (0, 2, 1, 3))
    lists = [jnp.transpose(x, (0, 2, 3, 1, 4)) for x in (nbr_src, nbr_tgt, pair_mask, pair_species)]
    gx_pack = sds((block, channels), f32)
    y_pack = sds((block + -(-2 * slots // channels) * sublanes, channels), f32)
    gy_pack = sds((len(degree) * atoms + sublanes, channels), f32)
    own, y_own, cot_own = call(
        functools.partial(pack_kernel, gx_spots, gy_links), "pack", (gx_pack, y_pack, gy_pack),
        (by_axis, features, cotangent, *lists), room=None,
    )
    y = gy_links[0].swap(y_own, "gy")
    (two,) = call(
        functools.partial(stack_kernel, block), "stack", (sds((2 * block, channels), f32),),
        (own, y), us=2,
    )
    blocks = [own, y] + [link.swap(two, "gx") for link in gx_links]
    tables = tuple(
        ((at, 0),) + tuple((2 + l, at) for l in range(len(gx_links))) for at in range(2)
    )
    homes = tuple(((0, table), (1, table)) for table in range(len(gx_links) + 1))
    far_links = (gy_links[3], gy_links[2])
    cot_far, cot_near = (link.swap(cot_own, "gy") for link in far_links)

    own_lanes = -(-3 * slots // channels) * channels
    rows, *weights = call(
        functools.partial(prep_kernel, gx_spots, gy_links),
        "prepare",
        (
            sds((sublanes, own_lanes), jnp.int32),
            sds((w_out.shape[1], 3 * hidden), bf16),
            sds((2 * hidden, 2 * w_out.shape[1]), bf16),
            sds((hidden, 3 * (orders + 2 * sublanes)), bf16),
            sds((orders, 3 * hidden), bf16),
        ),
        (*lists, w_in, species_emb, w_out),
    )
    far_pack = sds((channels // 2, channels), f32)
    *sent, near, far = call(
        functools.partial(tiles_kernel, orders, tables, homes), "tiles",
        tuple(sds((len(home) * block, channels), f32) for home in homes) + (far_pack,) * 2,
        (rows, *weights, y, *blocks, cot_own, cot_near, cot_far),
        [pltpu.VMEM((2, sublanes, sources), f32)], 32,
    )
    back_gy = [link.swap(value, "gy") for link, value in zip(far_links, (far, near))]
    came = [link.swap(value, "gx") for link, value in zip(gx_links, sent[1:])]
    own, y = call(
        functools.partial(add_kernel, len(sent)), "add", (gx_pack,) * 2, (sent[0], *came)
    )
    back = [own, gy_links[0].swap(y, "gy")]
    pos, feat = call(
        functools.partial(sum_kernel, len(back)), "sums",
        (sds(by_axis.shape, f32), sds(features.shape, f32)),
        (*back, *back_gy),
    )
    return jnp.transpose(pos, (0, 2, 1, 3)), feat


def solution(mesh):
    split = [P("gx", "gy")] * 7 + [P()] * 3
    return jax.shard_map(
        functools.partial(local, mesh.shape["gx"], mesh.shape["gy"]),
        mesh=mesh,
        in_specs=tuple(split),
        out_specs=(P("gx", "gy"), P("gx", "gy")),
        check_vma=False,
    )
```

time: 30.3 us -> 29.2 us (0.964)
  Pallas kernels: 6.08 us -> 5.24 us
  local copies, waits for them, and re-layouts: 1.43 us -> 0.77 us
  starting transfers between devices: 12.8 us -> 13.2 us
    pallas_call x7 -> x6, Pallas kernels: 6.08 us -> 5.24 us  [call(): pl.pallas_call(kernel, out_shape=out_shape, in_specs=[vmem] * len(operand...]
    unnamed x20, local copies, waits for them, and re-layouts: 1.43 us -> 0.77 us
    ppermute x11 -> x12, starting transfers between devices: 12.8 us -> 13.2 us  [swap(): lax.ppermute(value, axis, [(i, (i + self.delta(i)) % n) for i in range(n)])]
    ppermute x11 -> x12, waiting for transfers between devices: 9.04 us -> 9.02 us  [swap(): lax.ppermute(value, axis, [(i, (i + self.delta(i)) % n) for i in range(n)])]
  transfers between devices with their start and end apart: 11 -> 12, of which waited for: 7 -> 7; matrix products, arithmetic and copies ran while one was open for 0% -> 0% of each run, Pallas kernels for 12% -> 1%
where the time goes in v4:
time: 29.2 us; the launch traced here: 29 us
  starting transfers between devices  13.2 us (45%)
  waiting for transfers between devices  9.02 us (31%)
  Pallas kernels  5.24 us (18%)
  local copies, waits for them, and re-layouts  0.77 us (3%)
  between operations  0.75 us (3%)
    ppermute x12, starting transfers between devices, swap(): lax.ppermute(value, axis, [(i, (i + self.delta(i)) % n) for i in range(n)])  13.2 us
    ppermute x12, waiting for transfers between devices, swap(): lax.ppermute(value, axis, [(i, (i + self.delta(i)) % n) for i in range(n)])  9.02 us
    pallas_call x6, Pallas kernels, call(): pl.pallas_call(kernel, out_shape=out_shape, in_specs=[vmem] * len(operand...  5.24 us
    unnamed x20, local copies, waits for them, and re-layouts  0.77 us
  transfers between devices with their start and end apart: 12, of which 7 were waited for; matrix products, arithmetic and copies ran while one was open for 0% of the time, Pallas kernels for 1%

profile of v4, /device:TPU:0, one launch (start us, length us, event | category | flops | bytes accessed | tf_op | source)
XLA Modules:
  0.0 29.0 jit_solution(5961296578367489376)
XLA Ops:
  0.6 1.8 %pack.1 = (f32[40,128]{1,0:T(8,128)}, f32[64,128]{1,0:T(8,128)}, f32[296,128]{1,0:T(8,128)}) custom-call(f32[1,3,1,32]{3,2,1,0:T(1,128)} %bitcast.14, f32[1,1,32,128]{3,2,1,0:T(8,128)} %feat_ref.1, f32[1,1,32,1152]{3,2,1,0:T(8,128)} %cot_ref.1, s32[1,5,5,1,32]{4,3,2,1,0:T(1,128)} %bitcast.6, s32[1,5,5,1,32]{4,3,2,1,0:T(1,128)} %bitcast.8, ...), custom_call_target="tpu_custom_call" | custom-call | tf_op jit(solution)/shard_map/pack/pallas_call | solution.py:349
  2.4 3.0 %collective-permute-start = (f32[64,128]{1,0:T(8,128)}, f32[64,128]{1,0:T(8,128)S(1)}, u32[]{:S(2)}, u32[]{:S(2)}) collective-permute-start(f32[64,128]{1,0:T(8,128)} %get-tuple-element.25), channel_id=1, source_target_pairs={{0,1},{1,0},{2,3},{3,2},{4,5},{5,4},{6,7},{7,6},{8,9},{9,8},{10,11... | collective-permute-start | bytes 98312 | tf_op jit(solution)/shard_map/ppermute | solution.py:31
  5.4 3.6 %collective-permute-start.5 = (f32[296,128]{1,0:T(8,128)}, f32[296,128]{1,0:T(8,128)S(1)}, u32[]{:S(2)}, u32[]{:S(2)}) collective-permute-start(f32[296,128]{1,0:T(8,128)} %get-tuple-element.27.refs_10_), channel_id=1, source_target_pairs={{0,6},{1,7},{2,4},{3,5},{4,2},{5,3},{6,0},{7,1},{8,14},{9,15},{10,... | collective-permute-start | bytes 454664 | tf_op jit(solution)/shard_map/ppermute | solution.py:31
  9.0 0.0 collective-permute-start.4
  9.0 0.0 collective-permute-done.refs_1_.refs_4_.refs_6_
  9.0 0.7 %copy-done.6 = f32[40,128]{1,0:T(8,128)S(1)} copy-done((f32[40,128]{1,0:T(8,128)S(1)}, f32[40,128]{1,0:T(8,128)}, u32[]{:S(2)}) %copy-start.6) | copy-done | bytes 20504
  9.7 0.0 copy-start.5
  9.7 0.0 copy-start.8
  9.7 0.0 copy-start.9
  9.8 1.6 %collective-permute-start.3 = (f32[80,128]{1,0:T(8,128)S(1)}, f32[80,128]{1,0:T(8,128)S(1)}, u32[]{:S(2)}, u32[]{:S(2)}) collective-permute-start(f32[80,128]{1,0:T(8,128)S(1)} %stack.1), channel_id=1, source_target_pairs={{0,16},{8,24},{16,0},{24,8},{1,17},{9,25},{17,1},{25,9},{2,18},{10... | collective-permute-start | bytes 122888 | tf_op jit(solution)/shard_map/ppermute | solution.py:31
  11.3 0.0 collective-permute-start.2
  11.3 0.6 %collective-permute-start.1 = (f32[80,128]{1,0:T(8,128)S(1)}, f32[80,128]{1,0:T(8,128)S(1)}, u32[]{:S(2)}, u32[]{:S(2)}) collective-permute-start(f32[80,128]{1,0:T(8,128)S(1)} %stack.1), channel_id=1, source_target_pairs={{0,8},{8,0},{16,24},{24,16},{1,9},{9,1},{17,25},{25,17},{2,10},{10... | collective-permute-start | bytes 122888 | tf_op jit(solution)/shard_map/ppermute | solution.py:31
  12.0 0.2 prepare.1
  12.2 1.6 %collective-permute-done.3.refs_9_ = f32[80,128]{1,0:T(8,128)S(1)} collective-permute-done((f32[80,128]{1,0:T(8,128)S(1)}, f32[80,128]{1,0:T(8,128)S(1)}, u32[]{:S(2)}, u32[]{:S(2)}) %collective-permute-start.3) | collective-permute-done | bytes 40992 | tf_op jit(solution)/shard_map/ppermute | solution.py:31
  13.8 0.9 %collective-permute-done.2.refs_8_ = f32[80,128]{1,0:T(8,128)S(1)} collective-permute-done((f32[80,128]{1,0:T(8,128)S(1)}, f32[80,128]{1,0:T(8,128)S(1)}, u32[]{:S(2)}, u32[]{:S(2)}) %collective-permute-start.2) | collective-permute-done | bytes 40992 | tf_op jit(solution)/shard_map/ppermute | solution.py:31
  14.8 0.0 collective-permute-done.1.refs_7_
  14.8 0.0 collective-permute-done.5.refs_12_
  14.8 1.4 %collective-permute-done.4.refs_11_ = f32[296,128]{1,0:T(8,128)S(1)} collective-permute-done((f32[296,128]{1,0:T(8,128)}, f32[296,128]{1,0:T(8,128)S(1)}, u32[]{:S(2)}, u32[]{:S(2)}) %collective-permute-start.4) | collective-permute-done | bytes 151584 | tf_op jit(solution)/shard_map/ppermute | solution.py:31
  16.2 2.7 %tiles.1 = (f32[80,128]{1,0:T(8,128)S(1)}, f32[80,128]{1,0:T(8,128)S(1)}, f32[80,128]{1,0:T(8,128)S(1)}, f32[80,128]{1,0:T(8,128)S(1)}, f32[64,128]{1,0:T(8,128)S(1)}, /*index=5*/f32[64,128]{1,0:T(8,128)S(1)}) custom-call(s32[8,512]{1,0:T(8,128)S(1)} %get-tuple-element.20.rows_ref, bf16[384,96]{1,0:T(8,128)(2,1)S(1)} %get-tuple-element.21.refs_0_, ...), custom_call_target="tpu_custom_call" | custom-call | tf_op jit(solution)/shard_map/tiles/pallas_call | solution.py:349
  18.9 0.1 collective-permute-start.6
  18.9 1.6 %collective-permute-start.7 = (f32[80,128]{1,0:T(8,128)S(1)}, f32[80,128]{1,0:T(8,128)S(1)}, u32[]{:S(2)}, u32[]{:S(2)}) collective-permute-start(f32[80,128]{1,0:T(8,128)S(1)} %get-tuple-element.30), channel_id=1, source_target_pairs={{0,24},{8,16},{16,8},{24,0},{1,25},{9,17},{17,9},{25,1},{2,26},{10... | collective-permute-start | bytes 122888 | tf_op jit(solution)/shard_map/ppermute | solution.py:31
  20.5 0.5 %collective-permute-start.8 = (f32[80,128]{1,0:T(8,128)S(1)}, f32[80,128]{1,0:T(8,128)S(1)}, u32[]{:S(2)}, u32[]{:S(2)}) collective-permute-start(f32[80,128]{1,0:T(8,128)S(1)} %get-tuple-element.31), channel_id=1, source_target_pairs={{0,16},{8,24},{16,0},{24,8},{1,17},{9,25},{17,1},{25,9},{2,18},{10... | collective-permute-start | bytes 122888 | tf_op jit(solution)/shard_map/ppermute | solution.py:31
  21.1 1.7 %collective-permute-start.10 = (f32[64,128]{1,0:T(8,128)S(1)}, f32[64,128]{1,0:T(8,128)S(1)}, u32[]{:S(2)}, u32[]{:S(2)}) collective-permute-start(f32[64,128]{1,0:T(8,128)S(1)} %get-tuple-element.34), channel_id=1, source_target_pairs={{0,6},{1,7},{2,4},{3,5},{4,2},{5,3},{6,0},{7,1},{8,14},{9,15},{10,... | collective-permute-start | bytes 98312 | tf_op jit(solution)/shard_map/ppermute | solution.py:31
  22.7 0.0 collective-permute-start.11
  22.8 0.0 collective-permute-done.6.refs_1_
  22.8 0.0 collective-permute-done.7.refs_2_
  22.8 1.8 %collective-permute-done.8.refs_3_ = f32[80,128]{1,0:T(8,128)S(1)} collective-permute-done((f32[80,128]{1,0:T(8,128)S(1)}, f32[80,128]{1,0:T(8,128)S(1)}, u32[]{:S(2)}, u32[]{:S(2)}) %collective-permute-start.8) | collective-permute-done | bytes 40992 | tf_op jit(solution)/shard_map/ppermute | solution.py:31
  24.6 0.6 %collective-permute-start.9 = (f32[40,128]{1,0:T(8,128)S(1)}, f32[40,128]{1,0:T(8,128)S(1)}, u32[]{:S(2)}, u32[]{:S(2)}) collective-permute-start(f32[40,128]{1,0:T(8,128)S(1)} %get-tuple-element.33), channel_id=1, source_target_pairs={{0,1},{1,0},{2,3},{3,2},{4,5},{5,4},{6,7},{7,6},{8,9},{9,8},{10,11... | collective-permute-start | bytes 61448 | tf_op jit(solution)/shard_map/ppermute | solution.py:31
  25.1 1.8 %collective-permute-done.10.refs_2_ = f32[64,128]{1,0:T(8,128)S(1)} collective-permute-done((f32[64,128]{1,0:T(8,128)S(1)}, f32[64,128]{1,0:T(8,128)S(1)}, u32[]{:S(2)}, u32[]{:S(2)}) %collective-permute-start.10) | collective-permute-done | bytes 32800 | tf_op jit(solution)/shard_map/ppermute | solution.py:31
  26.9 0.1 collective-permute-done.11.refs_3_
  27.0 1.4 %collective-permute-done.9.refs_1_ = f32[40,128]{1,0:T(8,128)S(1)} collective-permute-done((f32[40,128]{1,0:T(8,128)S(1)}, f32[40,128]{1,0:T(8,128)S(1)}, u32[]{:S(2)}, u32[]{:S(2)}) %collective-permute-start.9) | collective-permute-done | bytes 20512 | tf_op jit(solution)/shard_map/ppermute | solution.py:31
  28.4 0.6 %sums.1 = (f32[1,3,1,32]{3,2,1,0:T(1,128)}, f32[1,1,32,128]{3,2,1,0:T(8,128)}) custom-call(f32[40,128]{1,0:T(8,128)S(1)} %get-tuple-element.32.refs_0_, f32[40,128]{1,0:T(8,128)S(1)} %collective-permute-done.9.refs_1_, f32[64,128]{1,0:T(8,128)S(1)} %collective-permute-done.10.refs_2_, f32[64,128]{1,0:T(8,128)S(1)} %collective-permute-done.11.refs_3_), custom_call_target="tpu_custom_call" | custom-call | tf_op jit(solution)/shard_map/sums/pallas_call | solution.py:349
  (18 shorter events, 0.0 us)
Async XLA Ops:
  2.4 6.6 %collective-permute-start = (f32[64,128]{1,0:T(8,128)}, f32[64,128]{1,0:T(8,128)S(1)}, u32[]{:S(2)}, u32[]{:S(2)}) collective-permute-start(f32[64,128]{1,0:T(8,128)} %get-tuple-element.25), channel_id=1, source_target_pairs={{0,1},{1,0},{2,3},{3,2},{4,5},{5,4},{6,7},{7,6},{8,9},{9,8},{10,11... | collective-permute-start | bytes 98312 | tf_op jit(solution)/shard_map/ppermute | solution.py:31
  5.4 9.4 %collective-permute-start.5 = (f32[296,128]{1,0:T(8,128)}, f32[296,128]{1,0:T(8,128)S(1)}, u32[]{:S(2)}, u32[]{:S(2)}) collective-permute-start(f32[296,128]{1,0:T(8,128)} %get-tuple-element.27.refs_10_), channel_id=1, source_target_pairs={{0,6},{1,7},{2,4},{3,5},{4,2},{5,3},{6,0},{7,1},{8,14},{9,15},{10,... | collective-permute-start | bytes 454664 | tf_op jit(solution)/shard_map/ppermute | solution.py:31
  9.0 7.2 %collective-permute-start.4 = (f32[296,128]{1,0:T(8,128)}, f32[296,128]{1,0:T(8,128)S(1)}, u32[]{:S(2)}, u32[]{:S(2)}) collective-permute-start(f32[296,128]{1,0:T(8,128)} %get-tuple-element.27.refs_10_), channel_id=1, source_target_pairs={{0,2},{1,3},{2,0},{3,1},{4,6},{5,7},{6,4},{7,5},{8,10},{9,11},{10,... | collective-permute-start | bytes 454664 | tf_op jit(solution)/shard_map/ppermute | solution.py:31
  9.0 0.7 %copy-start.6 = (f32[40,128]{1,0:T(8,128)S(1)}, f32[40,128]{1,0:T(8,128)}, u32[]{:S(2)}) copy-start(f32[40,128]{1,0:T(8,128)} %get-tuple-element.26.refs_0_.refs_5_) | copy-start | bytes 61444
  9.7 2.3 %copy-start.1 = (s32[1,1,5,5,32]{4,1,3,2,0:T(1,128)S(1)}, s32[1,1,5,5,32]{4,1,3,2,0:T(1,128)}, u32[]{:S(2)}) copy-start(s32[1,1,5,5,32]{4,1,3,2,0:T(1,128)} %param.13) | copy-start | bytes 9604
  9.7 2.3 %copy-start.2 = (s32[1,1,5,5,32]{4,1,3,2,0:T(1,128)S(1)}, s32[1,1,5,5,32]{4,1,3,2,0:T(1,128)}, u32[]{:S(2)}) copy-start(s32[1,1,5,5,32]{4,1,3,2,0:T(1,128)} %param.14) | copy-start | bytes 9604
  9.7 2.3 %copy-start.3 = (s32[1,1,5,5,32]{4,1,3,2,0:T(1,128)S(1)}, s32[1,1,5,5,32]{4,1,3,2,0:T(1,128)}, u32[]{:S(2)}) copy-start(s32[1,1,5,5,32]{4,1,3,2,0:T(1,128)} %param.15) | copy-start | bytes 9604
  9.7 2.3 %copy-start.4 = (s32[1,1,5,5,32]{4,1,3,2,0:T(1,128)S(1)}, s32[1,1,5,5,32]{4,1,3,2,0:T(1,128)}, u32[]{:S(2)}) copy-start(s32[1,1,5,5,32]{4,1,3,2,0:T(1,128)} %param.16) | copy-start | bytes 9604
  9.7 2.3 %copy-start.5 = (f32[32,384]{1,0:T(8,128)S(1)}, f32[32,384]{1,0:T(8,128)}, u32[]{:S(2)}) copy-start(f32[32,384]{1,0:T(8,128)} %out_ref.1) | copy-start | bytes 147460
  9.7 2.3 %copy-start.8 = (f32[10,32]{1,0:T(8,128)S(1)}, f32[10,32]{1,0:T(8,128)}, u32[]{:S(2)}) copy-start(f32[10,32]{1,0:T(8,128)} %emb_ref.1) | copy-start | bytes 3844
  9.7 2.3 %copy-start.9 = (f32[8,32]{1,0:T(8,128)S(1)}, f32[8,32]{1,0:T(8,128)}, u32[]{:S(2)}) copy-start(f32[8,32]{1,0:T(8,128)} %in_ref.1) | copy-start | bytes 3076
  9.7 6.4 %copy-start = (f32[296,128]{1,0:T(8,128)S(1)}, f32[296,128]{1,0:T(8,128)}, u32[]{:S(2)}) copy-start(f32[296,128]{1,0:T(8,128)} %get-tuple-element.27.refs_10_) | copy-start | bytes 454660
  9.8 4.1 %collective-permute-start.3 = (f32[80,128]{1,0:T(8,128)S(1)}, f32[80,128]{1,0:T(8,128)S(1)}, u32[]{:S(2)}, u32[]{:S(2)}) collective-permute-start(f32[80,128]{1,0:T(8,128)S(1)} %stack.1), channel_id=1, source_target_pairs={{0,16},{8,24},{16,0},{24,8},{1,17},{9,25},{17,1},{25,9},{2,18},{10... | collective-permute-start | bytes 122888 | tf_op jit(solution)/shard_map/ppermute | solution.py:31
  11.3 3.4 %collective-permute-start.2 = (f32[80,128]{1,0:T(8,128)S(1)}, f32[80,128]{1,0:T(8,128)S(1)}, u32[]{:S(2)}, u32[]{:S(2)}) collective-permute-start(f32[80,128]{1,0:T(8,128)S(1)} %stack.1), channel_id=1, source_target_pairs={{0,24},{8,16},{16,8},{24,0},{1,25},{9,17},{17,9},{25,1},{2,26},{10... | collective-permute-start | bytes 122888 | tf_op jit(solution)/shard_map/ppermute | solution.py:31
  11.3 3.4 %collective-permute-start.1 = (f32[80,128]{1,0:T(8,128)S(1)}, f32[80,128]{1,0:T(8,128)S(1)}, u32[]{:S(2)}, u32[]{:S(2)}) collective-permute-start(f32[80,128]{1,0:T(8,128)S(1)} %stack.1), channel_id=1, source_target_pairs={{0,8},{8,0},{16,24},{24,16},{1,9},{9,1},{17,25},{25,17},{2,10},{10... | collective-permute-start | bytes 122888 | tf_op jit(solution)/shard_map/ppermute | solution.py:31
  12.0 4.2 %copy-start.7 = (f32[40,128]{1,0:T(8,128)S(1)}, f32[40,128]{1,0:T(8,128)}, u32[]{:S(2)}) copy-start(f32[40,128]{1,0:T(8,128)} %get-tuple-element.26.refs_0_.refs_5_) | copy-start | bytes 61444
  18.9 3.9 %collective-permute-start.6 = (f32[80,128]{1,0:T(8,128)S(1)}, f32[80,128]{1,0:T(8,128)S(1)}, u32[]{:S(2)}, u32[]{:S(2)}) collective-permute-start(f32[80,128]{1,0:T(8,128)S(1)} %get-tuple-element.29), channel_id=1, source_target_pairs={{0,8},{8,0},{16,24},{24,16},{1,9},{9,1},{17,25},{25,17},{2,10},{10... | collective-permute-start | bytes 122888 | tf_op jit(solution)/shard_map/ppermute | solution.py:31
  18.9 3.8 %collective-permute-start.7 = (f32[80,128]{1,0:T(8,128)S(1)}, f32[80,128]{1,0:T(8,128)S(1)}, u32[]{:S(2)}, u32[]{:S(2)}) collective-permute-start(f32[80,128]{1,0:T(8,128)S(1)} %get-tuple-element.30), channel_id=1, source_target_pairs={{0,24},{8,16},{16,8},{24,0},{1,25},{9,17},{17,9},{25,1},{2,26},{10... | collective-permute-start | bytes 122888 | tf_op jit(solution)/shard_map/ppermute | solution.py:31
  20.5 4.0 %collective-permute-start.8 = (f32[80,128]{1,0:T(8,128)S(1)}, f32[80,128]{1,0:T(8,128)S(1)}, u32[]{:S(2)}, u32[]{:S(2)}) collective-permute-start(f32[80,128]{1,0:T(8,128)S(1)} %get-tuple-element.31), channel_id=1, source_target_pairs={{0,16},{8,24},{16,0},{24,8},{1,17},{9,25},{17,1},{25,9},{2,18},{10... | collective-permute-start | bytes 122888 | tf_op jit(solution)/shard_map/ppermute | solution.py:31
  21.1 5.8 %collective-permute-start.10 = (f32[64,128]{1,0:T(8,128)S(1)}, f32[64,128]{1,0:T(8,128)S(1)}, u32[]{:S(2)}, u32[]{:S(2)}) collective-permute-start(f32[64,128]{1,0:T(8,128)S(1)} %get-tuple-element.34), channel_id=1, source_target_pairs={{0,6},{1,7},{2,4},{3,5},{4,2},{5,3},{6,0},{7,1},{8,14},{9,15},{10,... | collective-permute-start | bytes 98312 | tf_op jit(solution)/shard_map/ppermute | solution.py:31
  22.7 4.3 %collective-permute-start.11 = (f32[64,128]{1,0:T(8,128)S(1)}, f32[64,128]{1,0:T(8,128)S(1)}, u32[]{:S(2)}, u32[]{:S(2)}) collective-permute-start(f32[64,128]{1,0:T(8,128)S(1)} %get-tuple-element.35), channel_id=1, source_target_pairs={{0,2},{1,3},{2,0},{3,1},{4,6},{5,7},{6,4},{7,5},{8,10},{9,11},{10,... | collective-permute-start | bytes 98312 | tf_op jit(solution)/shard_map/ppermute | solution.py:31
  24.6 3.8 %collective-permute-start.9 = (f32[40,128]{1,0:T(8,128)S(1)}, f32[40,128]{1,0:T(8,128)S(1)}, u32[]{:S(2)}, u32[]{:S(2)}) collective-permute-start(f32[40,128]{1,0:T(8,128)S(1)} %get-tuple-element.33), channel_id=1, source_target_pairs={{0,1},{1,0},{2,3},{3,2},{4,5},{5,4},{6,7},{7,6},{8,9},{9,8},{10,11... | collective-permute-start | bytes 61448 | tf_op jit(solution)/shard_map/ppermute | solution.py:31

commit v5 on v4

--- a/solution.py
+++ b/solution.py
@@ -113,31 +113,33 @@
     near, other = gy_links[0].delta(at_y), gy_links[1].delta(at_y)
     partner = at_y + near
     to_far = (partner + (partner >> 1)) & 1
+    lanes = -(-len(gx_spots) * pairs // channels) * channels
     write_rows(store, gx_spots, at_x, lists, near, 0, 0)
-    write_rows(store, gx_spots, at_x, lists, other, 1 + to_far, len(gx_spots) * pairs)
+    write_rows(store, gx_spots, at_x, lists, other, to_far, lanes)
 
 
 def stack_kernel(rows, *refs):
-    *refs, out_ref = refs
+    *refs, _, out_ref = refs
     for at, ref in enumerate(refs):
         out_ref[at * rows : (at + 1) * rows] = ref[0:rows]
 
 
 def prep_kernel(
     gx_spots, gy_links, src_ref, tgt_ref, mask_ref, spec_ref, in_ref, emb_ref, out_ref,
-    rows_ref, wide_ref, back_ref, first_ref, last_ref,
+    early_ref, late_ref, wide_ref, back_ref, first_ref, last_ref,
 ):
     pairs = src_ref.shape[4]
-    rows_ref[...] = jnp.zeros(rows_ref.shape, jnp.int32)
-
-    def store(row, lane, value):
-        rows_ref[row : row + 1, lane : lane + pairs] = value
-
     at_x, at_y = lax.axis_index("gx"), lax.axis_index("gy")
     lists = (src_ref, tgt_ref, mask_ref, spec_ref)
-    for place, link in enumerate((None, gy_links[2], gy_links[3])):
-        step_y = 0 if link is None else link.delta(at_y)
-        write_rows(store, gx_spots, at_x, lists, step_y, place, place * len(gx_spots) * pairs)
+    for rows_ref, links in ((early_ref, (None,)), (late_ref, (gy_links[2], gy_links[3]))):
+        rows_ref[...] = jnp.zeros(rows_ref.shape, jnp.int32)
+
+        def store(row, lane, value, rows_ref=rows_ref):
+            rows_ref[row : row + 1, lane : lane + pairs] = value
+
+        for place, link in enumerate(links):
+            step_y = 0 if link is None else link.delta(at_y)
+            write_rows(store, gx_spots, at_x, lists, step_y, place, place * len(gx_spots) * pairs)
     high, low = pieces(out_ref[...], 2)
     wide_ref[...] = jnp.concatenate([high, high, low], axis=0).T.astype(bf16)
     upper = jnp.concatenate([high, high], axis=1)
@@ -280,19 +282,25 @@
     return sums, -(pos_tgt[0:8] + pos_tgt[8:16])
 
 
-def tiles_kernel(orders, tables, homes, rows_ref, *refs):
+def all_rows(rows_ref, y_ref, block, late):
+    own = rows_ref[...]
+    count = (y_ref.shape[0] - block) // (2 * sublanes)
+    start = block + late * count * sublanes
+    chunks = [y_ref[start + at * sublanes : start + (at + 1) * sublanes] for at in range(count)]
+    rows = jnp.concatenate([own, jnp.concatenate(chunks, axis=1).astype(jnp.int32)], axis=1)
+    return rows, (slice(0, own.shape[1]), slice(own.shape[1], None))
+
+
+def early_kernel(orders, tables, rows_ref, *refs):
     refs = list(refs)
     weights = [refs.pop(0)[...] for _ in range(4)]
     y_ref = refs.pop(0)
     block_refs = [refs.pop(0) for _ in range(1 + max(ref for column in tables for ref, _ in column))]
-    cot_refs = [refs.pop(0) for _ in range(3)]
-    *outs, near_ref, far_ref, place = refs
-    atoms = (cot_refs[0].shape[0] - sublanes) // len(degree)
+    cot_ref = refs.pop(0)
+    *outs, place = refs
+    atoms = (cot_ref.shape[0] - sublanes) // len(degree)
     block = atoms + sublanes
-    own_rows = rows_ref[...]
-    chunks = [y_ref[at : at + sublanes] for at in range(block, y_ref.shape[0], sublanes)]
-    rows = jnp.concatenate([own_rows, jnp.concatenate(chunks, axis=1).astype(jnp.int32)], axis=1)
-    split = own_rows.shape[1]
+    rows, lanes = all_rows(rows_ref, y_ref, block, 0)
     columns = []
     for at, column in enumerate(tables):
         views = [block_refs[ref].at[start * block : (start + 1) * block] for ref, start in column]
@@ -300,20 +308,41 @@
             place[at, :, table * atoms : (table + 1) * atoms] = ref[atoms:, 0:atoms]
         src_pos = jnp.concatenate(pieces(place[at], 3), axis=0).astype(bf16)
         feats = pieces(jnp.concatenate([ref[0:atoms] for ref in views], axis=0), 2)
-        lanes = slice(split, None) if at else slice(0, split)
-        columns.append((lanes, src_pos, jnp.concatenate(feats, axis=0).T.astype(bf16)))
+        feats = jnp.concatenate(feats, axis=0).T.astype(bf16)
+        outs[4 * at][...] = src_pos
+        outs[4 * at + 1][...] = feats
+        columns.append((lanes[at], src_pos, feats))
+    sums, pos_tgt = slot_grads(rows, [cot_ref], columns, weights, orders)
+    for at, (pos, feat) in enumerate(sums):
+        outs[4 * at + 2][...] = pos
+        outs[4 * at + 3][...] = feat
+    outs[2][:, 0:atoms] = sums[0][0][:, 0:atoms] + pos_tgt
+
+
+def late_kernel(orders, homes, rows_ref, *refs):
+    refs = list(refs)
+    weights = [refs.pop(0)[...] for _ in range(4)]
+    y_ref = refs.pop(0)
+    held = [refs.pop(0) for _ in range(8)]
+    cot_refs = [refs.pop(0) for _ in range(2)]
+    *outs, near_ref, far_ref = refs
+    atoms = (cot_refs[0].shape[0] - sublanes) // len(degree)
+    block = atoms + sublanes
+    rows, lanes = all_rows(rows_ref, y_ref, block, 1)
+    columns = [(lanes[at], held[4 * at][...], held[4 * at + 1][...]) for at in range(2)]
     sums, pos_tgt = slot_grads(rows, cot_refs, columns, weights, orders)
+    sums = [
+        (pos + held[4 * at + 2][...], feat + held[4 * at + 3][...])
+        for at, (pos, feat) in enumerate(sums)
+    ]
     for ref, home in zip(outs, homes):
         for at, (column, table) in enumerate(home):
-            pos_src, feat_src = sums[column]
+            pos, feat = sums[column]
             part = slice(table * atoms, (table + 1) * atoms)
-            pos = pos_src[:, part]
-            if column == 0 and table == 0:
-                pos = pos + pos_tgt[:, 0:atoms]
-            ref[at * block : at * block + atoms] = feat_src[part]
+            ref[at * block : at * block + atoms] = feat[part]
             ref[at * block + atoms : (at + 1) * block] = jnp.zeros((sublanes, ref.shape[1]), f32)
-            ref[at * block + atoms : (at + 1) * block, 0:atoms] = pos
-    for at, ref in ((1, near_ref), (2, far_ref)):
+            ref[at * block + atoms : (at + 1) * block, 0:atoms] = pos[:, part]
+    for at, ref in enumerate((near_ref, far_ref)):
         ref[...] = jnp.zeros(ref.shape, f32)
         ref[0:sublanes, 0:atoms] = pos_tgt[:, at * atoms : (at + 1) * atoms]
 
@@ -377,44 +406,51 @@
     by_axis = jnp.transpose(positions, (0, 2, 1, 3))
     lists = [jnp.transpose(x, (0, 2, 3, 1, 4)) for x in (nbr_src, nbr_tgt, pair_mask, pair_species)]
     gx_pack = sds((block, channels), f32)
-    y_pack = sds((block + -(-2 * slots // channels) * sublanes, channels), f32)
+    y_pack = sds((block + 2 * -(-slots // channels) * sublanes, channels), f32)
     gy_pack = sds((len(degree) * atoms + sublanes, channels), f32)
     own, y_own, cot_own = call(
         functools.partial(pack_kernel, gx_spots, gy_links), "pack", (gx_pack, y_pack, gy_pack),
         (by_axis, features, cotangent, *lists), room=None,
     )
+    far_links = (gy_links[3], gy_links[2])
     y = gy_links[0].swap(y_own, "gy")
-    (two,) = call(
-        functools.partial(stack_kernel, block), "stack", (sds((2 * block, channels), f32),),
-        (own, y), us=2,
-    )
-    blocks = [own, y] + [link.swap(two, "gx") for link in gx_links]
     tables = tuple(
         ((at, 0),) + tuple((2 + l, at) for l in range(len(gx_links))) for at in range(2)
     )
     homes = tuple(((0, table), (1, table)) for table in range(len(gx_links) + 1))
-    far_links = (gy_links[3], gy_links[2])
-    cot_far, cot_near = (link.swap(cot_own, "gy") for link in far_links)
-
-    own_lanes = -(-3 * slots // channels) * channels
-    rows, *weights = call(
+
+    early_rows, late_rows, *weights = call(
         functools.partial(prep_kernel, gx_spots, gy_links),
         "prepare",
         (
-            sds((sublanes, own_lanes), jnp.int32),
+            *(sds((sublanes, -(-n * slots // channels) * channels), jnp.int32) for n in (1, 2)),
             sds((w_out.shape[1], 3 * hidden), bf16),
             sds((2 * hidden, 2 * w_out.shape[1]), bf16),
             sds((hidden, 3 * (orders + 2 * sublanes)), bf16),
             sds((orders, 3 * hidden), bf16),
         ),
-        (*lists, w_in, species_emb, w_out),
+        (*lists, w_in, species_emb, w_out), us=3,
+    )
+    late_cot = lax.optimization_barrier((cot_own, weights[-1]))[0]
+    cot_far, cot_near = (link.swap(late_cot, "gy") for link in far_links)
+    (two,) = call(
+        functools.partial(stack_kernel, block), "stack", (sds((2 * block, channels), f32),),
+        (own, y, weights[-1]), us=2,
+    )
+    blocks = [own, y] + [link.swap(two, "gx") for link in gx_links]
+    column = (
+        sds((3 * sublanes, sources), bf16), sds((channels, 2 * sources), bf16),
+        sds((sublanes, sources), f32), sds((sources, channels), f32),
+    )
+    held = call(
+        functools.partial(early_kernel, orders, tables), "early_tiles", column * 2,
+        (early_rows, *weights, y, *blocks, cot_own), [pltpu.VMEM((2, sublanes, sources), f32)], 24,
     )
     far_pack = sds((channels // 2, channels), f32)
     *sent, near, far = call(
-        functools.partial(tiles_kernel, orders, tables, homes), "tiles",
+        functools.partial(late_kernel, orders, homes), "late_tiles",
         tuple(sds((len(home) * block, channels), f32) for home in homes) + (far_pack,) * 2,
-        (rows, *weights, y, *blocks, cot_own, cot_near, cot_far),
-        [pltpu.VMEM((2, sublanes, sources), f32)], 32,
+        (late_rows, *weights, y, *held, cot_near, cot_far), room=24,
     )
     back_gy = [link.swap(value, "gy") for link, value in zip(far_links, (far, near))]
     came = [link.swap(value, "gx") for link, value in zip(gx_links, sent[1:])]

time: 29.2 us -> 28.8 us (0.986)
  waiting for transfers between devices: 9.02 us -> 7.16 us
  Pallas kernels: 5.24 us -> 6.55 us
  starting transfers between devices: 13.2 us -> 14.1 us
  local copies, waits for them, and re-layouts: 0.77 us -> 0.04 us
    ppermute x12, waiting for transfers between devices: 9.02 us -> 7.16 us  [swap(): lax.ppermute(value, axis, [(i, (i + self.delta(i)) % n) for i in range(n)])]
    pallas_call x6 -> x7, Pallas kernels: 5.24 us -> 6.55 us  [call(): pl.pallas_call(kernel, out_shape=out_shape, in_specs=[vmem] * len(operand...]
    ppermute x12, starting transfers between devices: 13.2 us -> 14.1 us  [swap(): lax.ppermute(value, axis, [(i, (i + self.delta(i)) % n) for i in range(n)])]
    unnamed x20 -> x18, local copies, waits for them, and re-layouts: 0.77 us -> 0.04 us
  transfers between devices with their start and end apart: 12 -> 12, of which waited for: 7 -> 7; matrix products, arithmetic and copies ran while one was open for 0% -> 0% of each run, Pallas kernels for 1% -> 7%
where the time goes in v5:
time: 28.8 us; the launch traced here: 28.7 us
  starting transfers between devices  14.1 us (49%)
  waiting for transfers between devices  7.16 us (25%)
  Pallas kernels  6.55 us (23%)
  between operations  0.79 us (3%)
    ppermute x12, starting transfers between devices, swap(): lax.ppermute(value, axis, [(i, (i + self.delta(i)) % n) for i in range(n)])  14.1 us
    ppermute x12, waiting for transfers between devices, swap(): lax.ppermute(value, axis, [(i, (i + self.delta(i)) % n) for i in range(n)])  7.16 us
    pallas_call x7, Pallas kernels, call(): pl.pallas_call(kernel, out_shape=out_shape, in_specs=[vmem] * len(operand...  6.55 us
  transfers between devices with their start and end apart: 12, of which 7 were waited for; matrix products, arithmetic and copies ran while one was open for 0% of the time, Pallas kernels for 7%

profile of v5, /device:TPU:0, one launch (start us, length us, event | category | flops | bytes accessed | tf_op | source)
XLA Modules:
  0.0 28.7 jit_solution(12393942769401336227)
XLA Ops:
  0.6 0.0 copy-start.2
  0.6 0.0 copy-start.3
  0.7 0.0 copy-start.4
  0.7 1.8 %pack.1 = (f32[40,128]{1,0:T(8,128)}, f32[72,128]{1,0:T(8,128)}, f32[296,128]{1,0:T(8,128)}) custom-call(f32[1,3,1,32]{3,2,1,0:T(1,128)} %bitcast.14, f32[1,1,32,128]{3,2,1,0:T(8,128)} %feat_ref.1, f32[1,1,32,1152]{3,2,1,0:T(8,128)} %cot_ref.1, s32[1,5,5,1,32]{4,3,2,1,0:T(1,128)} %bitcast.6, s32[1,5,5,1,32]{4,3,2,1,0:T(1,128)} %bitcast.8, ...), custom_call_target="tpu_custom_call" | custom-call | tf_op jit(solution)/shard_map/pack/pallas_call | solution.py:378
  2.5 3.0 %collective-permute-start = (f32[72,128]{1,0:T(8,128)}, f32[72,128]{1,0:T(8,128)S(1)}, u32[]{:S(2)}, u32[]{:S(2)}) collective-permute-start(f32[72,128]{1,0:T(8,128)} %get-tuple-element.35), channel_id=1, source_target_pairs={{0,1},{1,0},{2,3},{3,2},{4,5},{5,4},{6,7},{7,6},{8,9},{9,8},{10,11... | collective-permute-start | bytes 110600 | tf_op jit(solution)/shard_map/ppermute | solution.py:31
  5.5 0.2 prepare.1
  5.7 3.7 %collective-permute-start.5 = (f32[296,128]{1,0:T(8,128)S(1)}, f32[296,128]{1,0:T(8,128)S(1)}, u32[]{:S(2)}, u32[]{:S(2)}) collective-permute-start(f32[296,128]{1,0:T(8,128)S(1)} %copy-done), channel_id=1, source_target_pairs={{0,6},{1,7},{2,4},{3,5},{4,2},{5,3},{6,0},{7,1},{8,14},{9,15},{10,... | collective-permute-start | bytes 454664 | tf_op jit(solution)/shard_map/ppermute | solution.py:31
  9.4 0.0 collective-permute-start.4
  9.4 0.0 collective-permute-done.refs_1_.refs_4_.refs_6_
  9.4 1.6 %collective-permute-start.3 = (f32[80,128]{1,0:T(8,128)S(1)}, f32[80,128]{1,0:T(8,128)S(1)}, u32[]{:S(2)}, u32[]{:S(2)}) collective-permute-start(f32[80,128]{1,0:T(8,128)S(1)} %stack.1), channel_id=1, source_target_pairs={{0,16},{8,24},{16,0},{24,8},{1,17},{9,25},{17,1},{25,9},{2,18},{10... | collective-permute-start | bytes 122888 | tf_op jit(solution)/shard_map/ppermute | solution.py:31
  11.0 0.0 collective-permute-start.2
  11.0 0.6 %collective-permute-start.1 = (f32[80,128]{1,0:T(8,128)S(1)}, f32[80,128]{1,0:T(8,128)S(1)}, u32[]{:S(2)}, u32[]{:S(2)}) collective-permute-start(f32[80,128]{1,0:T(8,128)S(1)} %stack.1), channel_id=1, source_target_pairs={{0,8},{8,0},{16,24},{24,16},{1,9},{9,1},{17,25},{25,17},{2,10},{10... | collective-permute-start | bytes 122888 | tf_op jit(solution)/shard_map/ppermute | solution.py:31
  11.6 1.9 %collective-permute-done.3.refs_9_ = f32[80,128]{1,0:T(8,128)S(1)} collective-permute-done((f32[80,128]{1,0:T(8,128)S(1)}, f32[80,128]{1,0:T(8,128)S(1)}, u32[]{:S(2)}, u32[]{:S(2)}) %collective-permute-start.3) | collective-permute-done | bytes 40992 | tf_op jit(solution)/shard_map/ppermute | solution.py:31
  13.5 0.9 %collective-permute-done.2.refs_8_ = f32[80,128]{1,0:T(8,128)S(1)} collective-permute-done((f32[80,128]{1,0:T(8,128)S(1)}, f32[80,128]{1,0:T(8,128)S(1)}, u32[]{:S(2)}, u32[]{:S(2)}) %collective-permute-start.2) | collective-permute-done | bytes 40992 | tf_op jit(solution)/shard_map/ppermute | solution.py:31
  14.4 0.0 collective-permute-done.1.refs_7_
  14.4 1.8 %early_tiles.1 = (bf16[24,128]{1,0:T(8,128)(2,1)S(1)}, bf16[128,256]{1,0:T(8,128)(2,1)S(1)}, f32[8,128]{1,0:T(8,128)S(1)}, f32[128,128]{1,0:T(8,128)S(1)}, bf16[...) custom-call(s32[8,256]{1,0:T(8,128)S(1)} %get-tuple-element.36.rows_ref, ...), custom_call_target="tpu_custom_call" | custom-call | tf_op jit(solution)/shard_map/early_tiles/pallas_call | solution.py:378
  16.2 0.0 collective-permute-done.5.refs_14_
  16.2 0.2 collective-permute-done.4.refs_13_
  16.4 2.1 %late_tiles.1 = (f32[80,128]{1,0:T(8,128)S(1)}, f32[80,128]{1,0:T(8,128)S(1)}, f32[80,128]{1,0:T(8,128)S(1)}, f32[80,128]{1,0:T(8,128)S(1)}, f32[64,128]{1,0:T(8,128)S(1)}, /*index=5*/f32[64,128]{1,0:T(8,128)S(1)}) custom-call(s32[8,384]{1,0:T(8,128)S(1)} %get-tuple-element.30.rows_ref, bf16[384,96]{1,0:T(8,128)(2,1)S(1)} %get-tuple-element.31.refs_0_, ...), custom_call_target="tpu_custom_call" | custom-call | tf_op jit(solution)/shard_map/late_tiles/pallas_call | solution.py:378
  18.5 0.1 collective-permute-start.6
  18.6 1.6 %collective-permute-start.7 = (f32[80,128]{1,0:T(8,128)S(1)}, f32[80,128]{1,0:T(8,128)S(1)}, u32[]{:S(2)}, u32[]{:S(2)}) collective-permute-start(f32[80,128]{1,0:T(8,128)S(1)} %get-tuple-element.50), channel_id=1, source_target_pairs={{0,24},{8,16},{16,8},{24,0},{1,25},{9,17},{17,9},{25,1},{2,26},{10... | collective-permute-start | bytes 122888 | tf_op jit(solution)/shard_map/ppermute | solution.py:31
  20.2 0.5 %collective-permute-start.8 = (f32[80,128]{1,0:T(8,128)S(1)}, f32[80,128]{1,0:T(8,128)S(1)}, u32[]{:S(2)}, u32[]{:S(2)}) collective-permute-start(f32[80,128]{1,0:T(8,128)S(1)} %get-tuple-element.51), channel_id=1, source_target_pairs={{0,16},{8,24},{16,0},{24,8},{1,17},{9,25},{17,1},{25,9},{2,18},{10... | collective-permute-start | bytes 122888 | tf_op jit(solution)/shard_map/ppermute | solution.py:31
  20.7 2.1 %collective-permute-start.10 = (f32[64,128]{1,0:T(8,128)S(1)}, f32[64,128]{1,0:T(8,128)S(1)}, u32[]{:S(2)}, u32[]{:S(2)}) collective-permute-start(f32[64,128]{1,0:T(8,128)S(1)} %get-tuple-element.54), channel_id=1, source_target_pairs={{0,6},{1,7},{2,4},{3,5},{4,2},{5,3},{6,0},{7,1},{8,14},{9,15},{10,... | collective-permute-start | bytes 98312 | tf_op jit(solution)/shard_map/ppermute | solution.py:31
  22.9 0.0 collective-permute-start.11
  22.9 0.0 collective-permute-done.6.refs_1_
  22.9 0.0 collective-permute-done.7.refs_2_
  22.9 1.3 %collective-permute-done.8.refs_3_ = f32[80,128]{1,0:T(8,128)S(1)} collective-permute-done((f32[80,128]{1,0:T(8,128)S(1)}, f32[80,128]{1,0:T(8,128)S(1)}, u32[]{:S(2)}, u32[]{:S(2)}) %collective-permute-start.8) | collective-permute-done | bytes 40992 | tf_op jit(solution)/shard_map/ppermute | solution.py:31
  24.2 1.0 %collective-permute-start.9 = (f32[40,128]{1,0:T(8,128)S(1)}, f32[40,128]{1,0:T(8,128)S(1)}, u32[]{:S(2)}, u32[]{:S(2)}) collective-permute-start(f32[40,128]{1,0:T(8,128)S(1)} %get-tuple-element.53), channel_id=1, source_target_pairs={{0,1},{1,0},{2,3},{3,2},{4,5},{5,4},{6,7},{7,6},{8,9},{9,8},{10,11... | collective-permute-start | bytes 61448 | tf_op jit(solution)/shard_map/ppermute | solution.py:31
  25.2 1.3 %collective-permute-done.10.refs_2_ = f32[64,128]{1,0:T(8,128)S(1)} collective-permute-done((f32[64,128]{1,0:T(8,128)S(1)}, f32[64,128]{1,0:T(8,128)S(1)}, u32[]{:S(2)}, u32[]{:S(2)}) %collective-permute-start.10) | collective-permute-done | bytes 32800 | tf_op jit(solution)/shard_map/ppermute | solution.py:31
  26.4 0.4 %collective-permute-done.11.refs_3_ = f32[64,128]{1,0:T(8,128)S(1)} collective-permute-done((f32[64,128]{1,0:T(8,128)S(1)}, f32[64,128]{1,0:T(8,128)S(1)}, u32[]{:S(2)}, u32[]{:S(2)}) %collective-permute-start.11) | collective-permute-done | bytes 32800 | tf_op jit(solution)/shard_map/ppermute | solution.py:31
  26.8 1.3 %collective-permute-done.9.refs_1_ = f32[40,128]{1,0:T(8,128)S(1)} collective-permute-done((f32[40,128]{1,0:T(8,128)S(1)}, f32[40,128]{1,0:T(8,128)S(1)}, u32[]{:S(2)}, u32[]{:S(2)}) %collective-permute-start.9) | collective-permute-done | bytes 20512 | tf_op jit(solution)/shard_map/ppermute | solution.py:31
  28.1 0.6 %sums.1 = (f32[1,3,1,32]{3,2,1,0:T(1,128)}, f32[1,1,32,128]{3,2,1,0:T(8,128)}) custom-call(f32[40,128]{1,0:T(8,128)S(1)} %get-tuple-element.52.refs_0_, f32[40,128]{1,0:T(8,128)S(1)} %collective-permute-done.9.refs_1_, f32[64,128]{1,0:T(8,128)S(1)} %collective-permute-done.10.refs_2_, f32[64,128]{1,0:T(8,128)S(1)} %collective-permute-done.11.refs_3_), custom_call_target="tpu_custom_call" | custom-call | tf_op jit(solution)/shard_map/sums/pallas_call | solution.py:378
  (17 shorter events, 0.0 us)
Async XLA Ops:
  0.6 4.8 %copy-start.2 = (s32[1,1,5,5,32]{4,1,3,2,0:T(1,128)S(1)}, s32[1,1,5,5,32]{4,1,3,2,0:T(1,128)}, u32[]{:S(2)}) copy-start(s32[1,1,5,5,32]{4,1,3,2,0:T(1,128)} %param.13) | copy-start | bytes 9604
  0.6 4.8 %copy-start.3 = (s32[1,1,5,5,32]{4,1,3,2,0:T(1,128)S(1)}, s32[1,1,5,5,32]{4,1,3,2,0:T(1,128)}, u32[]{:S(2)}) copy-start(s32[1,1,5,5,32]{4,1,3,2,0:T(1,128)} %param.14) | copy-start | bytes 9604
  0.7 4.8 %copy-start.4 = (s32[1,1,5,5,32]{4,1,3,2,0:T(1,128)S(1)}, s32[1,1,5,5,32]{4,1,3,2,0:T(1,128)}, u32[]{:S(2)}) copy-start(s32[1,1,5,5,32]{4,1,3,2,0:T(1,128)} %param.15) | copy-start | bytes 9604
  0.7 4.8 %copy-start.5 = (s32[1,1,5,5,32]{4,1,3,2,0:T(1,128)S(1)}, s32[1,1,5,5,32]{4,1,3,2,0:T(1,128)}, u32[]{:S(2)}) copy-start(s32[1,1,5,5,32]{4,1,3,2,0:T(1,128)} %param.16) | copy-start | bytes 9604
  0.7 4.8 %copy-start.6 = (f32[32,384]{1,0:T(8,128)S(1)}, f32[32,384]{1,0:T(8,128)}, u32[]{:S(2)}) copy-start(f32[32,384]{1,0:T(8,128)} %out_ref.1) | copy-start | bytes 147460
  0.7 4.8 %copy-start.7 = (f32[10,32]{1,0:T(8,128)S(1)}, f32[10,32]{1,0:T(8,128)}, u32[]{:S(2)}) copy-start(f32[10,32]{1,0:T(8,128)} %emb_ref.1) | copy-start | bytes 3844
  0.7 4.8 %copy-start.8 = (f32[8,32]{1,0:T(8,128)S(1)}, f32[8,32]{1,0:T(8,128)}, u32[]{:S(2)}) copy-start(f32[8,32]{1,0:T(8,128)} %in_ref.1) | copy-start | bytes 3076
  2.5 3.2 %copy-start = (f32[296,128]{1,0:T(8,128)S(1)}, f32[296,128]{1,0:T(8,128)}, u32[]{:S(2)}) copy-start(f32[296,128]{1,0:T(8,128)} %get-tuple-element.47.refs_10_) | copy-start | bytes 454660
  2.5 6.9 %copy-start.1 = (f32[40,128]{1,0:T(8,128)S(1)}, f32[40,128]{1,0:T(8,128)}, u32[]{:S(2)}) copy-start(f32[40,128]{1,0:T(8,128)} %get-tuple-element.37.refs_0_.refs_5_) | copy-start | bytes 61444
  2.5 6.9 %collective-permute-start = (f32[72,128]{1,0:T(8,128)}, f32[72,128]{1,0:T(8,128)S(1)}, u32[]{:S(2)}, u32[]{:S(2)}) collective-permute-start(f32[72,128]{1,0:T(8,128)} %get-tuple-element.35), channel_id=1, source_target_pairs={{0,1},{1,0},{2,3},{3,2},{4,5},{5,4},{6,7},{7,6},{8,9},{9,8},{10,11... | collective-permute-start | bytes 110600 | tf_op jit(solution)/shard_map/ppermute | solution.py:31
  5.7 10.5 %collective-permute-start.5 = (f32[296,128]{1,0:T(8,128)S(1)}, f32[296,128]{1,0:T(8,128)S(1)}, u32[]{:S(2)}, u32[]{:S(2)}) collective-permute-start(f32[296,128]{1,0:T(8,128)S(1)} %copy-done), channel_id=1, source_target_pairs={{0,6},{1,7},{2,4},{3,5},{4,2},{5,3},{6,0},{7,1},{8,14},{9,15},{10,... | collective-permute-start | bytes 454664 | tf_op jit(solution)/shard_map/ppermute | solution.py:31
  9.4 7.0 %collective-permute-start.4 = (f32[296,128]{1,0:T(8,128)S(1)}, f32[296,128]{1,0:T(8,128)S(1)}, u32[]{:S(2)}, u32[]{:S(2)}) collective-permute-start(f32[296,128]{1,0:T(8,128)S(1)} %copy-done), channel_id=1, source_target_pairs={{0,2},{1,3},{2,0},{3,1},{4,6},{5,7},{6,4},{7,5},{8,10},{9,11},{10,... | collective-permute-start | bytes 454664 | tf_op jit(solution)/shard_map/ppermute | solution.py:31
  9.4 4.1 %collective-permute-start.3 = (f32[80,128]{1,0:T(8,128)S(1)}, f32[80,128]{1,0:T(8,128)S(1)}, u32[]{:S(2)}, u32[]{:S(2)}) collective-permute-start(f32[80,128]{1,0:T(8,128)S(1)} %stack.1), channel_id=1, source_target_pairs={{0,16},{8,24},{16,0},{24,8},{1,17},{9,25},{17,1},{25,9},{2,18},{10... | collective-permute-start | bytes 122888 | tf_op jit(solution)/shard_map/ppermute | solution.py:31
  11.0 3.4 %collective-permute-start.2 = (f32[80,128]{1,0:T(8,128)S(1)}, f32[80,128]{1,0:T(8,128)S(1)}, u32[]{:S(2)}, u32[]{:S(2)}) collective-permute-start(f32[80,128]{1,0:T(8,128)S(1)} %stack.1), channel_id=1, source_target_pairs={{0,24},{8,16},{16,8},{24,0},{1,25},{9,17},{17,9},{25,1},{2,26},{10... | collective-permute-start | bytes 122888 | tf_op jit(solution)/shard_map/ppermute | solution.py:31
  11.0 3.4 %collective-permute-start.1 = (f32[80,128]{1,0:T(8,128)S(1)}, f32[80,128]{1,0:T(8,128)S(1)}, u32[]{:S(2)}, u32[]{:S(2)}) collective-permute-start(f32[80,128]{1,0:T(8,128)S(1)} %stack.1), channel_id=1, source_target_pairs={{0,8},{8,0},{16,24},{24,16},{1,9},{9,1},{17,25},{25,17},{2,10},{10... | collective-permute-start | bytes 122888 | tf_op jit(solution)/shard_map/ppermute | solution.py:31
  18.5 4.3 %collective-permute-start.6 = (f32[80,128]{1,0:T(8,128)S(1)}, f32[80,128]{1,0:T(8,128)S(1)}, u32[]{:S(2)}, u32[]{:S(2)}) collective-permute-start(f32[80,128]{1,0:T(8,128)S(1)} %get-tuple-element.49), channel_id=1, source_target_pairs={{0,8},{8,0},{16,24},{24,16},{1,9},{9,1},{17,25},{25,17},{2,10},{10... | collective-permute-start | bytes 122888 | tf_op jit(solution)/shard_map/ppermute | solution.py:31
  18.6 4.3 %collective-permute-start.7 = (f32[80,128]{1,0:T(8,128)S(1)}, f32[80,128]{1,0:T(8,128)S(1)}, u32[]{:S(2)}, u32[]{:S(2)}) collective-permute-start(f32[80,128]{1,0:T(8,128)S(1)} %get-tuple-element.50), channel_id=1, source_target_pairs={{0,24},{8,16},{16,8},{24,0},{1,25},{9,17},{17,9},{25,1},{2,26},{10... | collective-permute-start | bytes 122888 | tf_op jit(solution)/shard_map/ppermute | solution.py:31
  20.2 4.0 %collective-permute-start.8 = (f32[80,128]{1,0:T(8,128)S(1)}, f32[80,128]{1,0:T(8,128)S(1)}, u32[]{:S(2)}, u32[]{:S(2)}) collective-permute-start(f32[80,128]{1,0:T(8,128)S(1)} %get-tuple-element.51), channel_id=1, source_target_pairs={{0,16},{8,24},{16,0},{24,8},{1,17},{9,25},{17,1},{25,9},{2,18},{10... | collective-permute-start | bytes 122888 | tf_op jit(solution)/shard_map/ppermute | solution.py:31
  20.7 5.7 %collective-permute-start.10 = (f32[64,128]{1,0:T(8,128)S(1)}, f32[64,128]{1,0:T(8,128)S(1)}, u32[]{:S(2)}, u32[]{:S(2)}) collective-permute-start(f32[64,128]{1,0:T(8,128)S(1)} %get-tuple-element.54), channel_id=1, source_target_pairs={{0,6},{1,7},{2,4},{3,5},{4,2},{5,3},{6,0},{7,1},{8,14},{9,15},{10,... | collective-permute-start | bytes 98312 | tf_op jit(solution)/shard_map/ppermute | solution.py:31
  22.9 3.9 %collective-permute-start.11 = (f32[64,128]{1,0:T(8,128)S(1)}, f32[64,128]{1,0:T(8,128)S(1)}, u32[]{:S(2)}, u32[]{:S(2)}) collective-permute-start(f32[64,128]{1,0:T(8,128)S(1)} %get-tuple-element.55), channel_id=1, source_target_pairs={{0,2},{1,3},{2,0},{3,1},{4,6},{5,7},{6,4},{7,5},{8,10},{9,11},{10,... | collective-permute-start | bytes 98312 | tf_op jit(solution)/shard_map/ppermute | solution.py:31
  24.2 3.8 %collective-permute-start.9 = (f32[40,128]{1,0:T(8,128)S(1)}, f32[40,128]{1,0:T(8,128)S(1)}, u32[]{:S(2)}, u32[]{:S(2)}) collective-permute-start(f32[40,128]{1,0:T(8,128)S(1)} %get-tuple-element.53), channel_id=1, source_target_pairs={{0,1},{1,0},{2,3},{3,2},{4,5},{5,4},{6,7},{7,6},{8,9},{9,8},{10,11... | collective-permute-start | bytes 61448 | tf_op jit(solution)/shard_map/ppermute | solution.py:31

commit v6 on v5

--- a/solution.py
+++ b/solution.py
@@ -66,12 +66,12 @@
     return lax.dot_general(a, b, (((0,), (0,)), ((), ())), preferred_element_type=f32)
 
 
-def write_rows(store, gx_spots, at_x, lists, step_y, place, start):
+def write_rows(store, gx_spots, at_x, lists, step_y, place, start, first_source=0):
     atoms = pairs = lists[0].shape[4]
     for slot, (table, link, sign) in enumerate(gx_spots):
         step_x = 0 if link is None else sign * link.delta(at_x)
         src, tgt, mask, spec = (ref[0, reach + step_x, reach + step_y] for ref in lists)
-        store(0, start + slot * pairs, src + table * atoms)
+        store(0, start + slot * pairs, src + (first_source + table * atoms))
         store(1, start + slot * pairs, tgt + place * atoms)
         store(2, start + slot * pairs, mask)
         store(3, start + slot * pairs, spec)
@@ -99,13 +99,13 @@
         y_ref[atoms + axis : atoms + axis + 1, 0:atoms] = row
         gy_ref[parts * atoms + axis : parts * atoms + axis + 1, 0:atoms] = row
 
-    base = atoms + sublanes
-    for start in range(base, y_ref.shape[0], sublanes):
+    block = atoms + sublanes
+    for start in range(block, y_ref.shape[0], sublanes):
         y_ref[start : start + sublanes] = zero
 
     def store(row, lane, value):
         chunk, lane = divmod(lane, channels)
-        at = base + chunk * sublanes + row
+        at = block + chunk * sublanes + row
         y_ref[at : at + 1, lane : lane + pairs] = value.astype(f32)
 
     at_x, at_y = lax.axis_index("gx"), lax.axis_index("gy")
@@ -113,9 +113,14 @@
     near, other = gy_links[0].delta(at_y), gy_links[1].delta(at_y)
     partner = at_y + near
     to_far = (partner + (partner >> 1)) & 1
-    lanes = -(-len(gx_spots) * pairs // channels) * channels
-    write_rows(store, gx_spots, at_x, lists, near, 0, 0)
-    write_rows(store, gx_spots, at_x, lists, other, to_far, lanes)
+    sources = (1 + max(table for table, _, _ in gx_spots)) * atoms
+    slots = len(gx_spots) * pairs
+    lane = 0
+    for own, step_y, place in ((1, near, 0), (2, other, to_far)):
+        base, chunks = partner_chunks(own * slots, slots, channels)
+        start = lane + own * slots - base
+        write_rows(store, gx_spots, at_x, lists, step_y, place, start, sources)
+        lane += chunks * channels
 
 
 def stack_kernel(rows, *refs):
@@ -177,11 +182,11 @@
     return jnp.where(lax.broadcasted_iota(jnp.int32, (count, ids.shape[1]), 0) == ids, 1.0, 0.0)
 
 
-def slot_grads(rows, cot_refs, columns, weights, orders):
+def slot_grads(rows, cot_refs, src_pos, feats, weights, orders):
     wide, back, first, last = weights
     slots = rows.shape[1]
-    sources = columns[0][1].shape[1]
-    channels = columns[0][2].shape[0]
+    sources = src_pos.shape[1]
+    channels = feats.shape[0]
     hidden = last.shape[1] // 3
     parts = len(degree)
     atoms = (cot_refs[0].shape[0] - sublanes) // parts
@@ -193,8 +198,7 @@
     offset = rows[4:6].astype(f32) * domain_side
 
     tgt_pos = [jnp.concatenate(pieces(ref[parts * atoms :, 0:atoms], 3), axis=0) for ref in cot_refs]
-    hots = [src_hot[:, lanes] for lanes, _, _ in columns]
-    from_src = jnp.concatenate([dot(c[1], hot) for c, hot in zip(columns, hots)], axis=1)
+    from_src = dot(src_pos, src_hot)
     from_tgt = dot(jnp.concatenate(tgt_pos, axis=1).astype(bf16), tgt_hot)
     from_src = from_src[0:8] + from_src[8:16] + from_src[16:24]
     from_tgt = from_tgt[0:8] + from_tgt[8:16] + from_tgt[16:24]
@@ -221,9 +225,7 @@
     act = before * gate
     d_act = gate * (1.0 + before * (1.0 - gate))
     radial = dot(wide, thrice(act))
-    gathered = jnp.concatenate(
-        [dot(c[2], jnp.concatenate([hot, hot], axis=0)) for c, hot in zip(columns, hots)], axis=1
-    )
+    gathered = dot(feats, jnp.concatenate([src_hot, src_hot], axis=0))
 
     root3, root5, root15 = math.sqrt(3.0), math.sqrt(5.0), math.sqrt(15.0)
     shapes = [
@@ -272,72 +274,66 @@
          jnp.zeros((sublanes - 3, slots), f32)], axis=0,
     )
     grad = jnp.concatenate(pieces(grad, 2), axis=0).astype(bf16)
+    pos_src = dot_rows(grad, src_hot)
     pos_tgt = dot_rows(grad, tgt_hot)
-    through = [p.astype(bf16) for p in pieces(through, 2)]
-    sums = []
-    for (lanes, _, _), hot in zip(columns, hots):
-        pos_src = dot_rows(grad[:, lanes], hot)
-        feat_src = dot_rows(hot, through[0][:, lanes]) + dot_rows(hot, through[1][:, lanes])
-        sums.append((pos_src[0:8] + pos_src[8:16], feat_src))
-    return sums, -(pos_tgt[0:8] + pos_tgt[8:16])
-
-
-def all_rows(rows_ref, y_ref, block, late):
+    feat_src = sum(dot_rows(src_hot, p.astype(bf16)) for p in pieces(through, 2))
+    return pos_src[0:8] + pos_src[8:16], -(pos_tgt[0:8] + pos_tgt[8:16]), feat_src
+
+
+def partner_chunks(first, slots, lanes):
+    base = first // lanes * lanes
+    return base, -(-(first + slots - base) // lanes)
+
+
+def all_rows(rows_ref, y_ref, start, chunks):
     own = rows_ref[...]
-    count = (y_ref.shape[0] - block) // (2 * sublanes)
-    start = block + late * count * sublanes
-    chunks = [y_ref[start + at * sublanes : start + (at + 1) * sublanes] for at in range(count)]
-    rows = jnp.concatenate([own, jnp.concatenate(chunks, axis=1).astype(jnp.int32)], axis=1)
-    return rows, (slice(0, own.shape[1]), slice(own.shape[1], None))
-
-
-def early_kernel(orders, tables, rows_ref, *refs):
+    parts = [y_ref[start + at * sublanes : start + (at + 1) * sublanes] for at in range(chunks)]
+    theirs = jnp.concatenate(parts, axis=1).astype(jnp.int32)
+    base = own.shape[1] - theirs.shape[1]
+    if base:
+        theirs = jnp.concatenate([jnp.zeros((sublanes, base), jnp.int32), theirs], axis=1)
+    return own + theirs
+
+
+def early_kernel(orders, tables, start, chunks, rows_ref, *refs):
     refs = list(refs)
     weights = [refs.pop(0)[...] for _ in range(4)]
     y_ref = refs.pop(0)
-    block_refs = [refs.pop(0) for _ in range(1 + max(ref for column in tables for ref, _ in column))]
-    cot_ref = refs.pop(0)
-    *outs, place = refs
+    block_refs = [refs.pop(0) for _ in range(1 + max(ref for ref, _ in tables))]
+    cot_ref, src_pos_ref, feats_ref, pos_ref, feat_ref, place = refs
     atoms = (cot_ref.shape[0] - sublanes) // len(degree)
     block = atoms + sublanes
-    rows, lanes = all_rows(rows_ref, y_ref, block, 0)
-    columns = []
-    for at, column in enumerate(tables):
-        views = [block_refs[ref].at[start * block : (start + 1) * block] for ref, start in column]
-        for table, ref in enumerate(views):
-            place[at, :, table * atoms : (table + 1) * atoms] = ref[atoms:, 0:atoms]
-        src_pos = jnp.concatenate(pieces(place[at], 3), axis=0).astype(bf16)
-        feats = pieces(jnp.concatenate([ref[0:atoms] for ref in views], axis=0), 2)
-        feats = jnp.concatenate(feats, axis=0).T.astype(bf16)
-        outs[4 * at][...] = src_pos
-        outs[4 * at + 1][...] = feats
-        columns.append((lanes[at], src_pos, feats))
-    sums, pos_tgt = slot_grads(rows, [cot_ref], columns, weights, orders)
-    for at, (pos, feat) in enumerate(sums):
-        outs[4 * at + 2][...] = pos
-        outs[4 * at + 3][...] = feat
-    outs[2][:, 0:atoms] = sums[0][0][:, 0:atoms] + pos_tgt
-
-
-def late_kernel(orders, homes, rows_ref, *refs):
+    views = [block_refs[ref].at[at * block : (at + 1) * block] for ref, at in tables]
+    for table, ref in enumerate(views):
+        place[:, table * atoms : (table + 1) * atoms] = ref[atoms:, 0:atoms]
+    src_pos_ref[...] = jnp.concatenate(pieces(place[...], 3), axis=0).astype(bf16)
+    feats = jnp.concatenate([ref[0:atoms] for ref in views], axis=0).T
+    feats_ref[...] = jnp.concatenate(pieces(feats, 2), axis=1).astype(bf16)
+    rows = all_rows(rows_ref, y_ref, start, chunks)
+    pos, pos_tgt, feat = slot_grads(
+        rows, [cot_ref], src_pos_ref[...], feats_ref[...], weights, orders
+    )
+    feat_ref[...] = feat
+    pos_ref[...] = pos
+    pos_ref[:, 0:atoms] = pos[:, 0:atoms] + pos_tgt
+
+
+def late_kernel(orders, homes, start, chunks, rows_ref, *refs):
     refs = list(refs)
     weights = [refs.pop(0)[...] for _ in range(4)]
-    y_ref = refs.pop(0)
-    held = [refs.pop(0) for _ in range(8)]
+    y_ref, src_pos_ref, feats_ref, held_pos, held_feat = (refs.pop(0) for _ in range(5))
     cot_refs = [refs.pop(0) for _ in range(2)]
     *outs, near_ref, far_ref = refs
     atoms = (cot_refs[0].shape[0] - sublanes) // len(degree)
     block = atoms + sublanes
-    rows, lanes = all_rows(rows_ref, y_ref, block, 1)
-    columns = [(lanes[at], held[4 * at][...], held[4 * at + 1][...]) for at in range(2)]
-    sums, pos_tgt = slot_grads(rows, cot_refs, columns, weights, orders)
-    sums = [
-        (pos + held[4 * at + 2][...], feat + held[4 * at + 3][...])
-        for at, (pos, feat) in enumerate(sums)
-    ]
+    rows = all_rows(rows_ref, y_ref, start, chunks)
+    pos, pos_tgt, feat = slot_grads(
+        rows, cot_refs, src_pos_ref[...], feats_ref[...], weights, orders
+    )
+    pos = pos + held_pos[...]
+    feat = feat + held_feat[...]
     for ref, home in zip(outs, homes):
-        for at, (column, table) in enumerate(home):
-            pos, feat = sums[column]
+        for at, table in enumerate(home):
             part = slice(table * atoms, (table + 1) * atoms)
             ref[at * block : at * block + atoms] = feat[part]
             ref[at * block + atoms : (at + 1) * block] = jnp.zeros((sublanes, ref.shape[1]), f32)
@@ -406,7 +402,8 @@
     by_axis = jnp.transpose(positions, (0, 2, 1, 3))
     lists = [jnp.transpose(x, (0, 2, 3, 1, 4)) for x in (nbr_src, nbr_tgt, pair_mask, pair_species)]
     gx_pack = sds((block, channels), f32)
-    y_pack = sds((block + 2 * -(-slots // channels) * sublanes, channels), f32)
+    chunks = [partner_chunks(own * slots, slots, channels)[1] for own in (1, 2)]
+    y_pack = sds((block + sum(chunks) * sublanes, channels), f32)
     gy_pack = sds((len(degree) * atoms + sublanes, channels), f32)
     own, y_own, cot_own = call(
         functools.partial(pack_kernel, gx_spots, gy_links), "pack", (gx_pack, y_pack, gy_pack),
@@ -414,16 +411,17 @@
     )
     far_links = (gy_links[3], gy_links[2])
     y = gy_links[0].swap(y_own, "gy")
-    tables = tuple(
-        ((at, 0),) + tuple((2 + l, at) for l in range(len(gx_links))) for at in range(2)
-    )
-    homes = tuple(((0, table), (1, table)) for table in range(len(gx_links) + 1))
-
+    many = len(gx_links) + 1
+    tables = [(at, 0) if not l else (1 + l, at) for at in range(2) for l in range(many)]
+    if gx_size == 4:
+        homes = ((0, many, 3, many + 3), (1, many + 1, 2, many + 2))
+    else:
+        homes = tuple((table, many + table) for table in range(many))
     early_rows, late_rows, *weights = call(
         functools.partial(prep_kernel, gx_spots, gy_links),
         "prepare",
         (
-            *(sds((sublanes, -(-n * slots // channels) * channels), jnp.int32) for n in (1, 2)),
+            *(sds((sublanes, -(-n * slots // channels) * channels), jnp.int32) for n in (2, 3)),
             sds((w_out.shape[1], 3 * hidden), bf16),
             sds((2 * hidden, 2 * w_out.shape[1]), bf16),
             sds((hidden, 3 * (orders + 2 * sublanes)), bf16),
@@ -438,24 +436,34 @@
         (own, y, weights[-1]), us=2,
     )
     blocks = [own, y] + [link.swap(two, "gx") for link in gx_links]
-    column = (
-        sds((3 * sublanes, sources), bf16), sds((channels, 2 * sources), bf16),
-        sds((sublanes, sources), f32), sds((sources, channels), f32),
+    table = (
+        sds((3 * sublanes, 2 * sources), bf16), sds((channels, 4 * sources), bf16),
+        sds((sublanes, 2 * sources), f32), sds((2 * sources, channels), f32),
     )
     held = call(
-        functools.partial(early_kernel, orders, tables), "early_tiles", column * 2,
-        (early_rows, *weights, y, *blocks, cot_own), [pltpu.VMEM((2, sublanes, sources), f32)], 24,
+        functools.partial(early_kernel, orders, tables, block, chunks[0]), "early_tiles", table,
+        (early_rows, *weights, y, *blocks, cot_own),
+        [pltpu.VMEM((sublanes, 2 * sources), f32)], 24,
     )
     far_pack = sds((channels // 2, channels), f32)
     *sent, near, far = call(
-        functools.partial(late_kernel, orders, homes), "late_tiles",
+        functools.partial(late_kernel, orders, homes, block + chunks[0] * sublanes, chunks[1]),
+        "late_tiles",
         tuple(sds((len(home) * block, channels), f32) for home in homes) + (far_pack,) * 2,
         (late_rows, *weights, y, *held, cot_near, cot_far), room=24,
     )
     back_gy = [link.swap(value, "gy") for link, value in zip(far_links, (far, near))]
-    came = [link.swap(value, "gx") for link, value in zip(gx_links, sent[1:])]
+    if gx_size == 4:
+        came = gx_links[0].swap(sent[1], "gx")
+        near_chip, far_chip = call(
+            functools.partial(add_kernel, 2), "add", (sds((2 * block, channels), f32),) * 2,
+            (sent[0], came),
+        )
+        sent, came = [near_chip], [gx_links[2].swap(far_chip, "gx")]
+    else:
+        came = [link.swap(value, "gx") for link, value in zip(gx_links, sent[1:])]
     own, y = call(
-        functools.partial(add_kernel, len(sent)), "add", (gx_pack,) * 2, (sent[0], *came)
+        functools.partial(add_kernel, 1 + len(came)), "add", (gx_pack,) * 2, (sent[0], *came)
     )
     back = [own, gy_links[0].swap(y, "gy")]
     pos, feat = call(

time: 28.8 us -> 28.4 us (0.986)
  starting transfers between devices: 14.1 us -> 13.1 us
  waiting for transfers between devices: 7.16 us -> 7.97 us
    ppermute x12 -> x11, starting transfers between devices: 14.1 us -> 13.1 us  [swap(): lax.ppermute(value, axis, [(i, (i + self.delta(i)) % n) for i in range(n)])]
    ppermute x12 -> x11, waiting for transfers between devices: 7.16 us -> 7.97 us  [swap(): lax.ppermute(value, axis, [(i, (i + self.delta(i)) % n) for i in range(n)])]
    pallas_call x7 -> x8, Pallas kernels: 6.55 us -> 6.33 us  [call(): pl.pallas_call(kernel, out_shape=out_shape, in_specs=[vmem] * len(operand...]
  transfers between devices with their start and end apart: 12 -> 11, of which waited for: 7 -> 8; matrix products, arithmetic and copies ran while one was open for 0% -> 0% of each run, Pallas kernels for 7% -> 7%
where the time goes in v6:
time: 28.4 us; the launch traced here: 28.2 us
  starting transfers between devices  13.1 us (46%)
  waiting for transfers between devices  7.97 us (28%)
  Pallas kernels  6.33 us (22%)
  between operations  0.79 us (3%)
    ppermute x11, starting transfers between devices, swap(): lax.ppermute(value, axis, [(i, (i + self.delta(i)) % n) for i in range(n)])  13.1 us
    ppermute x11, waiting for transfers between devices, swap(): lax.ppermute(value, axis, [(i, (i + self.delta(i)) % n) for i in range(n)])  7.97 us
    pallas_call x8, Pallas kernels, call(): pl.pallas_call(kernel, out_shape=out_shape, in_specs=[vmem] * len(operand...  6.33 us
  transfers between devices with their start and end apart: 11, of which 8 were waited for; matrix products, arithmetic and copies ran while one was open for 0% of the time, Pallas kernels for 7%

profile of v6, /device:TPU:0, one launch (start us, length us, event | category | flops | bytes accessed | tf_op | source)
XLA Modules:
  0.0 28.2 jit_solution(12442628600346782765)
XLA Ops:
  0.6 0.0 copy-start.2
  0.6 0.0 copy-start.3
  0.7 1.8 %pack.1 = (f32[40,128]{1,0:T(8,128)}, f32[72,128]{1,0:T(8,128)}, f32[296,128]{1,0:T(8,128)}) custom-call(f32[1,3,1,32]{3,2,1,0:T(1,128)} %bitcast.14, f32[1,1,32,128]{3,2,1,0:T(8,128)} %feat_ref.1, f32[1,1,32,1152]{3,2,1,0:T(8,128)} %cot_ref.1, s32[1,5,5,1,32]{4,3,2,1,0:T(1,128)} %bitcast.6, s32[1,5,5,1,32]{4,3,2,1,0:T(1,128)} %bitcast.8, ...), custom_call_target="tpu_custom_call" | custom-call | tf_op jit(solution)/shard_map/pack/pallas_call | solution.py:374
  2.5 3.0 %collective-permute-start = (f32[72,128]{1,0:T(8,128)}, f32[72,128]{1,0:T(8,128)S(1)}, u32[]{:S(2)}, u32[]{:S(2)}) collective-permute-start(f32[72,128]{1,0:T(8,128)} %get-tuple-element.31), channel_id=1, source_target_pairs={{0,1},{1,0},{2,3},{3,2},{4,5},{5,4},{6,7},{7,6},{8,9},{9,8},{10,11... | collective-permute-start | bytes 110600 | tf_op jit(solution)/shard_map/ppermute | solution.py:31
  5.5 0.0 copy-done.3
  5.5 0.0 copy-done.5
  5.5 0.2 prepare.1
  5.7 0.0 copy-done
  5.7 3.7 %collective-permute-start.5 = (f32[296,128]{1,0:T(8,128)S(1)}, f32[296,128]{1,0:T(8,128)S(1)}, u32[]{:S(2)}, u32[]{:S(2)}) collective-permute-start(f32[296,128]{1,0:T(8,128)S(1)} %copy-done), channel_id=1, source_target_pairs={{0,6},{1,7},{2,4},{3,5},{4,2},{5,3},{6,0},{7,1},{8,14},{9,15},{10,... | collective-permute-start | bytes 454664 | tf_op jit(solution)/shard_map/ppermute | solution.py:31
  9.4 0.0 collective-permute-start.4
  9.4 0.0 collective-permute-done.refs_1_.refs_4_.refs_6_
  9.4 1.6 %collective-permute-start.3 = (f32[80,128]{1,0:T(8,128)S(1)}, f32[80,128]{1,0:T(8,128)S(1)}, u32[]{:S(2)}, u32[]{:S(2)}) collective-permute-start(f32[80,128]{1,0:T(8,128)S(1)} %stack.1), channel_id=1, source_target_pairs={{0,16},{8,24},{16,0},{24,8},{1,17},{9,25},{17,1},{25,9},{2,18},{10... | collective-permute-start | bytes 122888 | tf_op jit(solution)/shard_map/ppermute | solution.py:31
  11.0 0.0 collective-permute-start.2
  11.0 0.6 %collective-permute-start.1 = (f32[80,128]{1,0:T(8,128)S(1)}, f32[80,128]{1,0:T(8,128)S(1)}, u32[]{:S(2)}, u32[]{:S(2)}) collective-permute-start(f32[80,128]{1,0:T(8,128)S(1)} %stack.1), channel_id=1, source_target_pairs={{0,8},{8,0},{16,24},{24,16},{1,9},{9,1},{17,25},{25,17},{2,10},{10... | collective-permute-start | bytes 122888 | tf_op jit(solution)/shard_map/ppermute | solution.py:31
  11.6 1.9 %collective-permute-done.3.refs_9_ = f32[80,128]{1,0:T(8,128)S(1)} collective-permute-done((f32[80,128]{1,0:T(8,128)S(1)}, f32[80,128]{1,0:T(8,128)S(1)}, u32[]{:S(2)}, u32[]{:S(2)}) %collective-permute-start.3) | collective-permute-done | bytes 40992 | tf_op jit(solution)/shard_map/ppermute | solution.py:31
  13.5 0.9 %collective-permute-done.2.refs_8_ = f32[80,128]{1,0:T(8,128)S(1)} collective-permute-done((f32[80,128]{1,0:T(8,128)S(1)}, f32[80,128]{1,0:T(8,128)S(1)}, u32[]{:S(2)}, u32[]{:S(2)}) %collective-permute-start.2) | collective-permute-done | bytes 40992 | tf_op jit(solution)/shard_map/ppermute | solution.py:31
  14.4 0.0 collective-permute-done.1.refs_7_
  14.4 1.7 %early_tiles.1 = (bf16[24,256]{1,0:T(8,128)(2,1)S(1)}, bf16[128,512]{1,0:T(8,128)(2,1)S(1)}, f32[8,256]{1,0:T(8,128)S(1)}, f32[256,128]{1,0:T(8,128)S(1)}) custom-call(s32[8,384]{1,0:T(8,128)S(1)} %get-tuple-element.32.rows_ref, bf16[384,96]{1,0:T(8,128)(2,1)S(1)} %get-tuple-element.27.refs_0_, bf16[64,768]{1,0:T(8,128)(2,1)S(1)} %get-tuple-element.28.refs_1_, ...), custom_call_target="tpu_custom_call" | custom-call | tf_op jit(solution)/shard_map/early_tiles/pallas_call | solution.py:374
  16.1 0.0 collective-permute-done.5.refs_10_
  16.1 0.3 collective-permute-done.4.refs_9_
  16.4 2.0 %late_tiles.1 = (f32[160,128]{1,0:T(8,128)S(1)}, f32[160,128]{1,0:T(8,128)S(1)}, f32[64,128]{1,0:T(8,128)S(1)}, f32[64,128]{1,0:T(8,128)S(1)}) custom-call(s32[8,512]{1,0:T(8,128)S(1)} %get-tuple-element.26.rows_ref, bf16[384,96]{1,0:T(8,128)(2,1)S(1)} %get-tuple-element.27.refs_0_, bf16[64,768]{1,0:T(8,128)(2,1)S(1)} %get-tuple-element.28.refs_1_, ...), custom_call_target="tpu_custom_call" | custom-call | tf_op jit(solution)/shard_map/late_tiles/pallas_call | solution.py:374
  18.4 0.1 collective-permute-start.6
  18.5 1.3 %collective-permute-done.6.refs_1_ = f32[160,128]{1,0:T(8,128)S(1)} collective-permute-done((f32[160,128]{1,0:T(8,128)S(1)}, f32[160,128]{1,0:T(8,128)S(1)}, u32[]{:S(2)}, u32[]{:S(2)}) %collective-permute-start.6) | collective-permute-done | bytes 81952 | tf_op jit(solution)/shard_map/ppermute | solution.py:31
  19.8 1.6 %collective-permute-start.7 = (f32[80,128]{1,0:T(8,128)S(1)}, f32[80,128]{1,0:T(8,128)S(1)}, u32[]{:S(2)}, u32[]{:S(2)}) collective-permute-start(f32[80,128]{1,0:T(8,128)S(1)} %get-tuple-element.43), channel_id=1, source_target_pairs={{0,16},{8,24},{16,0},{24,8},{1,17},{9,25},{17,1},{25,9},{2,18},{10... | collective-permute-start | bytes 122888 | tf_op jit(solution)/shard_map/ppermute | solution.py:31
  21.3 1.7 %collective-permute-start.9 = (f32[64,128]{1,0:T(8,128)S(1)}, f32[64,128]{1,0:T(8,128)S(1)}, u32[]{:S(2)}, u32[]{:S(2)}) collective-permute-start(f32[64,128]{1,0:T(8,128)S(1)} %get-tuple-element.46), channel_id=1, source_target_pairs={{0,6},{1,7},{2,4},{3,5},{4,2},{5,3},{6,0},{7,1},{8,14},{9,15},{10,... | collective-permute-start | bytes 98312 | tf_op jit(solution)/shard_map/ppermute | solution.py:31
  23.0 0.0 collective-permute-start.10
  23.0 0.8 %collective-permute-done.7.refs_1_ = f32[80,128]{1,0:T(8,128)S(1)} collective-permute-done((f32[80,128]{1,0:T(8,128)S(1)}, f32[80,128]{1,0:T(8,128)S(1)}, u32[]{:S(2)}, u32[]{:S(2)}) %collective-permute-start.7) | collective-permute-done | bytes 40992 | tf_op jit(solution)/shard_map/ppermute | solution.py:31
  23.8 0.9 %collective-permute-start.8 = (f32[40,128]{1,0:T(8,128)S(1)}, f32[40,128]{1,0:T(8,128)S(1)}, u32[]{:S(2)}, u32[]{:S(2)}) collective-permute-start(f32[40,128]{1,0:T(8,128)S(1)} %get-tuple-element.45), channel_id=1, source_target_pairs={{0,1},{1,0},{2,3},{3,2},{4,5},{5,4},{6,7},{7,6},{8,9},{9,8},{10,11... | collective-permute-start | bytes 61448 | tf_op jit(solution)/shard_map/ppermute | solution.py:31
  24.7 2.4 %collective-permute-done.9.refs_2_ = f32[64,128]{1,0:T(8,128)S(1)} collective-permute-done((f32[64,128]{1,0:T(8,128)S(1)}, f32[64,128]{1,0:T(8,128)S(1)}, u32[]{:S(2)}, u32[]{:S(2)}) %collective-permute-start.9) | collective-permute-done | bytes 32800 | tf_op jit(solution)/shard_map/ppermute | solution.py:31
  27.1 0.2 collective-permute-done.10.refs_3_
  27.3 0.3 %collective-permute-done.8.refs_1_ = f32[40,128]{1,0:T(8,128)S(1)} collective-permute-done((f32[40,128]{1,0:T(8,128)S(1)}, f32[40,128]{1,0:T(8,128)S(1)}, u32[]{:S(2)}, u32[]{:S(2)}) %collective-permute-start.8) | collective-permute-done | bytes 20512 | tf_op jit(solution)/shard_map/ppermute | solution.py:31
  27.6 0.6 %sums.1 = (f32[1,3,1,32]{3,2,1,0:T(1,128)}, f32[1,1,32,128]{3,2,1,0:T(8,128)}) custom-call(f32[40,128]{1,0:T(8,128)S(1)} %get-tuple-element.44.refs_0_, f32[40,128]{1,0:T(8,128)S(1)} %collective-permute-done.8.refs_1_, f32[64,128]{1,0:T(8,128)S(1)} %collective-permute-done.9.refs_2_, f32[64,128]{1,0:T(8,128)S(1)} %collective-permute-done.10.refs_3_), custom_call_target="tpu_custom_call" | custom-call | tf_op jit(solution)/shard_map/sums/pallas_call | solution.py:374
  (16 shorter events, 0.0 us)
Async XLA Ops:
  0.6 4.9 %copy-start.2 = (s32[1,1,5,5,32]{4,1,3,2,0:T(1,128)S(1)}, s32[1,1,5,5,32]{4,1,3,2,0:T(1,128)}, u32[]{:S(2)}) copy-start(s32[1,1,5,5,32]{4,1,3,2,0:T(1,128)} %param.13) | copy-start | bytes 9604
  0.6 4.8 %copy-start.3 = (s32[1,1,5,5,32]{4,1,3,2,0:T(1,128)S(1)}, s32[1,1,5,5,32]{4,1,3,2,0:T(1,128)}, u32[]{:S(2)}) copy-start(s32[1,1,5,5,32]{4,1,3,2,0:T(1,128)} %param.14) | copy-start | bytes 9604
  0.7 4.8 %copy-start.4 = (s32[1,1,5,5,32]{4,1,3,2,0:T(1,128)S(1)}, s32[1,1,5,5,32]{4,1,3,2,0:T(1,128)}, u32[]{:S(2)}) copy-start(s32[1,1,5,5,32]{4,1,3,2,0:T(1,128)} %param.15) | copy-start | bytes 9604
  0.7 4.8 %copy-start.5 = (s32[1,1,5,5,32]{4,1,3,2,0:T(1,128)S(1)}, s32[1,1,5,5,32]{4,1,3,2,0:T(1,128)}, u32[]{:S(2)}) copy-start(s32[1,1,5,5,32]{4,1,3,2,0:T(1,128)} %param.16) | copy-start | bytes 9604
  0.7 4.8 %copy-start.6 = (f32[32,384]{1,0:T(8,128)S(1)}, f32[32,384]{1,0:T(8,128)}, u32[]{:S(2)}) copy-start(f32[32,384]{1,0:T(8,128)} %out_ref.1) | copy-start | bytes 147460
  0.7 4.8 %copy-start.7 = (f32[10,32]{1,0:T(8,128)S(1)}, f32[10,32]{1,0:T(8,128)}, u32[]{:S(2)}) copy-start(f32[10,32]{1,0:T(8,128)} %emb_ref.1) | copy-start | bytes 3844
  0.7 4.8 %copy-start.8 = (f32[8,32]{1,0:T(8,128)S(1)}, f32[8,32]{1,0:T(8,128)}, u32[]{:S(2)}) copy-start(f32[8,32]{1,0:T(8,128)} %in_ref.1) | copy-start | bytes 3076
  2.5 3.2 %copy-start = (f32[296,128]{1,0:T(8,128)S(1)}, f32[296,128]{1,0:T(8,128)}, u32[]{:S(2)}) copy-start(f32[296,128]{1,0:T(8,128)} %get-tuple-element.39.refs_10_) | copy-start | bytes 454660
  2.5 6.9 %copy-start.1 = (f32[40,128]{1,0:T(8,128)S(1)}, f32[40,128]{1,0:T(8,128)}, u32[]{:S(2)}) copy-start(f32[40,128]{1,0:T(8,128)} %get-tuple-element.33.refs_0_.refs_5_) | copy-start | bytes 61444
  2.5 6.9 %collective-permute-start = (f32[72,128]{1,0:T(8,128)}, f32[72,128]{1,0:T(8,128)S(1)}, u32[]{:S(2)}, u32[]{:S(2)}) collective-permute-start(f32[72,128]{1,0:T(8,128)} %get-tuple-element.31), channel_id=1, source_target_pairs={{0,1},{1,0},{2,3},{3,2},{4,5},{5,4},{6,7},{7,6},{8,9},{9,8},{10,11... | collective-permute-start | bytes 110600 | tf_op jit(solution)/shard_map/ppermute | solution.py:31
  5.7 10.4 %collective-permute-start.5 = (f32[296,128]{1,0:T(8,128)S(1)}, f32[296,128]{1,0:T(8,128)S(1)}, u32[]{:S(2)}, u32[]{:S(2)}) collective-permute-start(f32[296,128]{1,0:T(8,128)S(1)} %copy-done), channel_id=1, source_target_pairs={{0,6},{1,7},{2,4},{3,5},{4,2},{5,3},{6,0},{7,1},{8,14},{9,15},{10,... | collective-permute-start | bytes 454664 | tf_op jit(solution)/shard_map/ppermute | solution.py:31
  9.4 7.0 %collective-permute-start.4 = (f32[296,128]{1,0:T(8,128)S(1)}, f32[296,128]{1,0:T(8,128)S(1)}, u32[]{:S(2)}, u32[]{:S(2)}) collective-permute-start(f32[296,128]{1,0:T(8,128)S(1)} %copy-done), channel_id=1, source_target_pairs={{0,2},{1,3},{2,0},{3,1},{4,6},{5,7},{6,4},{7,5},{8,10},{9,11},{10,... | collective-permute-start | bytes 454664 | tf_op jit(solution)/shard_map/ppermute | solution.py:31
  9.4 4.1 %collective-permute-start.3 = (f32[80,128]{1,0:T(8,128)S(1)}, f32[80,128]{1,0:T(8,128)S(1)}, u32[]{:S(2)}, u32[]{:S(2)}) collective-permute-start(f32[80,128]{1,0:T(8,128)S(1)} %stack.1), channel_id=1, source_target_pairs={{0,16},{8,24},{16,0},{24,8},{1,17},{9,25},{17,1},{25,9},{2,18},{10... | collective-permute-start | bytes 122888 | tf_op jit(solution)/shard_map/ppermute | solution.py:31
  11.0 3.4 %collective-permute-start.2 = (f32[80,128]{1,0:T(8,128)S(1)}, f32[80,128]{1,0:T(8,128)S(1)}, u32[]{:S(2)}, u32[]{:S(2)}) collective-permute-start(f32[80,128]{1,0:T(8,128)S(1)} %stack.1), channel_id=1, source_target_pairs={{0,24},{8,16},{16,8},{24,0},{1,25},{9,17},{17,9},{25,1},{2,26},{10... | collective-permute-start | bytes 122888 | tf_op jit(solution)/shard_map/ppermute | solution.py:31
  11.0 3.4 %collective-permute-start.1 = (f32[80,128]{1,0:T(8,128)S(1)}, f32[80,128]{1,0:T(8,128)S(1)}, u32[]{:S(2)}, u32[]{:S(2)}) collective-permute-start(f32[80,128]{1,0:T(8,128)S(1)} %stack.1), channel_id=1, source_target_pairs={{0,8},{8,0},{16,24},{24,16},{1,9},{9,1},{17,25},{25,17},{2,10},{10... | collective-permute-start | bytes 122888 | tf_op jit(solution)/shard_map/ppermute | solution.py:31
  18.4 1.3 %collective-permute-start.6 = (f32[160,128]{1,0:T(8,128)S(1)}, f32[160,128]{1,0:T(8,128)S(1)}, u32[]{:S(2)}, u32[]{:S(2)}) collective-permute-start(f32[160,128]{1,0:T(8,128)S(1)} %get-tuple-element.41), channel_id=1, source_target_pairs={{0,8},{8,0},{16,24},{24,16},{1,9},{9,1},{17,25},{25,17},{2,10},{10... | collective-permute-start | bytes 245768 | tf_op jit(solution)/shard_map/ppermute | solution.py:31
  19.8 4.1 %collective-permute-start.7 = (f32[80,128]{1,0:T(8,128)S(1)}, f32[80,128]{1,0:T(8,128)S(1)}, u32[]{:S(2)}, u32[]{:S(2)}) collective-permute-start(f32[80,128]{1,0:T(8,128)S(1)} %get-tuple-element.43), channel_id=1, source_target_pairs={{0,16},{8,24},{16,0},{24,8},{1,17},{9,25},{17,1},{25,9},{2,18},{10... | collective-permute-start | bytes 122888 | tf_op jit(solution)/shard_map/ppermute | solution.py:31
  21.3 5.8 %collective-permute-start.9 = (f32[64,128]{1,0:T(8,128)S(1)}, f32[64,128]{1,0:T(8,128)S(1)}, u32[]{:S(2)}, u32[]{:S(2)}) collective-permute-start(f32[64,128]{1,0:T(8,128)S(1)} %get-tuple-element.46), channel_id=1, source_target_pairs={{0,6},{1,7},{2,4},{3,5},{4,2},{5,3},{6,0},{7,1},{8,14},{9,15},{10,... | collective-permute-start | bytes 98312 | tf_op jit(solution)/shard_map/ppermute | solution.py:31
  23.0 4.3 %collective-permute-start.10 = (f32[64,128]{1,0:T(8,128)S(1)}, f32[64,128]{1,0:T(8,128)S(1)}, u32[]{:S(2)}, u32[]{:S(2)}) collective-permute-start(f32[64,128]{1,0:T(8,128)S(1)} %get-tuple-element.47), channel_id=1, source_target_pairs={{0,2},{1,3},{2,0},{3,1},{4,6},{5,7},{6,4},{7,5},{8,10},{9,11},{10,... | collective-permute-start | bytes 98312 | tf_op jit(solution)/shard_map/ppermute | solution.py:31
  23.8 3.8 %collective-permute-start.8 = (f32[40,128]{1,0:T(8,128)S(1)}, f32[40,128]{1,0:T(8,128)S(1)}, u32[]{:S(2)}, u32[]{:S(2)}) collective-permute-start(f32[40,128]{1,0:T(8,128)S(1)} %get-tuple-element.45), channel_id=1, source_target_pairs={{0,1},{1,0},{2,3},{3,2},{4,5},{5,4},{6,7},{7,6},{8,9},{9,8},{10,11... | collective-permute-start | bytes 61448 | tf_op jit(solution)/shard_map/ppermute | solution.py:31

commit v7 on v6

--- a/solution.py
+++ b/solution.py
@@ -178,6 +178,10 @@
     return jnp.concatenate([high, low, high], axis=0).astype(bf16)
 
 
+def lane_ids(rows, count):
+    return lax.broadcasted_iota(jnp.int32, (rows, count), 1)
+
+
 def onehot(ids, count):
     return jnp.where(lax.broadcasted_iota(jnp.int32, (count, ids.shape[1]), 0) == ids, 1.0, 0.0)
 
@@ -186,7 +190,7 @@
     wide, back, first, last = weights
     slots = rows.shape[1]
     sources = src_pos.shape[1]
-    channels = feats.shape[0]
+    channels = feats.shape[0] // 2
     hidden = last.shape[1] // 3
     parts = len(degree)
     atoms = (cot_refs[0].shape[0] - sublanes) // parts
@@ -198,7 +202,9 @@
     offset = rows[4:6].astype(f32) * domain_side
 
     tgt_pos = [jnp.concatenate(pieces(ref[parts * atoms :, 0:atoms], 3), axis=0) for ref in cot_refs]
-    from_src = dot(src_pos, src_hot)
+    gathered = dot(jnp.concatenate([feats, src_pos], axis=0), src_hot)
+    from_src = gathered[2 * channels :]
+    gathered = gathered[0:channels] + gathered[channels : 2 * channels]
     from_tgt = dot(jnp.concatenate(tgt_pos, axis=1).astype(bf16), tgt_hot)
     from_src = from_src[0:8] + from_src[8:16] + from_src[16:24]
     from_tgt = from_tgt[0:8] + from_tgt[8:16] + from_tgt[16:24]
@@ -225,8 +231,6 @@
     act = before * gate
     d_act = gate * (1.0 + before * (1.0 - gate))
     radial = dot(wide, thrice(act))
-    gathered = dot(feats, jnp.concatenate([src_hot, src_hot], axis=0))
-
     root3, root5, root15 = math.sqrt(3.0), math.sqrt(5.0), math.sqrt(15.0)
     shapes = [
         None, root3 * x, root3 * y, root3 * z, root15 * x * y, root15 * y * z,
@@ -235,6 +239,11 @@
     twice = lax.broadcasted_iota(jnp.int32, (2 * targets, slots), 0)
     twice = (twice // (2 * atoms)) * atoms + lax.rem(twice, atoms)
     twice = jnp.where(twice == rows[1:2], 1.0, 0.0).astype(bf16)
+    blocks = []
+    for ref in cot_refs:
+        block = [ref[m * atoms : (m + 1) * atoms] for m in range(parts)]
+        blocks += pieces(jnp.concatenate(block, axis=1), 2)
+    cots = dot_cols(jnp.concatenate(blocks, axis=0).astype(bf16), twice)
     d_shapes = [None] * parts
     d_radial = []
     through = None
@@ -244,10 +253,7 @@
         with_feats = own * gathered
         total = None
         for m in range(low, high):
-            blocks = []
-            for ref in cot_refs:
-                blocks += pieces(ref[m * atoms : (m + 1) * atoms], 2)
-            cot = dot_cols(jnp.concatenate(blocks, axis=0).astype(bf16), twice)
+            cot = cots[m * channels : (m + 1) * channels]
             if m:
                 d_shapes[m] = jnp.sum(with_feats * cot, axis=0, keepdims=True) * env
                 cot = cot * shapes[m]
@@ -274,9 +280,14 @@
          jnp.zeros((sublanes - 3, slots), f32)], axis=0,
     )
     grad = jnp.concatenate(pieces(grad, 2), axis=0).astype(bf16)
-    pos_src = dot_rows(grad, src_hot)
-    pos_tgt = dot_rows(grad, tgt_hot)
-    feat_src = sum(dot_rows(src_hot, p.astype(bf16)) for p in pieces(through, 2))
+    ids = rows.T
+    src_home = jnp.where(lane_ids(slots, sources) == ids[:, 0:1], 1.0, 0.0).astype(bf16)
+    tgt_home = jnp.where(lane_ids(slots, targets) == ids[:, 1:2], 1.0, 0.0).astype(bf16)
+    pos_tgt = dot(grad, tgt_home)
+    through = [p.astype(bf16) for p in pieces(through, 2)]
+    home = dot(jnp.concatenate([*through, grad], axis=0), src_home)
+    feat_src = (home[0:channels] + home[channels : 2 * channels]).T
+    pos_src = home[2 * channels :]
     return pos_src[0:8] + pos_src[8:16], -(pos_tgt[0:8] + pos_tgt[8:16]), feat_src
 
 
@@ -308,7 +319,7 @@
         place[:, table * atoms : (table + 1) * atoms] = ref[atoms:, 0:atoms]
     src_pos_ref[...] = jnp.concatenate(pieces(place[...], 3), axis=0).astype(bf16)
     feats = jnp.concatenate([ref[0:atoms] for ref in views], axis=0).T
-    feats_ref[...] = jnp.concatenate(pieces(feats, 2), axis=1).astype(bf16)
+    feats_ref[...] = jnp.concatenate(pieces(feats, 2), axis=0).astype(bf16)
     rows = all_rows(rows_ref, y_ref, start, chunks)
     pos, pos_tgt, feat = slot_grads(
         rows, [cot_ref], src_pos_ref[...], feats_ref[...], weights, orders
@@ -437,7 +448,7 @@
     )
     blocks = [own, y] + [link.swap(two, "gx") for link in gx_links]
     table = (
-        sds((3 * sublanes, 2 * sources), bf16), sds((channels, 4 * sources), bf16),
+        sds((3 * sublanes, 2 * sources), bf16), sds((2 * channels, 2 * sources), bf16),
         sds((sublanes, 2 * sources), f32), sds((2 * sources, channels), f32),
     )
     held = call(

time: 28.4 us -> 28.2 us (level)
  no operation moved by 1% of the time
where the time goes in v7:
time: 28.2 us; the launch traced here: 28 us
  starting transfers between devices  13.1 us (46%)
  waiting for transfers between devices  7.88 us (28%)
  Pallas kernels  6.21 us (22%)
  between operations  0.78 us (3%)
    ppermute x11, starting transfers between devices, swap(): lax.ppermute(value, axis, [(i, (i + self.delta(i)) % n) for i in range(n)])  13.1 us
    ppermute x11, waiting for transfers between devices, swap(): lax.ppermute(value, axis, [(i, (i + self.delta(i)) % n) for i in range(n)])  7.88 us
    pallas_call x8, Pallas kernels, call(): pl.pallas_call(kernel, out_shape=out_shape, in_specs=[vmem] * len(operand...  6.21 us
  transfers between devices with their start and end apart: 11, of which 8 were waited for; matrix products, arithmetic and copies ran while one was open for 0% of the time, Pallas kernels for 7%

profile of v7, /device:TPU:0, one launch (start us, length us, event | category | flops | bytes accessed | tf_op | source)
XLA Modules:
  0.0 28.0 jit_solution(1847284867108316504)
XLA Ops:
  0.6 0.0 copy-start.2
  0.6 0.0 copy-start.3
  0.7 0.0 copy-start.4
  0.7 0.0 copy-start.5
  0.7 0.0 copy-start.6
  0.7 1.8 %pack.1 = (f32[40,128]{1,0:T(8,128)}, f32[72,128]{1,0:T(8,128)}, f32[296,128]{1,0:T(8,128)}) custom-call(f32[1,3,1,32]{3,2,1,0:T(1,128)} %bitcast.14, f32[1,1,32,128]{3,2,1,0:T(8,128)} %feat_ref.1, f32[1,1,32,1152]{3,2,1,0:T(8,128)} %cot_ref.1, s32[1,5,5,1,32]{4,3,2,1,0:T(1,128)} %bitcast.6, s32[1,5,5,1,32]{4,3,2,1,0:T(1,128)} %bitcast.8, ...), custom_call_target="tpu_custom_call" | custom-call | tf_op jit(solution)/shard_map/pack/pallas_call | solution.py:385
  2.5 3.0 %collective-permute-start = (f32[72,128]{1,0:T(8,128)}, f32[72,128]{1,0:T(8,128)S(1)}, u32[]{:S(2)}, u32[]{:S(2)}) collective-permute-start(f32[72,128]{1,0:T(8,128)} %get-tuple-element.31), channel_id=1, source_target_pairs={{0,1},{1,0},{2,3},{3,2},{4,5},{5,4},{6,7},{7,6},{8,9},{9,8},{10,11... | collective-permute-start | bytes 110600 | tf_op jit(solution)/shard_map/ppermute | solution.py:31
  5.5 0.2 prepare.1
  5.7 3.7 %collective-permute-start.5 = (f32[296,128]{1,0:T(8,128)S(1)}, f32[296,128]{1,0:T(8,128)S(1)}, u32[]{:S(2)}, u32[]{:S(2)}) collective-permute-start(f32[296,128]{1,0:T(8,128)S(1)} %copy-done), channel_id=1, source_target_pairs={{0,6},{1,7},{2,4},{3,5},{4,2},{5,3},{6,0},{7,1},{8,14},{9,15},{10,... | collective-permute-start | bytes 454664 | tf_op jit(solution)/shard_map/ppermute | solution.py:31
  9.4 0.0 collective-permute-start.4
  9.4 0.0 collective-permute-done.refs_1_.refs_4_.refs_6_
  9.4 1.6 %collective-permute-start.3 = (f32[80,128]{1,0:T(8,128)S(1)}, f32[80,128]{1,0:T(8,128)S(1)}, u32[]{:S(2)}, u32[]{:S(2)}) collective-permute-start(f32[80,128]{1,0:T(8,128)S(1)} %stack.1), channel_id=1, source_target_pairs={{0,16},{8,24},{16,0},{24,8},{1,17},{9,25},{17,1},{25,9},{2,18},{10... | collective-permute-start | bytes 122888 | tf_op jit(solution)/shard_map/ppermute | solution.py:31
  11.0 0.0 collective-permute-start.2
  11.0 0.6 %collective-permute-start.1 = (f32[80,128]{1,0:T(8,128)S(1)}, f32[80,128]{1,0:T(8,128)S(1)}, u32[]{:S(2)}, u32[]{:S(2)}) collective-permute-start(f32[80,128]{1,0:T(8,128)S(1)} %stack.1), channel_id=1, source_target_pairs={{0,8},{8,0},{16,24},{24,16},{1,9},{9,1},{17,25},{25,17},{2,10},{10... | collective-permute-start | bytes 122888 | tf_op jit(solution)/shard_map/ppermute | solution.py:31
  11.6 1.9 %collective-permute-done.3.refs_9_ = f32[80,128]{1,0:T(8,128)S(1)} collective-permute-done((f32[80,128]{1,0:T(8,128)S(1)}, f32[80,128]{1,0:T(8,128)S(1)}, u32[]{:S(2)}, u32[]{:S(2)}) %collective-permute-start.3) | collective-permute-done | bytes 40992 | tf_op jit(solution)/shard_map/ppermute | solution.py:31
  13.5 0.9 %collective-permute-done.2.refs_8_ = f32[80,128]{1,0:T(8,128)S(1)} collective-permute-done((f32[80,128]{1,0:T(8,128)S(1)}, f32[80,128]{1,0:T(8,128)S(1)}, u32[]{:S(2)}, u32[]{:S(2)}) %collective-permute-start.2) | collective-permute-done | bytes 40992 | tf_op jit(solution)/shard_map/ppermute | solution.py:31
  14.4 0.0 collective-permute-done.1.refs_7_
  14.4 1.8 %early_tiles.1 = (bf16[24,256]{1,0:T(8,128)(2,1)S(1)}, bf16[256,256]{1,0:T(8,128)(2,1)S(1)}, f32[8,256]{1,0:T(8,128)S(1)}, f32[256,128]{1,0:T(8,128)S(1)}) custom-call(s32[8,384]{1,0:T(8,128)S(1)} %get-tuple-element.32.rows_ref, bf16[384,96]{1,0:T(8,128)(2,1)S(1)} %get-tuple-element.27.refs_0_, bf16[64,768]{1,0:T(8,128)(2,1)S(1)} %get-tuple-element.28.refs_1_, ...), custom_call_target="tpu_custom_call" | custom-call | tf_op jit(solution)/shard_map/early_tiles/pallas_call | solution.py:385
  16.2 0.0 collective-permute-done.5.refs_10_
  16.2 0.2 collective-permute-done.4.refs_9_
  16.4 1.8 %late_tiles.1 = (f32[160,128]{1,0:T(8,128)S(1)}, f32[160,128]{1,0:T(8,128)S(1)}, f32[64,128]{1,0:T(8,128)S(1)}, f32[64,128]{1,0:T(8,128)S(1)}) custom-call(s32[8,512]{1,0:T(8,128)S(1)} %get-tuple-element.26.rows_ref, bf16[384,96]{1,0:T(8,128)(2,1)S(1)} %get-tuple-element.27.refs_0_, bf16[64,768]{1,0:T(8,128)(2,1)S(1)} %get-tuple-element.28.refs_1_, ...), custom_call_target="tpu_custom_call" | custom-call | tf_op jit(solution)/shard_map/late_tiles/pallas_call | solution.py:385
  18.2 0.1 collective-permute-start.6
  18.3 1.3 %collective-permute-done.6.refs_1_ = f32[160,128]{1,0:T(8,128)S(1)} collective-permute-done((f32[160,128]{1,0:T(8,128)S(1)}, f32[160,128]{1,0:T(8,128)S(1)}, u32[]{:S(2)}, u32[]{:S(2)}) %collective-permute-start.6) | collective-permute-done | bytes 81952 | tf_op jit(solution)/shard_map/ppermute | solution.py:31
  19.6 1.6 %collective-permute-start.7 = (f32[80,128]{1,0:T(8,128)S(1)}, f32[80,128]{1,0:T(8,128)S(1)}, u32[]{:S(2)}, u32[]{:S(2)}) collective-permute-start(f32[80,128]{1,0:T(8,128)S(1)} %get-tuple-element.43), channel_id=1, source_target_pairs={{0,16},{8,24},{16,0},{24,8},{1,17},{9,25},{17,1},{25,9},{2,18},{10... | collective-permute-start | bytes 122888 | tf_op jit(solution)/shard_map/ppermute | solution.py:31
  21.1 1.8 %collective-permute-start.9 = (f32[64,128]{1,0:T(8,128)S(1)}, f32[64,128]{1,0:T(8,128)S(1)}, u32[]{:S(2)}, u32[]{:S(2)}) collective-permute-start(f32[64,128]{1,0:T(8,128)S(1)} %get-tuple-element.46), channel_id=1, source_target_pairs={{0,6},{1,7},{2,4},{3,5},{4,2},{5,3},{6,0},{7,1},{8,14},{9,15},{10,... | collective-permute-start | bytes 98312 | tf_op jit(solution)/shard_map/ppermute | solution.py:31
  22.9 0.0 collective-permute-start.10
  22.9 0.8 %collective-permute-done.7.refs_1_ = f32[80,128]{1,0:T(8,128)S(1)} collective-permute-done((f32[80,128]{1,0:T(8,128)S(1)}, f32[80,128]{1,0:T(8,128)S(1)}, u32[]{:S(2)}, u32[]{:S(2)}) %collective-permute-start.7) | collective-permute-done | bytes 40992 | tf_op jit(solution)/shard_map/ppermute | solution.py:31
  23.6 0.9 %collective-permute-start.8 = (f32[40,128]{1,0:T(8,128)S(1)}, f32[40,128]{1,0:T(8,128)S(1)}, u32[]{:S(2)}, u32[]{:S(2)}) collective-permute-start(f32[40,128]{1,0:T(8,128)S(1)} %get-tuple-element.45), channel_id=1, source_target_pairs={{0,1},{1,0},{2,3},{3,2},{4,5},{5,4},{6,7},{7,6},{8,9},{9,8},{10,11... | collective-permute-start | bytes 61448 | tf_op jit(solution)/shard_map/ppermute | solution.py:31
  24.6 2.4 %collective-permute-done.9.refs_2_ = f32[64,128]{1,0:T(8,128)S(1)} collective-permute-done((f32[64,128]{1,0:T(8,128)S(1)}, f32[64,128]{1,0:T(8,128)S(1)}, u32[]{:S(2)}, u32[]{:S(2)}) %collective-permute-start.9) | collective-permute-done | bytes 32800 | tf_op jit(solution)/shard_map/ppermute | solution.py:31
  26.9 0.2 collective-permute-done.10.refs_3_
  27.1 0.3 %collective-permute-done.8.refs_1_ = f32[40,128]{1,0:T(8,128)S(1)} collective-permute-done((f32[40,128]{1,0:T(8,128)S(1)}, f32[40,128]{1,0:T(8,128)S(1)}, u32[]{:S(2)}, u32[]{:S(2)}) %collective-permute-start.8) | collective-permute-done | bytes 20512 | tf_op jit(solution)/shard_map/ppermute | solution.py:31
  27.4 0.6 %sums.1 = (f32[1,3,1,32]{3,2,1,0:T(1,128)}, f32[1,1,32,128]{3,2,1,0:T(8,128)}) custom-call(f32[40,128]{1,0:T(8,128)S(1)} %get-tuple-element.44.refs_0_, f32[40,128]{1,0:T(8,128)S(1)} %collective-permute-done.8.refs_1_, f32[64,128]{1,0:T(8,128)S(1)} %collective-permute-done.9.refs_2_, f32[64,128]{1,0:T(8,128)S(1)} %collective-permute-done.10.refs_3_), custom_call_target="tpu_custom_call" | custom-call | tf_op jit(solution)/shard_map/sums/pallas_call | solution.py:385
  (16 shorter events, 0.0 us)
Async XLA Ops:
  0.6 4.9 %copy-start.2 = (s32[1,1,5,5,32]{4,1,3,2,0:T(1,128)S(1)}, s32[1,1,5,5,32]{4,1,3,2,0:T(1,128)}, u32[]{:S(2)}) copy-start(s32[1,1,5,5,32]{4,1,3,2,0:T(1,128)} %param.13) | copy-start | bytes 9604
  0.6 4.8 %copy-start.3 = (s32[1,1,5,5,32]{4,1,3,2,0:T(1,128)S(1)}, s32[1,1,5,5,32]{4,1,3,2,0:T(1,128)}, u32[]{:S(2)}) copy-start(s32[1,1,5,5,32]{4,1,3,2,0:T(1,128)} %param.14) | copy-start | bytes 9604
  0.7 4.8 %copy-start.4 = (s32[1,1,5,5,32]{4,1,3,2,0:T(1,128)S(1)}, s32[1,1,5,5,32]{4,1,3,2,0:T(1,128)}, u32[]{:S(2)}) copy-start(s32[1,1,5,5,32]{4,1,3,2,0:T(1,128)} %param.15) | copy-start | bytes 9604
  0.7 4.8 %copy-start.5 = (s32[1,1,5,5,32]{4,1,3,2,0:T(1,128)S(1)}, s32[1,1,5,5,32]{4,1,3,2,0:T(1,128)}, u32[]{:S(2)}) copy-start(s32[1,1,5,5,32]{4,1,3,2,0:T(1,128)} %param.16) | copy-start | bytes 9604
  0.7 4.8 %copy-start.6 = (f32[32,384]{1,0:T(8,128)S(1)}, f32[32,384]{1,0:T(8,128)}, u32[]{:S(2)}) copy-start(f32[32,384]{1,0:T(8,128)} %out_ref.1) | copy-start | bytes 147460
  0.7 4.8 %copy-start.7 = (f32[10,32]{1,0:T(8,128)S(1)}, f32[10,32]{1,0:T(8,128)}, u32[]{:S(2)}) copy-start(f32[10,32]{1,0:T(8,128)} %emb_ref.1) | copy-start | bytes 3844
  0.7 4.8 %copy-start.8 = (f32[8,32]{1,0:T(8,128)S(1)}, f32[8,32]{1,0:T(8,128)}, u32[]{:S(2)}) copy-start(f32[8,32]{1,0:T(8,128)} %in_ref.1) | copy-start | bytes 3076
  2.5 3.2 %copy-start = (f32[296,128]{1,0:T(8,128)S(1)}, f32[296,128]{1,0:T(8,128)}, u32[]{:S(2)}) copy-start(f32[296,128]{1,0:T(8,128)} %get-tuple-element.39.refs_10_) | copy-start | bytes 454660
  2.5 6.9 %copy-start.1 = (f32[40,128]{1,0:T(8,128)S(1)}, f32[40,128]{1,0:T(8,128)}, u32[]{:S(2)}) copy-start(f32[40,128]{1,0:T(8,128)} %get-tuple-element.33.refs_0_.refs_5_) | copy-start | bytes 61444
  2.5 6.9 %collective-permute-start = (f32[72,128]{1,0:T(8,128)}, f32[72,128]{1,0:T(8,128)S(1)}, u32[]{:S(2)}, u32[]{:S(2)}) collective-permute-start(f32[72,128]{1,0:T(8,128)} %get-tuple-element.31), channel_id=1, source_target_pairs={{0,1},{1,0},{2,3},{3,2},{4,5},{5,4},{6,7},{7,6},{8,9},{9,8},{10,11... | collective-permute-start | bytes 110600 | tf_op jit(solution)/shard_map/ppermute | solution.py:31
  5.7 10.5 %collective-permute-start.5 = (f32[296,128]{1,0:T(8,128)S(1)}, f32[296,128]{1,0:T(8,128)S(1)}, u32[]{:S(2)}, u32[]{:S(2)}) collective-permute-start(f32[296,128]{1,0:T(8,128)S(1)} %copy-done), channel_id=1, source_target_pairs={{0,6},{1,7},{2,4},{3,5},{4,2},{5,3},{6,0},{7,1},{8,14},{9,15},{10,... | collective-permute-start | bytes 454664 | tf_op jit(solution)/shard_map/ppermute | solution.py:31
  9.4 7.0 %collective-permute-start.4 = (f32[296,128]{1,0:T(8,128)S(1)}, f32[296,128]{1,0:T(8,128)S(1)}, u32[]{:S(2)}, u32[]{:S(2)}) collective-permute-start(f32[296,128]{1,0:T(8,128)S(1)} %copy-done), channel_id=1, source_target_pairs={{0,2},{1,3},{2,0},{3,1},{4,6},{5,7},{6,4},{7,5},{8,10},{9,11},{10,... | collective-permute-start | bytes 454664 | tf_op jit(solution)/shard_map/ppermute | solution.py:31
  9.4 4.1 %collective-permute-start.3 = (f32[80,128]{1,0:T(8,128)S(1)}, f32[80,128]{1,0:T(8,128)S(1)}, u32[]{:S(2)}, u32[]{:S(2)}) collective-permute-start(f32[80,128]{1,0:T(8,128)S(1)} %stack.1), channel_id=1, source_target_pairs={{0,16},{8,24},{16,0},{24,8},{1,17},{9,25},{17,1},{25,9},{2,18},{10... | collective-permute-start | bytes 122888 | tf_op jit(solution)/shard_map/ppermute | solution.py:31
  11.0 3.4 %collective-permute-start.2 = (f32[80,128]{1,0:T(8,128)S(1)}, f32[80,128]{1,0:T(8,128)S(1)}, u32[]{:S(2)}, u32[]{:S(2)}) collective-permute-start(f32[80,128]{1,0:T(8,128)S(1)} %stack.1), channel_id=1, source_target_pairs={{0,24},{8,16},{16,8},{24,0},{1,25},{9,17},{17,9},{25,1},{2,26},{10... | collective-permute-start | bytes 122888 | tf_op jit(solution)/shard_map/ppermute | solution.py:31
  11.0 3.4 %collective-permute-start.1 = (f32[80,128]{1,0:T(8,128)S(1)}, f32[80,128]{1,0:T(8,128)S(1)}, u32[]{:S(2)}, u32[]{:S(2)}) collective-permute-start(f32[80,128]{1,0:T(8,128)S(1)} %stack.1), channel_id=1, source_target_pairs={{0,8},{8,0},{16,24},{24,16},{1,9},{9,1},{17,25},{25,17},{2,10},{10... | collective-permute-start | bytes 122888 | tf_op jit(solution)/shard_map/ppermute | solution.py:31
  18.2 1.3 %collective-permute-start.6 = (f32[160,128]{1,0:T(8,128)S(1)}, f32[160,128]{1,0:T(8,128)S(1)}, u32[]{:S(2)}, u32[]{:S(2)}) collective-permute-start(f32[160,128]{1,0:T(8,128)S(1)} %get-tuple-element.41), channel_id=1, source_target_pairs={{0,8},{8,0},{16,24},{24,16},{1,9},{9,1},{17,25},{25,17},{2,10},{10... | collective-permute-start | bytes 245768 | tf_op jit(solution)/shard_map/ppermute | solution.py:31
  19.6 4.1 %collective-permute-start.7 = (f32[80,128]{1,0:T(8,128)S(1)}, f32[80,128]{1,0:T(8,128)S(1)}, u32[]{:S(2)}, u32[]{:S(2)}) collective-permute-start(f32[80,128]{1,0:T(8,128)S(1)} %get-tuple-element.43), channel_id=1, source_target_pairs={{0,16},{8,24},{16,0},{24,8},{1,17},{9,25},{17,1},{25,9},{2,18},{10... | collective-permute-start | bytes 122888 | tf_op jit(solution)/shard_map/ppermute | solution.py:31
  21.1 5.8 %collective-permute-start.9 = (f32[64,128]{1,0:T(8,128)S(1)}, f32[64,128]{1,0:T(8,128)S(1)}, u32[]{:S(2)}, u32[]{:S(2)}) collective-permute-start(f32[64,128]{1,0:T(8,128)S(1)} %get-tuple-element.46), channel_id=1, source_target_pairs={{0,6},{1,7},{2,4},{3,5},{4,2},{5,3},{6,0},{7,1},{8,14},{9,15},{10,... | collective-permute-start | bytes 98312 | tf_op jit(solution)/shard_map/ppermute | solution.py:31
  22.9 4.3 %collective-permute-start.10 = (f32[64,128]{1,0:T(8,128)S(1)}, f32[64,128]{1,0:T(8,128)S(1)}, u32[]{:S(2)}, u32[]{:S(2)}) collective-permute-start(f32[64,128]{1,0:T(8,128)S(1)} %get-tuple-element.47), channel_id=1, source_target_pairs={{0,2},{1,3},{2,0},{3,1},{4,6},{5,7},{6,4},{7,5},{8,10},{9,11},{10,... | collective-permute-start | bytes 98312 | tf_op jit(solution)/shard_map/ppermute | solution.py:31
  23.6 3.8 %collective-permute-start.8 = (f32[40,128]{1,0:T(8,128)S(1)}, f32[40,128]{1,0:T(8,128)S(1)}, u32[]{:S(2)}, u32[]{:S(2)}) collective-permute-start(f32[40,128]{1,0:T(8,128)S(1)} %get-tuple-element.45), channel_id=1, source_target_pairs={{0,1},{1,0},{2,3},{3,2},{4,5},{5,4},{6,7},{7,6},{8,9},{9,8},{10,11... | collective-permute-start | bytes 61448 | tf_op jit(solution)/shard_map/ppermute | solution.py:31

commit v8 on v7

--- a/solution.py
+++ b/solution.py
@@ -396,6 +396,16 @@
     )(*operands)
 
 
+def diagonal(value, gx_link, gy_link):
+    n, m = gx_link.peers, gy_link.peers
+    pairs = []
+    for i in range(n):
+        for j in range(m):
+            to = ((i + gx_link.delta(i)) % n) * m + (j + gy_link.delta(j)) % m
+            pairs.append((i * m + j, to))
+    return lax.ppermute(value, ("gx", "gy"), pairs)
+
+
 def local(
     gx_size, gy_size, positions, features, cotangent, nbr_src, nbr_tgt, pair_mask, pair_species,
     w_in, species_emb, w_out,
@@ -425,7 +435,7 @@
     many = len(gx_links) + 1
     tables = [(at, 0) if not l else (1 + l, at) for at in range(2) for l in range(many)]
     if gx_size == 4:
-        homes = ((0, many, 3, many + 3), (1, many + 1, 2, many + 2))
+        homes = ((0, 3, many, many + 3), (1, 2, many + 1, many + 2))
     else:
         homes = tuple((table, many + table) for table in range(many))
     early_rows, late_rows, *weights = call(
@@ -466,17 +476,19 @@
     back_gy = [link.swap(value, "gy") for link, value in zip(far_links, (far, near))]
     if gx_size == 4:
         came = gx_links[0].swap(sent[1], "gx")
-        near_chip, far_chip = call(
-            functools.partial(add_kernel, 2), "add", (sds((2 * block, channels), f32),) * 2,
-            (sent[0], came),
+        own, x, y, xy = call(
+            functools.partial(add_kernel, 2), "add", (gx_pack,) * 4, (sent[0], came)
         )
-        sent, came = [near_chip], [gx_links[2].swap(far_chip, "gx")]
+        back = [
+            own, diagonal(xy, gx_links[2], gy_links[0]), gx_links[2].swap(x, "gx"),
+            gy_links[0].swap(y, "gy"),
+        ]
     else:
         came = [link.swap(value, "gx") for link, value in zip(gx_links, sent[1:])]
-    own, y = call(
-        functools.partial(add_kernel, 1 + len(came)), "add", (gx_pack,) * 2, (sent[0], *came)
-    )
-    back = [own, gy_links[0].swap(y, "gy")]
+        own, y = call(
+            functools.partial(add_kernel, len(sent)), "add", (gx_pack,) * 2, (sent[0], *came)
+        )
+        back = [own, gy_links[0].swap(y, "gy")]
     pos, feat = call(
         functools.partial(sum_kernel, len(back)), "sums",
         (sds(by_axis.shape, f32), sds(features.shape, f32)),

time: 28.2 us -> 28.1 us (level)
  waiting for transfers between devices: 7.88 us -> 6.27 us
  starting transfers between devices: 13.1 us -> 14.6 us
    ppermute x0 -> x1, starting transfers between devices: none -> 2.47 us  [diagonal(): return lax.ppermute(value, ('gx', 'gy'), pairs)]
    ppermute x11, waiting for transfers between devices: 7.88 us -> 5.49 us  [swap(): lax.ppermute(value, axis, [(i, (i + self.delta(i)) % n) for i in range(n)])]
    ppermute x11, starting transfers between devices: 13.1 us -> 12.1 us  [swap(): lax.ppermute(value, axis, [(i, (i + self.delta(i)) % n) for i in range(n)])]
    ppermute x0 -> x1, waiting for transfers between devices: none -> 0.77 us  [diagonal(): return lax.ppermute(value, ('gx', 'gy'), pairs)]
    pallas_call x8 -> x7, Pallas kernels: 6.21 us -> 6.22 us  [call(): pl.pallas_call(kernel, out_shape=out_shape, in_specs=[vmem] * len(operand...]
  transfers between devices with their start and end apart: 11 -> 12, of which waited for: 8 -> 8; matrix products, arithmetic and copies ran while one was open for 0% -> 0% of each run, Pallas kernels for 7% -> 7%
where the time goes in v8:
time: 28.1 us; the launch traced here: 27.9 us
  starting transfers between devices  14.6 us (52%)
  waiting for transfers between devices  6.27 us (22%)
  Pallas kernels  6.22 us (22%)
  between operations  0.78 us (3%)
    ppermute x11, starting transfers between devices, swap(): lax.ppermute(value, axis, [(i, (i + self.delta(i)) % n) for i in range(n)])  12.1 us
    pallas_call x7, Pallas kernels, call(): pl.pallas_call(kernel, out_shape=out_shape, in_specs=[vmem] * len(operand...  6.22 us
    ppermute x11, waiting for transfers between devices, swap(): lax.ppermute(value, axis, [(i, (i + self.delta(i)) % n) for i in range(n)])  5.49 us
    ppermute x1, starting transfers between devices, diagonal(): return lax.ppermute(value, ('gx', 'gy'), pairs)  2.47 us
    ppermute x1, waiting for transfers between devices, diagonal(): return lax.ppermute(value, ('gx', 'gy'), pairs)  0.77 us
  transfers between devices with their start and end apart: 12, of which 8 were waited for; matrix products, arithmetic and copies ran while one was open for 0% of the time, Pallas kernels for 7%

profile of v8, /device:TPU:0, one launch (start us, length us, event | category | flops | bytes accessed | tf_op | source)
XLA Modules:
  0.0 27.9 jit_solution(13512695229545420266)
XLA Ops:
  0.6 0.0 copy-start.2
  0.6 0.0 copy-start.3
  0.7 1.8 %pack.1 = (f32[40,128]{1,0:T(8,128)}, f32[72,128]{1,0:T(8,128)}, f32[296,128]{1,0:T(8,128)}) custom-call(f32[1,3,1,32]{3,2,1,0:T(1,128)} %bitcast.14, f32[1,1,32,128]{3,2,1,0:T(8,128)} %feat_ref.1, f32[1,1,32,1152]{3,2,1,0:T(8,128)} %cot_ref.1, s32[1,5,5,1,32]{4,3,2,1,0:T(1,128)} %bitcast.6, s32[1,5,5,1,32]{4,3,2,1,0:T(1,128)} %bitcast.8, ...), custom_call_target="tpu_custom_call" | custom-call | tf_op jit(solution)/shard_map/pack/pallas_call | solution.py:385
  2.5 3.0 %collective-permute-start = (f32[72,128]{1,0:T(8,128)}, f32[72,128]{1,0:T(8,128)S(1)}, u32[]{:S(2)}, u32[]{:S(2)}) collective-permute-start(f32[72,128]{1,0:T(8,128)} %get-tuple-element.31), channel_id=1, source_target_pairs={{0,1},{1,0},{2,3},{3,2},{4,5},{5,4},{6,7},{7,6},{8,9},{9,8},{10,11... | collective-permute-start | bytes 110600 | tf_op jit(solution)/shard_map/ppermute | solution.py:31
  5.5 0.0 copy-done.3
  5.5 0.2 prepare.1
  5.7 3.7 %collective-permute-start.5 = (f32[296,128]{1,0:T(8,128)S(1)}, f32[296,128]{1,0:T(8,128)S(1)}, u32[]{:S(2)}, u32[]{:S(2)}) collective-permute-start(f32[296,128]{1,0:T(8,128)S(1)} %copy-done), channel_id=1, source_target_pairs={{0,6},{1,7},{2,4},{3,5},{4,2},{5,3},{6,0},{7,1},{8,14},{9,15},{10,... | collective-permute-start | bytes 454664 | tf_op jit(solution)/shard_map/ppermute | solution.py:31
  9.4 0.0 collective-permute-start.4
  9.4 0.0 collective-permute-done.refs_1_.refs_4_.refs_6_
  9.4 1.6 %collective-permute-start.3 = (f32[80,128]{1,0:T(8,128)S(1)}, f32[80,128]{1,0:T(8,128)S(1)}, u32[]{:S(2)}, u32[]{:S(2)}) collective-permute-start(f32[80,128]{1,0:T(8,128)S(1)} %stack.1), channel_id=1, source_target_pairs={{0,16},{8,24},{16,0},{24,8},{1,17},{9,25},{17,1},{25,9},{2,18},{10... | collective-permute-start | bytes 122888 | tf_op jit(solution)/shard_map/ppermute | solution.py:31
  11.0 0.0 collective-permute-start.2
  11.0 0.6 %collective-permute-start.1 = (f32[80,128]{1,0:T(8,128)S(1)}, f32[80,128]{1,0:T(8,128)S(1)}, u32[]{:S(2)}, u32[]{:S(2)}) collective-permute-start(f32[80,128]{1,0:T(8,128)S(1)} %stack.1), channel_id=1, source_target_pairs={{0,8},{8,0},{16,24},{24,16},{1,9},{9,1},{17,25},{25,17},{2,10},{10... | collective-permute-start | bytes 122888 | tf_op jit(solution)/shard_map/ppermute | solution.py:31
  11.6 1.9 %collective-permute-done.3.refs_9_ = f32[80,128]{1,0:T(8,128)S(1)} collective-permute-done((f32[80,128]{1,0:T(8,128)S(1)}, f32[80,128]{1,0:T(8,128)S(1)}, u32[]{:S(2)}, u32[]{:S(2)}) %collective-permute-start.3) | collective-permute-done | bytes 40992 | tf_op jit(solution)/shard_map/ppermute | solution.py:31
  13.5 0.9 %collective-permute-done.2.refs_8_ = f32[80,128]{1,0:T(8,128)S(1)} collective-permute-done((f32[80,128]{1,0:T(8,128)S(1)}, f32[80,128]{1,0:T(8,128)S(1)}, u32[]{:S(2)}, u32[]{:S(2)}) %collective-permute-start.2) | collective-permute-done | bytes 40992 | tf_op jit(solution)/shard_map/ppermute | solution.py:31
  14.4 0.0 collective-permute-done.1.refs_7_
  14.4 1.8 %early_tiles.1 = (bf16[24,256]{1,0:T(8,128)(2,1)S(1)}, bf16[256,256]{1,0:T(8,128)(2,1)S(1)}, f32[8,256]{1,0:T(8,128)S(1)}, f32[256,128]{1,0:T(8,128)S(1)}) custom-call(s32[8,384]{1,0:T(8,128)S(1)} %get-tuple-element.32.rows_ref, bf16[384,96]{1,0:T(8,128)(2,1)S(1)} %get-tuple-element.27.refs_0_, bf16[64,768]{1,0:T(8,128)(2,1)S(1)} %get-tuple-element.28.refs_1_, ...), custom_call_target="tpu_custom_call" | custom-call | tf_op jit(solution)/shard_map/early_tiles/pallas_call | solution.py:385
  16.2 0.0 collective-permute-done.5.refs_10_
  16.2 0.2 collective-permute-done.4.refs_9_
  16.4 1.8 %late_tiles.1 = (f32[160,128]{1,0:T(8,128)S(1)}, f32[160,128]{1,0:T(8,128)S(1)}, f32[64,128]{1,0:T(8,128)S(1)}, f32[64,128]{1,0:T(8,128)S(1)}) custom-call(s32[8,512]{1,0:T(8,128)S(1)} %get-tuple-element.26.rows_ref, bf16[384,96]{1,0:T(8,128)(2,1)S(1)} %get-tuple-element.27.refs_0_, bf16[64,768]{1,0:T(8,128)(2,1)S(1)} %get-tuple-element.28.refs_1_, ...), custom_call_target="tpu_custom_call" | custom-call | tf_op jit(solution)/shard_map/late_tiles/pallas_call | solution.py:385
  18.2 0.1 collective-permute-start.6
  18.3 2.1 %collective-permute-start.10 = (f32[64,128]{1,0:T(8,128)S(1)}, f32[64,128]{1,0:T(8,128)S(1)}, u32[]{:S(2)}, u32[]{:S(2)}) collective-permute-start(f32[64,128]{1,0:T(8,128)S(1)} %get-tuple-element.46), channel_id=1, source_target_pairs={{0,6},{1,7},{2,4},{3,5},{4,2},{5,3},{6,0},{7,1},{8,14},{9,15},{10,... | collective-permute-start | bytes 98312 | tf_op jit(solution)/shard_map/ppermute | solution.py:31
  20.4 0.0 collective-permute-start.11
  20.4 0.0 collective-permute-done.6.refs_1_
  20.4 2.5 %collective-permute-start.7 = (f32[40,128]{1,0:T(8,128)S(1)}, f32[40,128]{1,0:T(8,128)S(1)}, u32[]{:S(2)}, u32[]{:S(2)}) collective-permute-start(f32[40,128]{1,0:T(8,128)S(1)} %get-tuple-element.43), channel_id=1, source_target_pairs={{0,17},{1,16},{2,19},{3,18},{4,21},{5,20},{6,23},{7,22},{8,25},{9,... | collective-permute-start | bytes 61448 | tf_op jit(solution)/shard_map/ppermute | solution.py:406
  22.9 0.6 %collective-permute-start.8 = (f32[40,128]{1,0:T(8,128)S(1)}, f32[40,128]{1,0:T(8,128)S(1)}, u32[]{:S(2)}, u32[]{:S(2)}) collective-permute-start(f32[40,128]{1,0:T(8,128)S(1)} %get-tuple-element.44), channel_id=1, source_target_pairs={{0,16},{8,24},{16,0},{24,8},{1,17},{9,25},{17,1},{25,9},{2,18},{10... | collective-permute-start | bytes 61448 | tf_op jit(solution)/shard_map/ppermute | solution.py:31
  23.5 0.5 %collective-permute-start.9 = (f32[40,128]{1,0:T(8,128)S(1)}, f32[40,128]{1,0:T(8,128)S(1)}, u32[]{:S(2)}, u32[]{:S(2)}) collective-permute-start(f32[40,128]{1,0:T(8,128)S(1)} %get-tuple-element.45), channel_id=1, source_target_pairs={{0,1},{1,0},{2,3},{3,2},{4,5},{5,4},{6,7},{7,6},{8,9},{9,8},{10,11... | collective-permute-start | bytes 61448 | tf_op jit(solution)/shard_map/ppermute | solution.py:31
  24.0 0.3 %collective-permute-done.10.refs_4_ = f32[64,128]{1,0:T(8,128)S(1)} collective-permute-done((f32[64,128]{1,0:T(8,128)S(1)}, f32[64,128]{1,0:T(8,128)S(1)}, u32[]{:S(2)}, u32[]{:S(2)}) %collective-permute-start.10) | collective-permute-done | bytes 32800 | tf_op jit(solution)/shard_map/ppermute | solution.py:31
  24.3 0.3 %collective-permute-done.11.refs_5_ = f32[64,128]{1,0:T(8,128)S(1)} collective-permute-done((f32[64,128]{1,0:T(8,128)S(1)}, f32[64,128]{1,0:T(8,128)S(1)}, u32[]{:S(2)}, u32[]{:S(2)}) %collective-permute-start.11) | collective-permute-done | bytes 32800 | tf_op jit(solution)/shard_map/ppermute | solution.py:31
  24.6 0.8 %collective-permute-done.7.refs_1_ = f32[40,128]{1,0:T(8,128)S(1)} collective-permute-done((f32[40,128]{1,0:T(8,128)S(1)}, f32[40,128]{1,0:T(8,128)S(1)}, u32[]{:S(2)}, u32[]{:S(2)}) %collective-permute-start.7) | collective-permute-done | bytes 20512 | tf_op jit(solution)/shard_map/ppermute | solution.py:406
  25.4 1.3 %collective-permute-done.8.refs_2_ = f32[40,128]{1,0:T(8,128)S(1)} collective-permute-done((f32[40,128]{1,0:T(8,128)S(1)}, f32[40,128]{1,0:T(8,128)S(1)}, u32[]{:S(2)}, u32[]{:S(2)}) %collective-permute-start.8) | collective-permute-done | bytes 20512 | tf_op jit(solution)/shard_map/ppermute | solution.py:31
  26.7 0.6 %collective-permute-done.9.refs_3_ = f32[40,128]{1,0:T(8,128)S(1)} collective-permute-done((f32[40,128]{1,0:T(8,128)S(1)}, f32[40,128]{1,0:T(8,128)S(1)}, u32[]{:S(2)}, u32[]{:S(2)}) %collective-permute-start.9) | collective-permute-done | bytes 20512 | tf_op jit(solution)/shard_map/ppermute | solution.py:31
  27.3 0.6 %sums.1 = (f32[1,3,1,32]{3,2,1,0:T(1,128)}, f32[1,1,32,128]{3,2,1,0:T(8,128)}) custom-call(f32[40,128]{1,0:T(8,128)S(1)} %get-tuple-element.42.refs_0_, f32[40,128]{1,0:T(8,128)S(1)} %collective-permute-done.7.refs_1_, f32[40,128]{1,0:T(8,128)S(1)} %collective-permute-done.8.refs_2_, f32[40,128]{1,0:T(8,128)S(1)} %collective-permute-done.9.refs_3_, ...), custom_call_target="tpu_custom_call" | custom-call | tf_op jit(solution)/shard_map/sums/pallas_call | solution.py:385
  (17 shorter events, 0.0 us)
Async XLA Ops:
  0.6 4.9 %copy-start.2 = (s32[1,1,5,5,32]{4,1,3,2,0:T(1,128)S(1)}, s32[1,1,5,5,32]{4,1,3,2,0:T(1,128)}, u32[]{:S(2)}) copy-start(s32[1,1,5,5,32]{4,1,3,2,0:T(1,128)} %param.13) | copy-start | bytes 9604
  0.6 4.8 %copy-start.3 = (s32[1,1,5,5,32]{4,1,3,2,0:T(1,128)S(1)}, s32[1,1,5,5,32]{4,1,3,2,0:T(1,128)}, u32[]{:S(2)}) copy-start(s32[1,1,5,5,32]{4,1,3,2,0:T(1,128)} %param.14) | copy-start | bytes 9604
  0.7 4.8 %copy-start.4 = (s32[1,1,5,5,32]{4,1,3,2,0:T(1,128)S(1)}, s32[1,1,5,5,32]{4,1,3,2,0:T(1,128)}, u32[]{:S(2)}) copy-start(s32[1,1,5,5,32]{4,1,3,2,0:T(1,128)} %param.15) | copy-start | bytes 9604
  0.7 4.8 %copy-start.5 = (s32[1,1,5,5,32]{4,1,3,2,0:T(1,128)S(1)}, s32[1,1,5,5,32]{4,1,3,2,0:T(1,128)}, u32[]{:S(2)}) copy-start(s32[1,1,5,5,32]{4,1,3,2,0:T(1,128)} %param.16) | copy-start | bytes 9604
  0.7 4.8 %copy-start.6 = (f32[32,384]{1,0:T(8,128)S(1)}, f32[32,384]{1,0:T(8,128)}, u32[]{:S(2)}) copy-start(f32[32,384]{1,0:T(8,128)} %out_ref.1) | copy-start | bytes 147460
  0.7 4.8 %copy-start.7 = (f32[10,32]{1,0:T(8,128)S(1)}, f32[10,32]{1,0:T(8,128)}, u32[]{:S(2)}) copy-start(f32[10,32]{1,0:T(8,128)} %emb_ref.1) | copy-start | bytes 3844
  0.7 4.8 %copy-start.8 = (f32[8,32]{1,0:T(8,128)S(1)}, f32[8,32]{1,0:T(8,128)}, u32[]{:S(2)}) copy-start(f32[8,32]{1,0:T(8,128)} %in_ref.1) | copy-start | bytes 3076
  2.5 3.2 %copy-start = (f32[296,128]{1,0:T(8,128)S(1)}, f32[296,128]{1,0:T(8,128)}, u32[]{:S(2)}) copy-start(f32[296,128]{1,0:T(8,128)} %get-tuple-element.39.refs_10_) | copy-start | bytes 454660
  2.5 6.9 %copy-start.1 = (f32[40,128]{1,0:T(8,128)S(1)}, f32[40,128]{1,0:T(8,128)}, u32[]{:S(2)}) copy-start(f32[40,128]{1,0:T(8,128)} %get-tuple-element.33.refs_0_.refs_5_) | copy-start | bytes 61444
  2.5 6.9 %collective-permute-start = (f32[72,128]{1,0:T(8,128)}, f32[72,128]{1,0:T(8,128)S(1)}, u32[]{:S(2)}, u32[]{:S(2)}) collective-permute-start(f32[72,128]{1,0:T(8,128)} %get-tuple-element.31), channel_id=1, source_target_pairs={{0,1},{1,0},{2,3},{3,2},{4,5},{5,4},{6,7},{7,6},{8,9},{9,8},{10,11... | collective-permute-start | bytes 110600 | tf_op jit(solution)/shard_map/ppermute | solution.py:31
  5.7 10.5 %collective-permute-start.5 = (f32[296,128]{1,0:T(8,128)S(1)}, f32[296,128]{1,0:T(8,128)S(1)}, u32[]{:S(2)}, u32[]{:S(2)}) collective-permute-start(f32[296,128]{1,0:T(8,128)S(1)} %copy-done), channel_id=1, source_target_pairs={{0,6},{1,7},{2,4},{3,5},{4,2},{5,3},{6,0},{7,1},{8,14},{9,15},{10,... | collective-permute-start | bytes 454664 | tf_op jit(solution)/shard_map/ppermute | solution.py:31
  9.4 7.0 %collective-permute-start.4 = (f32[296,128]{1,0:T(8,128)S(1)}, f32[296,128]{1,0:T(8,128)S(1)}, u32[]{:S(2)}, u32[]{:S(2)}) collective-permute-start(f32[296,128]{1,0:T(8,128)S(1)} %copy-done), channel_id=1, source_target_pairs={{0,2},{1,3},{2,0},{3,1},{4,6},{5,7},{6,4},{7,5},{8,10},{9,11},{10,... | collective-permute-start | bytes 454664 | tf_op jit(solution)/shard_map/ppermute | solution.py:31
  9.4 4.1 %collective-permute-start.3 = (f32[80,128]{1,0:T(8,128)S(1)}, f32[80,128]{1,0:T(8,128)S(1)}, u32[]{:S(2)}, u32[]{:S(2)}) collective-permute-start(f32[80,128]{1,0:T(8,128)S(1)} %stack.1), channel_id=1, source_target_pairs={{0,16},{8,24},{16,0},{24,8},{1,17},{9,25},{17,1},{25,9},{2,18},{10... | collective-permute-start | bytes 122888 | tf_op jit(solution)/shard_map/ppermute | solution.py:31
  11.0 3.4 %collective-permute-start.2 = (f32[80,128]{1,0:T(8,128)S(1)}, f32[80,128]{1,0:T(8,128)S(1)}, u32[]{:S(2)}, u32[]{:S(2)}) collective-permute-start(f32[80,128]{1,0:T(8,128)S(1)} %stack.1), channel_id=1, source_target_pairs={{0,24},{8,16},{16,8},{24,0},{1,25},{9,17},{17,9},{25,1},{2,26},{10... | collective-permute-start | bytes 122888 | tf_op jit(solution)/shard_map/ppermute | solution.py:31
  11.0 3.4 %collective-permute-start.1 = (f32[80,128]{1,0:T(8,128)S(1)}, f32[80,128]{1,0:T(8,128)S(1)}, u32[]{:S(2)}, u32[]{:S(2)}) collective-permute-start(f32[80,128]{1,0:T(8,128)S(1)} %stack.1), channel_id=1, source_target_pairs={{0,8},{8,0},{16,24},{24,16},{1,9},{9,1},{17,25},{25,17},{2,10},{10... | collective-permute-start | bytes 122888 | tf_op jit(solution)/shard_map/ppermute | solution.py:31
  18.2 2.2 %collective-permute-start.6 = (f32[160,128]{1,0:T(8,128)S(1)}, f32[160,128]{1,0:T(8,128)S(1)}, u32[]{:S(2)}, u32[]{:S(2)}) collective-permute-start(f32[160,128]{1,0:T(8,128)S(1)} %get-tuple-element.41), channel_id=1, source_target_pairs={{0,8},{8,0},{16,24},{24,16},{1,9},{9,1},{17,25},{25,17},{2,10},{10... | collective-permute-start | bytes 245768 | tf_op jit(solution)/shard_map/ppermute | solution.py:31
  18.3 6.0 %collective-permute-start.10 = (f32[64,128]{1,0:T(8,128)S(1)}, f32[64,128]{1,0:T(8,128)S(1)}, u32[]{:S(2)}, u32[]{:S(2)}) collective-permute-start(f32[64,128]{1,0:T(8,128)S(1)} %get-tuple-element.46), channel_id=1, source_target_pairs={{0,6},{1,7},{2,4},{3,5},{4,2},{5,3},{6,0},{7,1},{8,14},{9,15},{10,... | collective-permute-start | bytes 98312 | tf_op jit(solution)/shard_map/ppermute | solution.py:31
  20.4 4.2 %collective-permute-start.11 = (f32[64,128]{1,0:T(8,128)S(1)}, f32[64,128]{1,0:T(8,128)S(1)}, u32[]{:S(2)}, u32[]{:S(2)}) collective-permute-start(f32[64,128]{1,0:T(8,128)S(1)} %get-tuple-element.47), channel_id=1, source_target_pairs={{0,2},{1,3},{2,0},{3,1},{4,6},{5,7},{6,4},{7,5},{8,10},{9,11},{10,... | collective-permute-start | bytes 98312 | tf_op jit(solution)/shard_map/ppermute | solution.py:31
  20.4 4.9 %collective-permute-start.7 = (f32[40,128]{1,0:T(8,128)S(1)}, f32[40,128]{1,0:T(8,128)S(1)}, u32[]{:S(2)}, u32[]{:S(2)}) collective-permute-start(f32[40,128]{1,0:T(8,128)S(1)} %get-tuple-element.43), channel_id=1, source_target_pairs={{0,17},{1,16},{2,19},{3,18},{4,21},{5,20},{6,23},{7,22},{8,25},{9,... | collective-permute-start | bytes 61448 | tf_op jit(solution)/shard_map/ppermute | solution.py:406
  22.9 3.8 %collective-permute-start.8 = (f32[40,128]{1,0:T(8,128)S(1)}, f32[40,128]{1,0:T(8,128)S(1)}, u32[]{:S(2)}, u32[]{:S(2)}) collective-permute-start(f32[40,128]{1,0:T(8,128)S(1)} %get-tuple-element.44), channel_id=1, source_target_pairs={{0,16},{8,24},{16,0},{24,8},{1,17},{9,25},{17,1},{25,9},{2,18},{10... | collective-permute-start | bytes 61448 | tf_op jit(solution)/shard_map/ppermute | solution.py:31
  23.5 3.8 %collective-permute-start.9 = (f32[40,128]{1,0:T(8,128)S(1)}, f32[40,128]{1,0:T(8,128)S(1)}, u32[]{:S(2)}, u32[]{:S(2)}) collective-permute-start(f32[40,128]{1,0:T(8,128)S(1)} %get-tuple-element.45), channel_id=1, source_target_pairs={{0,1},{1,0},{2,3},{3,2},{4,5},{5,4},{6,7},{7,6},{8,9},{9,8},{10,11... | collective-permute-start | bytes 61448 | tf_op jit(solution)/shard_map/ppermute | solution.py:31

commit v9 on v8

--- a/solution.py
+++ b/solution.py
@@ -154,7 +154,7 @@
     spare = jnp.zeros((sublanes * 2 - emb_ref.shape[0], hidden), f32)
     high, low = pieces(jnp.concatenate([in_ref[...], emb_ref[...], spare], axis=0), 2)
     first_ref[...] = jnp.concatenate([high, high, low], axis=0).T.astype(bf16)
-    last_ref[...] = jnp.concatenate([high[0:orders], high[0:orders], low[0:orders]], axis=1).astype(bf16)
+    last_ref[...] = jnp.concatenate([high[0:orders], high[0:orders], low[0:orders]], axis=1)
 
 
 def radial_waves(dist, orders):
@@ -202,7 +202,7 @@
     offset = rows[4:6].astype(f32) * domain_side
 
     tgt_pos = [jnp.concatenate(pieces(ref[parts * atoms :, 0:atoms], 3), axis=0) for ref in cot_refs]
-    gathered = dot(jnp.concatenate([feats, src_pos], axis=0), src_hot)
+    gathered = dot(jnp.concatenate([feats, src_pos.astype(bf16)], axis=0), src_hot)
     from_src = gathered[2 * channels :]
     gathered = gathered[0:channels] + gathered[channels : 2 * channels]
     from_tgt = dot(jnp.concatenate(tgt_pos, axis=1).astype(bf16), tgt_hot)
@@ -267,7 +267,7 @@
         [p.astype(bf16) for p in pieces(jnp.concatenate(d_radial, axis=0), 2)], axis=0
     ))
     d_before = (d_hidden[0:hidden] + d_hidden[hidden:]) * (d_act * env)
-    to_basis = dot(last, thrice(d_before))
+    to_basis = dot(last.astype(bf16), thrice(d_before))
     d_dist = jnp.sum(to_basis * d_basis, axis=0, keepdims=True) + to_env * d_env
 
     s = d_shapes
@@ -317,7 +317,7 @@
     views = [block_refs[ref].at[at * block : (at + 1) * block] for ref, at in tables]
     for table, ref in enumerate(views):
         place[:, table * atoms : (table + 1) * atoms] = ref[atoms:, 0:atoms]
-    src_pos_ref[...] = jnp.concatenate(pieces(place[...], 3), axis=0).astype(bf16)
+    src_pos_ref[...] = jnp.concatenate(pieces(place[...], 3), axis=0)
     feats = jnp.concatenate([ref[0:atoms] for ref in views], axis=0).T
     feats_ref[...] = jnp.concatenate(pieces(feats, 2), axis=0).astype(bf16)
     rows = all_rows(rows_ref, y_ref, start, chunks)
@@ -446,7 +446,7 @@
             sds((w_out.shape[1], 3 * hidden), bf16),
             sds((2 * hidden, 2 * w_out.shape[1]), bf16),
             sds((hidden, 3 * (orders + 2 * sublanes)), bf16),
-            sds((orders, 3 * hidden), bf16),
+            sds((orders, 3 * hidden), f32),
         ),
         (*lists, w_in, species_emb, w_out), us=3,
     )
@@ -458,7 +458,7 @@
     )
     blocks = [own, y] + [link.swap(two, "gx") for link in gx_links]
     table = (
-        sds((3 * sublanes, 2 * sources), bf16), sds((2 * channels, 2 * sources), bf16),
+        sds((3 * sublanes, 2 * sources), f32), sds((2 * channels, 2 * sources), bf16),
         sds((sublanes, 2 * sources), f32), sds((2 * sources, channels), f32),
     )
     held = call(

time: 28.1 us -> 28.1 us (level)
  no operation moved by 1% of the time
where the time goes in v9:
time: 28.1 us; the launch traced here: 27.9 us
  starting transfers between devices  14.6 us (52%)
  waiting for transfers between devices  6.27 us (22%)
  Pallas kernels  6.22 us (22%)
  between operations  0.78 us (3%)
    ppermute x11, starting transfers between devices, swap(): lax.ppermute(value, axis, [(i, (i + self.delta(i)) % n) for i in range(n)])  12.1 us
    pallas_call x7, Pallas kernels, call(): pl.pallas_call(kernel, out_shape=out_shape, in_specs=[vmem] * len(operand...  6.22 us
    ppermute x11, waiting for transfers between devices, swap(): lax.ppermute(value, axis, [(i, (i + self.delta(i)) % n) for i in range(n)])  5.5 us
    ppermute x1, starting transfers between devices, diagonal(): return lax.ppermute(value, ('gx', 'gy'), pairs)  2.47 us
    ppermute x1, waiting for transfers between devices, diagonal(): return lax.ppermute(value, ('gx', 'gy'), pairs)  0.77 us
  transfers between devices with their start and end apart: 12, of which 8 were waited for; matrix products, arithmetic and copies ran while one was open for 0% of the time, Pallas kernels for 7%

profile of v9, /device:TPU:0, one launch (start us, length us, event | category | flops | bytes accessed | tf_op | source)
XLA Modules:
  0.0 27.9 jit_solution(13165705849793379600)
XLA Ops:
  0.6 0.0 copy-start.2
  0.6 0.0 copy-start.3
  0.7 1.8 %pack.1 = (f32[40,128]{1,0:T(8,128)}, f32[72,128]{1,0:T(8,128)}, f32[296,128]{1,0:T(8,128)}) custom-call(f32[1,3,1,32]{3,2,1,0:T(1,128)} %bitcast.14, f32[1,1,32,128]{3,2,1,0:T(8,128)} %feat_ref.1, f32[1,1,32,1152]{3,2,1,0:T(8,128)} %cot_ref.1, s32[1,5,5,1,32]{4,3,2,1,0:T(1,128)} %bitcast.6, s32[1,5,5,1,32]{4,3,2,1,0:T(1,128)} %bitcast.8, ...), custom_call_target="tpu_custom_call" | custom-call | tf_op jit(solution)/shard_map/pack/pallas_call | solution.py:385
  2.5 3.0 %collective-permute-start = (f32[72,128]{1,0:T(8,128)}, f32[72,128]{1,0:T(8,128)S(1)}, u32[]{:S(2)}, u32[]{:S(2)}) collective-permute-start(f32[72,128]{1,0:T(8,128)} %get-tuple-element.31), channel_id=1, source_target_pairs={{0,1},{1,0},{2,3},{3,2},{4,5},{5,4},{6,7},{7,6},{8,9},{9,8},{10,11... | collective-permute-start | bytes 110600 | tf_op jit(solution)/shard_map/ppermute | solution.py:31
  5.5 0.0 copy-done.3
  5.5 0.2 prepare.1
  5.7 3.7 %collective-permute-start.5 = (f32[296,128]{1,0:T(8,128)S(1)}, f32[296,128]{1,0:T(8,128)S(1)}, u32[]{:S(2)}, u32[]{:S(2)}) collective-permute-start(f32[296,128]{1,0:T(8,128)S(1)} %copy-done), channel_id=1, source_target_pairs={{0,6},{1,7},{2,4},{3,5},{4,2},{5,3},{6,0},{7,1},{8,14},{9,15},{10,... | collective-permute-start | bytes 454664 | tf_op jit(solution)/shard_map/ppermute | solution.py:31
  9.4 0.0 collective-permute-start.4
  9.4 0.0 collective-permute-done.refs_1_.refs_4_.refs_6_
  9.4 1.6 %collective-permute-start.3 = (f32[80,128]{1,0:T(8,128)S(1)}, f32[80,128]{1,0:T(8,128)S(1)}, u32[]{:S(2)}, u32[]{:S(2)}) collective-permute-start(f32[80,128]{1,0:T(8,128)S(1)} %stack.1), channel_id=1, source_target_pairs={{0,16},{8,24},{16,0},{24,8},{1,17},{9,25},{17,1},{25,9},{2,18},{10... | collective-permute-start | bytes 122888 | tf_op jit(solution)/shard_map/ppermute | solution.py:31
  11.0 0.0 collective-permute-start.2
  11.0 0.6 %collective-permute-start.1 = (f32[80,128]{1,0:T(8,128)S(1)}, f32[80,128]{1,0:T(8,128)S(1)}, u32[]{:S(2)}, u32[]{:S(2)}) collective-permute-start(f32[80,128]{1,0:T(8,128)S(1)} %stack.1), channel_id=1, source_target_pairs={{0,8},{8,0},{16,24},{24,16},{1,9},{9,1},{17,25},{25,17},{2,10},{10... | collective-permute-start | bytes 122888 | tf_op jit(solution)/shard_map/ppermute | solution.py:31
  11.6 1.9 %collective-permute-done.3.refs_9_ = f32[80,128]{1,0:T(8,128)S(1)} collective-permute-done((f32[80,128]{1,0:T(8,128)S(1)}, f32[80,128]{1,0:T(8,128)S(1)}, u32[]{:S(2)}, u32[]{:S(2)}) %collective-permute-start.3) | collective-permute-done | bytes 40992 | tf_op jit(solution)/shard_map/ppermute | solution.py:31
  13.5 0.9 %collective-permute-done.2.refs_8_ = f32[80,128]{1,0:T(8,128)S(1)} collective-permute-done((f32[80,128]{1,0:T(8,128)S(1)}, f32[80,128]{1,0:T(8,128)S(1)}, u32[]{:S(2)}, u32[]{:S(2)}) %collective-permute-start.2) | collective-permute-done | bytes 40992 | tf_op jit(solution)/shard_map/ppermute | solution.py:31
  14.4 0.0 collective-permute-done.1.refs_7_
  14.4 1.8 %early_tiles.1 = (f32[24,256]{1,0:T(8,128)S(1)}, bf16[256,256]{1,0:T(8,128)(2,1)S(1)}, f32[8,256]{1,0:T(8,128)S(1)}, f32[256,128]{1,0:T(8,128)S(1)}) custom-call(s32[8,384]{1,0:T(8,128)S(1)} %get-tuple-element.32.rows_ref, bf16[384,96]{1,0:T(8,128)(2,1)S(1)} %get-tuple-element.27.refs_0_, bf16[64,768]{1,0:T(8,128)(2,1)S(1)} %get-tuple-element.28.refs_1_, ...), custom_call_target="tpu_custom_call" | custom-call | tf_op jit(solution)/shard_map/early_tiles/pallas_call | solution.py:385
  16.2 0.0 collective-permute-done.5.refs_10_
  16.2 0.2 collective-permute-done.4.refs_9_
  16.4 1.8 %late_tiles.1 = (f32[160,128]{1,0:T(8,128)S(1)}, f32[160,128]{1,0:T(8,128)S(1)}, f32[64,128]{1,0:T(8,128)S(1)}, f32[64,128]{1,0:T(8,128)S(1)}) custom-call(s32[8,512]{1,0:T(8,128)S(1)} %get-tuple-element.26.rows_ref, bf16[384,96]{1,0:T(8,128)(2,1)S(1)} %get-tuple-element.27.refs_0_, bf16[64,768]{1,0:T(8,128)(2,1)S(1)} %get-tuple-element.28.refs_1_, ...), custom_call_target="tpu_custom_call" | custom-call | tf_op jit(solution)/shard_map/late_tiles/pallas_call | solution.py:385
  18.2 0.1 collective-permute-start.6
  18.3 2.1 %collective-permute-start.10 = (f32[64,128]{1,0:T(8,128)S(1)}, f32[64,128]{1,0:T(8,128)S(1)}, u32[]{:S(2)}, u32[]{:S(2)}) collective-permute-start(f32[64,128]{1,0:T(8,128)S(1)} %get-tuple-element.46), channel_id=1, source_target_pairs={{0,6},{1,7},{2,4},{3,5},{4,2},{5,3},{6,0},{7,1},{8,14},{9,15},{10,... | collective-permute-start | bytes 98312 | tf_op jit(solution)/shard_map/ppermute | solution.py:31
  20.4 0.0 collective-permute-start.11
  20.4 0.0 collective-permute-done.6.refs_1_
  20.4 2.5 %collective-permute-start.7 = (f32[40,128]{1,0:T(8,128)S(1)}, f32[40,128]{1,0:T(8,128)S(1)}, u32[]{:S(2)}, u32[]{:S(2)}) collective-permute-start(f32[40,128]{1,0:T(8,128)S(1)} %get-tuple-element.43), channel_id=1, source_target_pairs={{0,17},{1,16},{2,19},{3,18},{4,21},{5,20},{6,23},{7,22},{8,25},{9,... | collective-permute-start | bytes 61448 | tf_op jit(solution)/shard_map/ppermute | solution.py:406
  22.9 0.6 %collective-permute-start.8 = (f32[40,128]{1,0:T(8,128)S(1)}, f32[40,128]{1,0:T(8,128)S(1)}, u32[]{:S(2)}, u32[]{:S(2)}) collective-permute-start(f32[40,128]{1,0:T(8,128)S(1)} %get-tuple-element.44), channel_id=1, source_target_pairs={{0,16},{8,24},{16,0},{24,8},{1,17},{9,25},{17,1},{25,9},{2,18},{10... | collective-permute-start | bytes 61448 | tf_op jit(solution)/shard_map/ppermute | solution.py:31
  23.5 0.5 %collective-permute-start.9 = (f32[40,128]{1,0:T(8,128)S(1)}, f32[40,128]{1,0:T(8,128)S(1)}, u32[]{:S(2)}, u32[]{:S(2)}) collective-permute-start(f32[40,128]{1,0:T(8,128)S(1)} %get-tuple-element.45), channel_id=1, source_target_pairs={{0,1},{1,0},{2,3},{3,2},{4,5},{5,4},{6,7},{7,6},{8,9},{9,8},{10,11... | collective-permute-start | bytes 61448 | tf_op jit(solution)/shard_map/ppermute | solution.py:31
  24.0 0.3 %collective-permute-done.10.refs_4_ = f32[64,128]{1,0:T(8,128)S(1)} collective-permute-done((f32[64,128]{1,0:T(8,128)S(1)}, f32[64,128]{1,0:T(8,128)S(1)}, u32[]{:S(2)}, u32[]{:S(2)}) %collective-permute-start.10) | collective-permute-done | bytes 32800 | tf_op jit(solution)/shard_map/ppermute | solution.py:31
  24.3 0.3 %collective-permute-done.11.refs_5_ = f32[64,128]{1,0:T(8,128)S(1)} collective-permute-done((f32[64,128]{1,0:T(8,128)S(1)}, f32[64,128]{1,0:T(8,128)S(1)}, u32[]{:S(2)}, u32[]{:S(2)}) %collective-permute-start.11) | collective-permute-done | bytes 32800 | tf_op jit(solution)/shard_map/ppermute | solution.py:31
  24.6 0.8 %collective-permute-done.7.refs_1_ = f32[40,128]{1,0:T(8,128)S(1)} collective-permute-done((f32[40,128]{1,0:T(8,128)S(1)}, f32[40,128]{1,0:T(8,128)S(1)}, u32[]{:S(2)}, u32[]{:S(2)}) %collective-permute-start.7) | collective-permute-done | bytes 20512 | tf_op jit(solution)/shard_map/ppermute | solution.py:406
  25.4 1.3 %collective-permute-done.8.refs_2_ = f32[40,128]{1,0:T(8,128)S(1)} collective-permute-done((f32[40,128]{1,0:T(8,128)S(1)}, f32[40,128]{1,0:T(8,128)S(1)}, u32[]{:S(2)}, u32[]{:S(2)}) %collective-permute-start.8) | collective-permute-done | bytes 20512 | tf_op jit(solution)/shard_map/ppermute | solution.py:31
  26.7 0.6 %collective-permute-done.9.refs_3_ = f32[40,128]{1,0:T(8,128)S(1)} collective-permute-done((f32[40,128]{1,0:T(8,128)S(1)}, f32[40,128]{1,0:T(8,128)S(1)}, u32[]{:S(2)}, u32[]{:S(2)}) %collective-permute-start.9) | collective-permute-done | bytes 20512 | tf_op jit(solution)/shard_map/ppermute | solution.py:31
  27.3 0.6 %sums.1 = (f32[1,3,1,32]{3,2,1,0:T(1,128)}, f32[1,1,32,128]{3,2,1,0:T(8,128)}) custom-call(f32[40,128]{1,0:T(8,128)S(1)} %get-tuple-element.42.refs_0_, f32[40,128]{1,0:T(8,128)S(1)} %collective-permute-done.7.refs_1_, f32[40,128]{1,0:T(8,128)S(1)} %collective-permute-done.8.refs_2_, f32[40,128]{1,0:T(8,128)S(1)} %collective-permute-done.9.refs_3_, ...), custom_call_target="tpu_custom_call" | custom-call | tf_op jit(solution)/shard_map/sums/pallas_call | solution.py:385
  (17 shorter events, 0.0 us)
Async XLA Ops:
  0.6 4.9 %copy-start.2 = (s32[1,1,5,5,32]{4,1,3,2,0:T(1,128)S(1)}, s32[1,1,5,5,32]{4,1,3,2,0:T(1,128)}, u32[]{:S(2)}) copy-start(s32[1,1,5,5,32]{4,1,3,2,0:T(1,128)} %param.13) | copy-start | bytes 9604
  0.6 4.8 %copy-start.3 = (s32[1,1,5,5,32]{4,1,3,2,0:T(1,128)S(1)}, s32[1,1,5,5,32]{4,1,3,2,0:T(1,128)}, u32[]{:S(2)}) copy-start(s32[1,1,5,5,32]{4,1,3,2,0:T(1,128)} %param.14) | copy-start | bytes 9604
  0.7 4.8 %copy-start.4 = (s32[1,1,5,5,32]{4,1,3,2,0:T(1,128)S(1)}, s32[1,1,5,5,32]{4,1,3,2,0:T(1,128)}, u32[]{:S(2)}) copy-start(s32[1,1,5,5,32]{4,1,3,2,0:T(1,128)} %param.15) | copy-start | bytes 9604
  0.7 4.8 %copy-start.5 = (s32[1,1,5,5,32]{4,1,3,2,0:T(1,128)S(1)}, s32[1,1,5,5,32]{4,1,3,2,0:T(1,128)}, u32[]{:S(2)}) copy-start(s32[1,1,5,5,32]{4,1,3,2,0:T(1,128)} %param.16) | copy-start | bytes 9604
  0.7 4.8 %copy-start.6 = (f32[32,384]{1,0:T(8,128)S(1)}, f32[32,384]{1,0:T(8,128)}, u32[]{:S(2)}) copy-start(f32[32,384]{1,0:T(8,128)} %out_ref.1) | copy-start | bytes 147460
  0.7 4.8 %copy-start.7 = (f32[10,32]{1,0:T(8,128)S(1)}, f32[10,32]{1,0:T(8,128)}, u32[]{:S(2)}) copy-start(f32[10,32]{1,0:T(8,128)} %emb_ref.1) | copy-start | bytes 3844
  0.7 4.8 %copy-start.8 = (f32[8,32]{1,0:T(8,128)S(1)}, f32[8,32]{1,0:T(8,128)}, u32[]{:S(2)}) copy-start(f32[8,32]{1,0:T(8,128)} %in_ref.1) | copy-start | bytes 3076
  2.5 3.2 %copy-start = (f32[296,128]{1,0:T(8,128)S(1)}, f32[296,128]{1,0:T(8,128)}, u32[]{:S(2)}) copy-start(f32[296,128]{1,0:T(8,128)} %get-tuple-element.39.refs_10_) | copy-start | bytes 454660
  2.5 6.9 %copy-start.1 = (f32[40,128]{1,0:T(8,128)S(1)}, f32[40,128]{1,0:T(8,128)}, u32[]{:S(2)}) copy-start(f32[40,128]{1,0:T(8,128)} %get-tuple-element.33.refs_0_.refs_5_) | copy-start | bytes 61444
  2.5 6.9 %collective-permute-start = (f32[72,128]{1,0:T(8,128)}, f32[72,128]{1,0:T(8,128)S(1)}, u32[]{:S(2)}, u32[]{:S(2)}) collective-permute-start(f32[72,128]{1,0:T(8,128)} %get-tuple-element.31), channel_id=1, source_target_pairs={{0,1},{1,0},{2,3},{3,2},{4,5},{5,4},{6,7},{7,6},{8,9},{9,8},{10,11... | collective-permute-start | bytes 110600 | tf_op jit(solution)/shard_map/ppermute | solution.py:31
  5.7 10.5 %collective-permute-start.5 = (f32[296,128]{1,0:T(8,128)S(1)}, f32[296,128]{1,0:T(8,128)S(1)}, u32[]{:S(2)}, u32[]{:S(2)}) collective-permute-start(f32[296,128]{1,0:T(8,128)S(1)} %copy-done), channel_id=1, source_target_pairs={{0,6},{1,7},{2,4},{3,5},{4,2},{5,3},{6,0},{7,1},{8,14},{9,15},{10,... | collective-permute-start | bytes 454664 | tf_op jit(solution)/shard_map/ppermute | solution.py:31
  9.4 7.0 %collective-permute-start.4 = (f32[296,128]{1,0:T(8,128)S(1)}, f32[296,128]{1,0:T(8,128)S(1)}, u32[]{:S(2)}, u32[]{:S(2)}) collective-permute-start(f32[296,128]{1,0:T(8,128)S(1)} %copy-done), channel_id=1, source_target_pairs={{0,2},{1,3},{2,0},{3,1},{4,6},{5,7},{6,4},{7,5},{8,10},{9,11},{10,... | collective-permute-start | bytes 454664 | tf_op jit(solution)/shard_map/ppermute | solution.py:31
  9.4 4.1 %collective-permute-start.3 = (f32[80,128]{1,0:T(8,128)S(1)}, f32[80,128]{1,0:T(8,128)S(1)}, u32[]{:S(2)}, u32[]{:S(2)}) collective-permute-start(f32[80,128]{1,0:T(8,128)S(1)} %stack.1), channel_id=1, source_target_pairs={{0,16},{8,24},{16,0},{24,8},{1,17},{9,25},{17,1},{25,9},{2,18},{10... | collective-permute-start | bytes 122888 | tf_op jit(solution)/shard_map/ppermute | solution.py:31
  11.0 3.4 %collective-permute-start.2 = (f32[80,128]{1,0:T(8,128)S(1)}, f32[80,128]{1,0:T(8,128)S(1)}, u32[]{:S(2)}, u32[]{:S(2)}) collective-permute-start(f32[80,128]{1,0:T(8,128)S(1)} %stack.1), channel_id=1, source_target_pairs={{0,24},{8,16},{16,8},{24,0},{1,25},{9,17},{17,9},{25,1},{2,26},{10... | collective-permute-start | bytes 122888 | tf_op jit(solution)/shard_map/ppermute | solution.py:31
  11.0 3.4 %collective-permute-start.1 = (f32[80,128]{1,0:T(8,128)S(1)}, f32[80,128]{1,0:T(8,128)S(1)}, u32[]{:S(2)}, u32[]{:S(2)}) collective-permute-start(f32[80,128]{1,0:T(8,128)S(1)} %stack.1), channel_id=1, source_target_pairs={{0,8},{8,0},{16,24},{24,16},{1,9},{9,1},{17,25},{25,17},{2,10},{10... | collective-permute-start | bytes 122888 | tf_op jit(solution)/shard_map/ppermute | solution.py:31
  18.2 2.2 %collective-permute-start.6 = (f32[160,128]{1,0:T(8,128)S(1)}, f32[160,128]{1,0:T(8,128)S(1)}, u32[]{:S(2)}, u32[]{:S(2)}) collective-permute-start(f32[160,128]{1,0:T(8,128)S(1)} %get-tuple-element.41), channel_id=1, source_target_pairs={{0,8},{8,0},{16,24},{24,16},{1,9},{9,1},{17,25},{25,17},{2,10},{10... | collective-permute-start | bytes 245768 | tf_op jit(solution)/shard_map/ppermute | solution.py:31
  18.3 6.0 %collective-permute-start.10 = (f32[64,128]{1,0:T(8,128)S(1)}, f32[64,128]{1,0:T(8,128)S(1)}, u32[]{:S(2)}, u32[]{:S(2)}) collective-permute-start(f32[64,128]{1,0:T(8,128)S(1)} %get-tuple-element.46), channel_id=1, source_target_pairs={{0,6},{1,7},{2,4},{3,5},{4,2},{5,3},{6,0},{7,1},{8,14},{9,15},{10,... | collective-permute-start | bytes 98312 | tf_op jit(solution)/shard_map/ppermute | solution.py:31
  20.4 4.2 %collective-permute-start.11 = (f32[64,128]{1,0:T(8,128)S(1)}, f32[64,128]{1,0:T(8,128)S(1)}, u32[]{:S(2)}, u32[]{:S(2)}) collective-permute-start(f32[64,128]{1,0:T(8,128)S(1)} %get-tuple-element.47), channel_id=1, source_target_pairs={{0,2},{1,3},{2,0},{3,1},{4,6},{5,7},{6,4},{7,5},{8,10},{9,11},{10,... | collective-permute-start | bytes 98312 | tf_op jit(solution)/shard_map/ppermute | solution.py:31
  20.4 4.9 %collective-permute-start.7 = (f32[40,128]{1,0:T(8,128)S(1)}, f32[40,128]{1,0:T(8,128)S(1)}, u32[]{:S(2)}, u32[]{:S(2)}) collective-permute-start(f32[40,128]{1,0:T(8,128)S(1)} %get-tuple-element.43), channel_id=1, source_target_pairs={{0,17},{1,16},{2,19},{3,18},{4,21},{5,20},{6,23},{7,22},{8,25},{9,... | collective-permute-start | bytes 61448 | tf_op jit(solution)/shard_map/ppermute | solution.py:406
  22.9 3.8 %collective-permute-start.8 = (f32[40,128]{1,0:T(8,128)S(1)}, f32[40,128]{1,0:T(8,128)S(1)}, u32[]{:S(2)}, u32[]{:S(2)}) collective-permute-start(f32[40,128]{1,0:T(8,128)S(1)} %get-tuple-element.44), channel_id=1, source_target_pairs={{0,16},{8,24},{16,0},{24,8},{1,17},{9,25},{17,1},{25,9},{2,18},{10... | collective-permute-start | bytes 61448 | tf_op jit(solution)/shard_map/ppermute | solution.py:31
  23.5 3.8 %collective-permute-start.9 = (f32[40,128]{1,0:T(8,128)S(1)}, f32[40,128]{1,0:T(8,128)S(1)}, u32[]{:S(2)}, u32[]{:S(2)}) collective-permute-start(f32[40,128]{1,0:T(8,128)S(1)} %get-tuple-element.45), channel_id=1, source_target_pairs={{0,1},{1,0},{2,3},{3,2},{4,5},{5,4},{6,7},{7,6},{8,9},{9,8},{10,11... | collective-permute-start | bytes 61448 | tf_op jit(solution)/shard_map/ppermute | solution.py:31

commit v10 on v9

--- a/solution.py
+++ b/solution.py
@@ -333,7 +333,7 @@
     refs = list(refs)
     weights = [refs.pop(0)[...] for _ in range(4)]
     y_ref, src_pos_ref, feats_ref, held_pos, held_feat = (refs.pop(0) for _ in range(5))
-    cot_refs = [refs.pop(0) for _ in range(2)]
+    cot_refs = [refs.pop(0) for _ in range(2)][::-1]
     *outs, near_ref, far_ref = refs
     atoms = (cot_refs[0].shape[0] - sublanes) // len(degree)
     block = atoms + sublanes
@@ -433,7 +433,7 @@
     far_links = (gy_links[3], gy_links[2])
     y = gy_links[0].swap(y_own, "gy")
     many = len(gx_links) + 1
-    tables = [(at, 0) if not l else (1 + l, at) for at in range(2) for l in range(many)]
+    tables = [(at, 0) if not l else (1 + many - l, at) for at in range(2) for l in range(many)]
     if gx_size == 4:
         homes = ((0, 3, many, many + 3), (1, 2, many + 1, many + 2))
     else:
@@ -450,13 +450,16 @@
         ),
         (*lists, w_in, species_emb, w_out), us=3,
     )
-    late_cot = lax.optimization_barrier((cot_own, weights[-1]))[0]
+    (turn,) = call(
+        functools.partial(stack_kernel, orders), "turn", (sds(w_in.shape, f32),), (w_in, w_in), us=3
+    )
+    late_cot = lax.optimization_barrier((cot_own, turn))[0]
     cot_far, cot_near = (link.swap(late_cot, "gy") for link in far_links)
     (two,) = call(
         functools.partial(stack_kernel, block), "stack", (sds((2 * block, channels), f32),),
-        (own, y, weights[-1]), us=2,
-    )
-    blocks = [own, y] + [link.swap(two, "gx") for link in gx_links]
+        (own, y, turn), us=2,
+    )
+    blocks = [own, y] + [link.swap(two, "gx") for link in gx_links[::-1]]
     table = (
         sds((3 * sublanes, 2 * sources), f32), sds((2 * channels, 2 * sources), bf16),
         sds((sublanes, 2 * sources), f32), sds((2 * sources, channels), f32),
@@ -471,7 +474,7 @@
         functools.partial(late_kernel, orders, homes, block + chunks[0] * sublanes, chunks[1]),
         "late_tiles",
         tuple(sds((len(home) * block, channels), f32) for home in homes) + (far_pack,) * 2,
-        (late_rows, *weights, y, *held, cot_near, cot_far), room=24,
+        (late_rows, *weights, y, *held, cot_far, cot_near), room=24,
     )
     back_gy = [link.swap(value, "gy") for link, value in zip(far_links, (far, near))]
     if gx_size == 4:
@@ -480,8 +483,8 @@
             functools.partial(add_kernel, 2), "add", (gx_pack,) * 4, (sent[0], came)
         )
         back = [
-            own, diagonal(xy, gx_links[2], gy_links[0]), gx_links[2].swap(x, "gx"),
-            gy_links[0].swap(y, "gy"),
+            own, diagonal(xy, gx_links[2], gy_links[0]), gy_links[0].swap(y, "gy"),
+            gx_links[2].swap(x, "gx"),
         ]
     else:
         came = [link.swap(value, "gx") for link, value in zip(gx_links, sent[1:])]

time: 28.1 us -> 28 us (level)
  waiting for transfers between devices: 6.27 us -> 5.91 us
  starting transfers between devices: 14.6 us -> 14.9 us
    ppermute x11, waiting for transfers between devices: 5.5 us -> 5.04 us  [swap(): lax.ppermute(value, axis, [(i, (i + self.delta(i)) % n) for i in range(n)])]
    ppermute x11, starting transfers between devices: 12.1 us -> 12.5 us  [swap(): lax.ppermute(value, axis, [(i, (i + self.delta(i)) % n) for i in range(n)])]
    pallas_call x7 -> x8, Pallas kernels: 6.22 us -> 6.18 us  [call(): pl.pallas_call(kernel, out_shape=out_shape, in_specs=[vmem] * len(operand...]
  transfers between devices with their start and end apart: 12 -> 12, of which waited for: 8 -> 7; matrix products, arithmetic and copies ran while one was open for 0% -> 0% of each run, Pallas kernels for 7% -> 7%
where the time goes in v10:
time: 28 us; the launch traced here: 27.8 us
  starting transfers between devices  14.9 us (53%)
  Pallas kernels  6.18 us (22%)
  waiting for transfers between devices  5.91 us (21%)
  between operations  0.77 us (3%)
    ppermute x11, starting transfers between devices, swap(): lax.ppermute(value, axis, [(i, (i + self.delta(i)) % n) for i in range(n)])  12.5 us
    pallas_call x8, Pallas kernels, call(): pl.pallas_call(kernel, out_shape=out_shape, in_specs=[vmem] * len(operand...  6.18 us
    ppermute x11, waiting for transfers between devices, swap(): lax.ppermute(value, axis, [(i, (i + self.delta(i)) % n) for i in range(n)])  5.04 us
    ppermute x1, starting transfers between devices, diagonal(): return lax.ppermute(value, ('gx', 'gy'), pairs)  2.47 us
    ppermute x1, waiting for transfers between devices, diagonal(): return lax.ppermute(value, ('gx', 'gy'), pairs)  0.87 us
  transfers between devices with their start and end apart: 12, of which 7 were waited for; matrix products, arithmetic and copies ran while one was open for 0% of the time, Pallas kernels for 7%

profile of v10, /device:TPU:0, one launch (start us, length us, event | category | flops | bytes accessed | tf_op | source)
XLA Modules:
  0.0 27.8 jit_solution(18171080756920116934)
XLA Ops:
  0.6 1.8 %pack.1 = (f32[40,128]{1,0:T(8,128)}, f32[72,128]{1,0:T(8,128)}, f32[296,128]{1,0:T(8,128)}) custom-call(f32[1,3,1,32]{3,2,1,0:T(1,128)} %bitcast.14, f32[1,1,32,128]{3,2,1,0:T(8,128)} %feat_ref.1, f32[1,1,32,1152]{3,2,1,0:T(8,128)} %cot_ref.1, s32[1,5,5,1,32]{4,3,2,1,0:T(1,128)} %bitcast.6, s32[1,5,5,1,32]{4,3,2,1,0:T(1,128)} %bitcast.8, ...), custom_call_target="tpu_custom_call" | custom-call | tf_op jit(solution)/shard_map/pack/pallas_call | solution.py:385
  2.4 3.0 %collective-permute-start = (f32[72,128]{1,0:T(8,128)}, f32[72,128]{1,0:T(8,128)S(1)}, u32[]{:S(2)}, u32[]{:S(2)}) collective-permute-start(f32[72,128]{1,0:T(8,128)} %get-tuple-element.31), channel_id=1, source_target_pairs={{0,1},{1,0},{2,3},{3,2},{4,5},{5,4},{6,7},{7,6},{8,9},{9,8},{10,11... | collective-permute-start | bytes 110600 | tf_op jit(solution)/shard_map/ppermute | solution.py:31
  5.4 3.7 %collective-permute-start.4 = (f32[296,128]{1,0:T(8,128)S(1)}, f32[296,128]{1,0:T(8,128)S(1)}, u32[]{:S(2)}, u32[]{:S(2)}) collective-permute-start(f32[296,128]{1,0:T(8,128)S(1)} %copy-done), channel_id=1, source_target_pairs={{0,6},{1,7},{2,4},{3,5},{4,2},{5,3},{6,0},{7,1},{8,14},{9,15},{10,... | collective-permute-start | bytes 454664 | tf_op jit(solution)/shard_map/ppermute | solution.py:31
  9.1 0.0 collective-permute-start.5
  9.1 0.0 collective-permute-done.refs_1_.refs_4_.refs_6_
  9.1 0.0 copy-start.2
  9.1 0.0 copy-start.3
  9.1 0.0 copy-start.4
  9.1 0.0 copy-start.5
  9.1 0.0 copy-start.6
  9.1 0.0 copy-start.7
  9.1 1.6 %collective-permute-start.1 = (f32[80,128]{1,0:T(8,128)S(1)}, f32[80,128]{1,0:T(8,128)S(1)}, u32[]{:S(2)}, u32[]{:S(2)}) collective-permute-start(f32[80,128]{1,0:T(8,128)S(1)} %stack.1), channel_id=1, source_target_pairs={{0,16},{8,24},{16,0},{24,8},{1,17},{9,25},{17,1},{25,9},{2,18},{10... | collective-permute-start | bytes 122888 | tf_op jit(solution)/shard_map/ppermute | solution.py:31
  10.7 0.0 collective-permute-start.2
  10.7 0.6 %collective-permute-start.3 = (f32[80,128]{1,0:T(8,128)S(1)}, f32[80,128]{1,0:T(8,128)S(1)}, u32[]{:S(2)}, u32[]{:S(2)}) collective-permute-start(f32[80,128]{1,0:T(8,128)S(1)} %stack.1), channel_id=1, source_target_pairs={{0,8},{8,0},{16,24},{24,16},{1,9},{9,1},{17,25},{25,17},{2,10},{10... | collective-permute-start | bytes 122888 | tf_op jit(solution)/shard_map/ppermute | solution.py:31
  11.4 0.2 prepare.1
  11.6 1.6 %collective-permute-done.1.refs_7_ = f32[80,128]{1,0:T(8,128)S(1)} collective-permute-done((f32[80,128]{1,0:T(8,128)S(1)}, f32[80,128]{1,0:T(8,128)S(1)}, u32[]{:S(2)}, u32[]{:S(2)}) %collective-permute-start.1) | collective-permute-done | bytes 40992 | tf_op jit(solution)/shard_map/ppermute | solution.py:31
  13.2 0.9 %collective-permute-done.2.refs_8_ = f32[80,128]{1,0:T(8,128)S(1)} collective-permute-done((f32[80,128]{1,0:T(8,128)S(1)}, f32[80,128]{1,0:T(8,128)S(1)}, u32[]{:S(2)}, u32[]{:S(2)}) %collective-permute-start.2) | collective-permute-done | bytes 40992 | tf_op jit(solution)/shard_map/ppermute | solution.py:31
  14.1 0.0 collective-permute-done.3.refs_9_
  14.1 1.8 %early_tiles.1 = (f32[24,256]{1,0:T(8,128)S(1)}, bf16[256,256]{1,0:T(8,128)(2,1)S(1)}, f32[8,256]{1,0:T(8,128)S(1)}, f32[256,128]{1,0:T(8,128)S(1)}) custom-call(s32[8,384]{1,0:T(8,128)S(1)} %get-tuple-element.32.rows_ref, bf16[384,96]{1,0:T(8,128)(2,1)S(1)} %get-tuple-element.27.refs_0_, bf16[64,768]{1,0:T(8,128)(2,1)S(1)} %get-tuple-element.28.refs_1_, ...), custom_call_target="tpu_custom_call" | custom-call | tf_op jit(solution)/shard_map/early_tiles/pallas_call | solution.py:385
  15.9 0.1 collective-permute-done.5.refs_10_
  16.1 1.8 %late_tiles.1 = (f32[160,128]{1,0:T(8,128)S(1)}, f32[160,128]{1,0:T(8,128)S(1)}, f32[64,128]{1,0:T(8,128)S(1)}, f32[64,128]{1,0:T(8,128)S(1)}) custom-call(s32[8,512]{1,0:T(8,128)S(1)} %get-tuple-element.26.rows_ref, bf16[384,96]{1,0:T(8,128)(2,1)S(1)} %get-tuple-element.27.refs_0_, bf16[64,768]{1,0:T(8,128)(2,1)S(1)} %get-tuple-element.28.refs_1_, ...), custom_call_target="tpu_custom_call" | custom-call | tf_op jit(solution)/shard_map/late_tiles/pallas_call | solution.py:385
  17.9 0.1 collective-permute-start.6
  17.9 2.5 %collective-permute-start.10 = (f32[64,128]{1,0:T(8,128)S(1)}, f32[64,128]{1,0:T(8,128)S(1)}, u32[]{:S(2)}, u32[]{:S(2)}) collective-permute-start(f32[64,128]{1,0:T(8,128)S(1)} %get-tuple-element.46), channel_id=1, source_target_pairs={{0,6},{1,7},{2,4},{3,5},{4,2},{5,3},{6,0},{7,1},{8,14},{9,15},{10,... | collective-permute-start | bytes 98312 | tf_op jit(solution)/shard_map/ppermute | solution.py:31
  20.4 0.0 collective-permute-done.6.refs_1_
  20.5 2.5 %collective-permute-start.7 = (f32[40,128]{1,0:T(8,128)S(1)}, f32[40,128]{1,0:T(8,128)S(1)}, u32[]{:S(2)}, u32[]{:S(2)}) collective-permute-start(f32[40,128]{1,0:T(8,128)S(1)} %get-tuple-element.43), channel_id=1, source_target_pairs={{0,17},{1,16},{2,19},{3,18},{4,21},{5,20},{6,23},{7,22},{8,25},{9,... | collective-permute-start | bytes 61448 | tf_op jit(solution)/shard_map/ppermute | solution.py:406
  22.9 0.5 %collective-permute-start.8 = (f32[40,128]{1,0:T(8,128)S(1)}, f32[40,128]{1,0:T(8,128)S(1)}, u32[]{:S(2)}, u32[]{:S(2)}) collective-permute-start(f32[40,128]{1,0:T(8,128)S(1)} %get-tuple-element.44), channel_id=1, source_target_pairs={{0,1},{1,0},{2,3},{3,2},{4,5},{5,4},{6,7},{7,6},{8,9},{9,8},{10,11... | collective-permute-start | bytes 61448 | tf_op jit(solution)/shard_map/ppermute | solution.py:31
  23.4 0.6 %collective-permute-start.9 = (f32[40,128]{1,0:T(8,128)S(1)}, f32[40,128]{1,0:T(8,128)S(1)}, u32[]{:S(2)}, u32[]{:S(2)}) collective-permute-start(f32[40,128]{1,0:T(8,128)S(1)} %get-tuple-element.45), channel_id=1, source_target_pairs={{0,16},{8,24},{16,0},{24,8},{1,17},{9,25},{17,1},{25,9},{2,18},{10... | collective-permute-start | bytes 61448 | tf_op jit(solution)/shard_map/ppermute | solution.py:31
  24.0 0.3 %collective-permute-done.11.refs_5_ = f32[64,128]{1,0:T(8,128)S(1)} collective-permute-done((f32[64,128]{1,0:T(8,128)S(1)}, f32[64,128]{1,0:T(8,128)S(1)}, u32[]{:S(2)}, u32[]{:S(2)}) %collective-permute-start.11) | collective-permute-done | bytes 32800 | tf_op jit(solution)/shard_map/ppermute | solution.py:31
  24.4 0.9 %collective-permute-done.7.refs_1_ = f32[40,128]{1,0:T(8,128)S(1)} collective-permute-done((f32[40,128]{1,0:T(8,128)S(1)}, f32[40,128]{1,0:T(8,128)S(1)}, u32[]{:S(2)}, u32[]{:S(2)}) %collective-permute-start.7) | collective-permute-done | bytes 20512 | tf_op jit(solution)/shard_map/ppermute | solution.py:406
  25.2 1.5 %collective-permute-done.8.refs_2_ = f32[40,128]{1,0:T(8,128)S(1)} collective-permute-done((f32[40,128]{1,0:T(8,128)S(1)}, f32[40,128]{1,0:T(8,128)S(1)}, u32[]{:S(2)}, u32[]{:S(2)}) %collective-permute-start.8) | collective-permute-done | bytes 20512 | tf_op jit(solution)/shard_map/ppermute | solution.py:31
  26.7 0.5 %collective-permute-done.9.refs_3_ = f32[40,128]{1,0:T(8,128)S(1)} collective-permute-done((f32[40,128]{1,0:T(8,128)S(1)}, f32[40,128]{1,0:T(8,128)S(1)}, u32[]{:S(2)}, u32[]{:S(2)}) %collective-permute-start.9) | collective-permute-done | bytes 20512 | tf_op jit(solution)/shard_map/ppermute | solution.py:31
  27.2 0.6 %sums.1 = (f32[1,3,1,32]{3,2,1,0:T(1,128)}, f32[1,1,32,128]{3,2,1,0:T(8,128)}) custom-call(f32[40,128]{1,0:T(8,128)S(1)} %get-tuple-element.42.refs_0_, f32[40,128]{1,0:T(8,128)S(1)} %collective-permute-done.7.refs_1_, f32[40,128]{1,0:T(8,128)S(1)} %collective-permute-done.8.refs_2_, f32[40,128]{1,0:T(8,128)S(1)} %collective-permute-done.9.refs_3_, ...), custom_call_target="tpu_custom_call" | custom-call | tf_op jit(solution)/shard_map/sums/pallas_call | solution.py:385
  (18 shorter events, 0.1 us)
Async XLA Ops:
  0.6 4.8 %copy-start.8 = (f32[8,32]{1,0:T(8,128)S(1)}, f32[8,32]{1,0:T(8,128)}, u32[]{:S(2)}) copy-start(f32[8,32]{1,0:T(8,128)} %refs_1_.1) | copy-start | bytes 3076
  2.4 3.0 %copy-start = (f32[296,128]{1,0:T(8,128)S(1)}, f32[296,128]{1,0:T(8,128)}, u32[]{:S(2)}) copy-start(f32[296,128]{1,0:T(8,128)} %get-tuple-element.39.refs_10_) | copy-start | bytes 454660
  2.4 6.6 %copy-start.1 = (f32[40,128]{1,0:T(8,128)S(1)}, f32[40,128]{1,0:T(8,128)}, u32[]{:S(2)}) copy-start(f32[40,128]{1,0:T(8,128)} %get-tuple-element.33.refs_0_.refs_5_) | copy-start | bytes 61444
  2.4 6.6 %collective-permute-start = (f32[72,128]{1,0:T(8,128)}, f32[72,128]{1,0:T(8,128)S(1)}, u32[]{:S(2)}, u32[]{:S(2)}) collective-permute-start(f32[72,128]{1,0:T(8,128)} %get-tuple-element.31), channel_id=1, source_target_pairs={{0,1},{1,0},{2,3},{3,2},{4,5},{5,4},{6,7},{7,6},{8,9},{9,8},{10,11... | collective-permute-start | bytes 110600 | tf_op jit(solution)/shard_map/ppermute | solution.py:31
  5.4 10.5 %collective-permute-start.4 = (f32[296,128]{1,0:T(8,128)S(1)}, f32[296,128]{1,0:T(8,128)S(1)}, u32[]{:S(2)}, u32[]{:S(2)}) collective-permute-start(f32[296,128]{1,0:T(8,128)S(1)} %copy-done), channel_id=1, source_target_pairs={{0,6},{1,7},{2,4},{3,5},{4,2},{5,3},{6,0},{7,1},{8,14},{9,15},{10,... | collective-permute-start | bytes 454664 | tf_op jit(solution)/shard_map/ppermute | solution.py:31
  9.1 7.0 %collective-permute-start.5 = (f32[296,128]{1,0:T(8,128)S(1)}, f32[296,128]{1,0:T(8,128)S(1)}, u32[]{:S(2)}, u32[]{:S(2)}) collective-permute-start(f32[296,128]{1,0:T(8,128)S(1)} %copy-done), channel_id=1, source_target_pairs={{0,2},{1,3},{2,0},{3,1},{4,6},{5,7},{6,4},{7,5},{8,10},{9,11},{10,... | collective-permute-start | bytes 454664 | tf_op jit(solution)/shard_map/ppermute | solution.py:31
  9.1 2.3 %copy-start.2 = (s32[1,1,5,5,32]{4,1,3,2,0:T(1,128)S(1)}, s32[1,1,5,5,32]{4,1,3,2,0:T(1,128)}, u32[]{:S(2)}) copy-start(s32[1,1,5,5,32]{4,1,3,2,0:T(1,128)} %param.13) | copy-start | bytes 9604
  9.1 2.3 %copy-start.3 = (s32[1,1,5,5,32]{4,1,3,2,0:T(1,128)S(1)}, s32[1,1,5,5,32]{4,1,3,2,0:T(1,128)}, u32[]{:S(2)}) copy-start(s32[1,1,5,5,32]{4,1,3,2,0:T(1,128)} %param.14) | copy-start | bytes 9604
  9.1 2.3 %copy-start.4 = (s32[1,1,5,5,32]{4,1,3,2,0:T(1,128)S(1)}, s32[1,1,5,5,32]{4,1,3,2,0:T(1,128)}, u32[]{:S(2)}) copy-start(s32[1,1,5,5,32]{4,1,3,2,0:T(1,128)} %param.15) | copy-start | bytes 9604
  9.1 2.3 %copy-start.5 = (s32[1,1,5,5,32]{4,1,3,2,0:T(1,128)S(1)}, s32[1,1,5,5,32]{4,1,3,2,0:T(1,128)}, u32[]{:S(2)}) copy-start(s32[1,1,5,5,32]{4,1,3,2,0:T(1,128)} %param.16) | copy-start | bytes 9604
  9.1 2.3 %copy-start.6 = (f32[32,384]{1,0:T(8,128)S(1)}, f32[32,384]{1,0:T(8,128)}, u32[]{:S(2)}) copy-start(f32[32,384]{1,0:T(8,128)} %out_ref.1) | copy-start | bytes 147460
  9.1 2.3 %copy-start.7 = (f32[10,32]{1,0:T(8,128)S(1)}, f32[10,32]{1,0:T(8,128)}, u32[]{:S(2)}) copy-start(f32[10,32]{1,0:T(8,128)} %emb_ref.1) | copy-start | bytes 3844
  9.1 4.1 %collective-permute-start.1 = (f32[80,128]{1,0:T(8,128)S(1)}, f32[80,128]{1,0:T(8,128)S(1)}, u32[]{:S(2)}, u32[]{:S(2)}) collective-permute-start(f32[80,128]{1,0:T(8,128)S(1)} %stack.1), channel_id=1, source_target_pairs={{0,16},{8,24},{16,0},{24,8},{1,17},{9,25},{17,1},{25,9},{2,18},{10... | collective-permute-start | bytes 122888 | tf_op jit(solution)/shard_map/ppermute | solution.py:31
  10.7 3.4 %collective-permute-start.2 = (f32[80,128]{1,0:T(8,128)S(1)}, f32[80,128]{1,0:T(8,128)S(1)}, u32[]{:S(2)}, u32[]{:S(2)}) collective-permute-start(f32[80,128]{1,0:T(8,128)S(1)} %stack.1), channel_id=1, source_target_pairs={{0,24},{8,16},{16,8},{24,0},{1,25},{9,17},{17,9},{25,1},{2,26},{10... | collective-permute-start | bytes 122888 | tf_op jit(solution)/shard_map/ppermute | solution.py:31
  10.7 3.4 %collective-permute-start.3 = (f32[80,128]{1,0:T(8,128)S(1)}, f32[80,128]{1,0:T(8,128)S(1)}, u32[]{:S(2)}, u32[]{:S(2)}) collective-permute-start(f32[80,128]{1,0:T(8,128)S(1)} %stack.1), channel_id=1, source_target_pairs={{0,8},{8,0},{16,24},{24,16},{1,9},{9,1},{17,25},{25,17},{2,10},{10... | collective-permute-start | bytes 122888 | tf_op jit(solution)/shard_map/ppermute | solution.py:31
  17.9 2.6 %collective-permute-start.6 = (f32[160,128]{1,0:T(8,128)S(1)}, f32[160,128]{1,0:T(8,128)S(1)}, u32[]{:S(2)}, u32[]{:S(2)}) collective-permute-start(f32[160,128]{1,0:T(8,128)S(1)} %get-tuple-element.41), channel_id=1, source_target_pairs={{0,8},{8,0},{16,24},{24,16},{1,9},{9,1},{17,25},{25,17},{2,10},{10... | collective-permute-start | bytes 245768 | tf_op jit(solution)/shard_map/ppermute | solution.py:31
  17.9 6.1 %collective-permute-start.10 = (f32[64,128]{1,0:T(8,128)S(1)}, f32[64,128]{1,0:T(8,128)S(1)}, u32[]{:S(2)}, u32[]{:S(2)}) collective-permute-start(f32[64,128]{1,0:T(8,128)S(1)} %get-tuple-element.46), channel_id=1, source_target_pairs={{0,6},{1,7},{2,4},{3,5},{4,2},{5,3},{6,0},{7,1},{8,14},{9,15},{10,... | collective-permute-start | bytes 98312 | tf_op jit(solution)/shard_map/ppermute | solution.py:31
  20.4 3.9 %collective-permute-start.11 = (f32[64,128]{1,0:T(8,128)S(1)}, f32[64,128]{1,0:T(8,128)S(1)}, u32[]{:S(2)}, u32[]{:S(2)}) collective-permute-start(f32[64,128]{1,0:T(8,128)S(1)} %get-tuple-element.47), channel_id=1, source_target_pairs={{0,2},{1,3},{2,0},{3,1},{4,6},{5,7},{6,4},{7,5},{8,10},{9,11},{10,... | collective-permute-start | bytes 98312 | tf_op jit(solution)/shard_map/ppermute | solution.py:31
  20.5 4.8 %collective-permute-start.7 = (f32[40,128]{1,0:T(8,128)S(1)}, f32[40,128]{1,0:T(8,128)S(1)}, u32[]{:S(2)}, u32[]{:S(2)}) collective-permute-start(f32[40,128]{1,0:T(8,128)S(1)} %get-tuple-element.43), channel_id=1, source_target_pairs={{0,17},{1,16},{2,19},{3,18},{4,21},{5,20},{6,23},{7,22},{8,25},{9,... | collective-permute-start | bytes 61448 | tf_op jit(solution)/shard_map/ppermute | solution.py:406
  22.9 3.8 %collective-permute-start.8 = (f32[40,128]{1,0:T(8,128)S(1)}, f32[40,128]{1,0:T(8,128)S(1)}, u32[]{:S(2)}, u32[]{:S(2)}) collective-permute-start(f32[40,128]{1,0:T(8,128)S(1)} %get-tuple-element.44), channel_id=1, source_target_pairs={{0,1},{1,0},{2,3},{3,2},{4,5},{5,4},{6,7},{7,6},{8,9},{9,8},{10,11... | collective-permute-start | bytes 61448 | tf_op jit(solution)/shard_map/ppermute | solution.py:31
  23.4 3.8 %collective-permute-start.9 = (f32[40,128]{1,0:T(8,128)S(1)}, f32[40,128]{1,0:T(8,128)S(1)}, u32[]{:S(2)}, u32[]{:S(2)}) collective-permute-start(f32[40,128]{1,0:T(8,128)S(1)} %get-tuple-element.45), channel_id=1, source_target_pairs={{0,16},{8,24},{16,0},{24,8},{1,17},{9,25},{17,1},{25,9},{2,18},{10... | collective-permute-start | bytes 61448 | tf_op jit(solution)/shard_map/ppermute | solution.py:31
